TPU v7x, 32 devices: a whole 2x2x4 slice. The times are simulated.
32 devices in a mesh: rad: 8 (over z, y), ang: 4 (over x, core).
Axes of the slice: x: 2, y: 2, z: 4, core: 2. Of those that a mesh axis runs over, the one named last changes fastest.
Arguments:
- nonlin: bfloat16 [2, 512, 32768], P(None, 'rad', 'ang'), may hold values from -6 to 6
- state: float32 [2, 512, 32768], P(None, 'rad', 'ang'), may hold values from -6 to 6
- inverse: float32 [32, 2, 1024, 1024], P(('ang', 'rad')), may hold values from -0.1875 to 0.1875
- pair_of_slot: int32 [32], P(('ang', 'rad')), may hold values from 0 to 31, each once
Outputs:
- new_state: float32 [2, 512, 32768], P(None, 'rad', 'ang')
Inputs may be any that keep to these rules, and one draw needn't show every extreme that they name: Slot s of the window holds degrees pair_of_slot[s] and 511 - pair_of_slot[s]; every pair once.
All inputs are finite; a program needn't handle non-finite values.
Results may differ from a plain program's by a relative error of at most 0.0003.
Values may be sent and summed in bfloat16 or wider, within the bound.
No kernel may reach another device: no remote copies, remote signals or barrier semaphores. Data moves between devices by JAX's collectives and lax.ppermute only.
A program may use at most 128 MiB of HBM per device.

v0:
```python
import math

import jax
import jax.numpy as jnp
from jax import lax
from jax.sharding import PartitionSpec as P

inner_radius = 0.35
outer_radius = 1.0
blend_weight = 0.5


def padded_2(array, sides, width):
    for axis, dim in sides:
        peers, length = (lax.axis_size(axis), array.shape[dim])
        up = [(i, (i + 1) % peers) for i in range(peers - 1)]
        down = [(j, i) for i, j in up]
        last = lax.slice_in_dim(array, length - width, length, axis=dim)
        leading = lax.slice_in_dim(array, 0, width, axis=dim)
        before = lax.ppermute(last, axis, up)
        after = lax.ppermute(leading, axis, down)
        array = jnp.concatenate([before, array, after], axis=dim)
    return array


def radius_at(level_index, total_levels):
    scaled = level_index / (total_levels - 1.0)
    stretch = (1.0 - blend_weight) * scaled + blend_weight * (1.0 - jnp.cos(math.pi * scaled)) / 2.0
    return inner_radius + (outer_radius - inner_radius) * stretch


def forcing(padded, old_state, first_level, total_levels):
    count = padded.shape[1] - 2
    values = padded.astype(jnp.float32)
    level_index = jnp.arange(count, dtype=jnp.float32) + first_level
    radius_here = radius_at(level_index, total_levels)
    step_below = radius_here - radius_at(level_index - 1.0, total_levels)
    step_above = radius_at(level_index + 1.0, total_levels) - radius_here
    at_inner = level_index == 0.0
    at_outer = level_index == total_levels - 1.0
    weight_below = jnp.where(
        at_inner,
        0.0,
        jnp.where(
            at_outer, -1.0 / step_below, -step_above / (step_below * (step_below + step_above))
        ),
    )
    weight_here = jnp.where(
        at_inner,
        -1.0 / step_above,
        jnp.where(
            at_outer, 1.0 / step_below, (step_above - step_below) / (step_below * step_above)
        ),
    )
    weight_above = jnp.where(
        at_inner,
        1.0 / step_above,
        jnp.where(at_outer, 0.0, step_below / (step_above * (step_below + step_above))),
    )
    centre = values[:, 1:-1]
    derivative = (
        weight_below[None, :, None] * values[:, :-2]
        + weight_here[None, :, None] * centre
        + weight_above[None, :, None] * values[:, 2:]
    )
    time_step = 0.5 * (outer_radius - inner_radius) / (total_levels - 1.0)
    return old_state + time_step * (derivative + 2.0 * centre / radius_here[None, :, None])


def lower_mask(column_count, pair_index):
    half_cols = column_count // 2
    column_index = jnp.arange(column_count, dtype=jnp.int32)
    first_half = column_index < pair_index + 1
    second_half = (column_index >= half_cols) & (column_index - half_cols < pair_index)
    return jnp.where(column_index < half_cols, first_half, second_half)


def apply_inverse(block, matrices, pair_index):
    field_count, level_count, column_count = block.shape
    row_count = field_count * level_count
    flattened = block.reshape(row_count, column_count)
    stacked = matrices.reshape(2 * row_count, row_count)
    both_parts = jnp.dot(
        stacked, flattened, precision=lax.Precision.HIGHEST, preferred_element_type=jnp.float32
    )
    both_parts = both_parts.reshape(2, row_count, column_count)
    lower_part = both_parts[0]
    upper_part = both_parts[1]
    chosen = jnp.where(lower_mask(column_count, pair_index)[None, :], lower_part, upper_part)
    return chosen.reshape(field_count, level_count, column_count)


def local(nonlin, state, inverse, pair_of_slot):
    levels = nonlin.shape[1]
    groups = lax.axis_size("rad")
    width = nonlin.shape[2] // groups
    total_levels = levels * groups * 1.0
    padded = padded_2(nonlin, (("rad", 1),), 1)
    first_level = (lax.axis_index("rad") * levels).astype(jnp.float32)
    right_side = forcing(padded, state, first_level, total_levels)
    columns = lax.all_to_all(
        right_side.reshape(2, levels, groups, width), "rad", split_axis=2, concat_axis=1, tiled=True
    )
    columns = columns.reshape(2, levels * groups, width)
    solved = apply_inverse(columns, inverse[0], pair_of_slot[0])
    returned = lax.all_to_all(
        solved.reshape(2, groups, levels, 1, width), "rad", split_axis=1, concat_axis=3, tiled=True
    )
    return returned.reshape(2, levels, groups * width)


def solution(mesh):
    placed = (
        P(None, "rad", "ang"),
        P(None, "rad", "ang"),
        P(("ang", "rad"), None, None, None),
        P(("ang", "rad")),
    )
    return jax.shard_map(
        local, mesh=mesh, in_specs=placed, out_specs=P(None, "rad", "ang"), check_vma=False
    )
```

profile of v0, /device:TPU:8, one launch (start us, length us, event | category | flops | bytes accessed | tf_op | source)
XLA Modules:
  0.0 298.2 jit_solution(6941762105127486296)
XLA Ops:
  0.0 1.1 fusion.13
  1.1 3.4 %collective-permute-start = (bf16[2,1,8192]{2,1,0:T(2,128)(2,1)S(1)}, bf16[2,1,8192]{2,1,0:T(2,128)(2,1)S(1)}, u32[]{:S(2)}, u32[]{:S(2)}) collective-permute-start(bf16[2,1,8192]{2,1,0:T(2,128)(2,1)S(1)} %get-tuple-element.7), channel_id=1, source_target_pairs={{0,4},{4,8},{8,12},{12,16},{16,20},{20,24},{24,28},{1,5},{5,9},{9,... | collective-permute-start | bytes 98312 | tf_op jit(solution)/shard_map/ppermute | solution.py:20
  4.6 3.3 %collective-permute-start.1 = (bf16[2,1,8192]{2,1,0:T(2,128)(2,1)S(1)}, bf16[2,1,8192]{2,1,0:T(2,128)(2,1)S(1)}, u32[]{:S(2)}, u32[]{:S(2)}) collective-permute-start(bf16[2,1,8192]{2,1,0:T(2,128)(2,1)S(1)} %get-tuple-element.8), channel_id=1, source_target_pairs={{4,0},{8,4},{12,8},{16,12},{20,16},{24,20},{28,24},{5,1},{9,5},{13... | collective-permute-start | bytes 98312 | tf_op jit(solution)/shard_map/ppermute | solution.py:21
  7.9 0.0 copy-start
  7.9 0.1 divide_select_fusion
  8.0 0.1 multiply_add_fusion
  8.1 0.1 collective-permute-done
  8.2 2.5 collective-permute-done.1
  10.7 2.3 maximum_convert_fusion
  13.0 0.0 copy-done
  13.1 2.1 fusion.3
  15.1 2.5 copy.20
  17.7 6.2 %all-to-all-start = ((f32[2,64,8,1024]{3,1,0,2:T(8,128)}), f32[2,64,8,1024]{3,1,0,2:T(8,128)}, u32[]{:S(2)}, u32[]{:S(2)}) async-start(f32[2,64,8,1024]{3,1,0,2:T(8,128)} %bitcast.28), calls=%async_computation | async-start | bytes 8388608 | tf_op jit(solution)/shard_map/all_to_all | solution.py:101
  24.5 88.6 %all-to-all-done = f32[2,64,8,1024]{3,1,0,2:T(8,128)} async-done(((f32[2,64,8,1024]{3,1,0,2:T(8,128)}), f32[2,64,8,1024]{3,1,0,2:T(8,128)}, u32[]{:S(2)}, u32[]{:S(2)}) %all-to-all-start) | async-done | bytes 4194336 | tf_op jit(solution)/shard_map/all_to_all | solution.py:101
  113.1 2.8 copy.13
  115.9 54.6 %convolution_bitcast_fusion = f32[2048,1024]{0,1:T(8,128)S(1)} fusion(f32[1024,1024]{1,0:T(8,128)S(1)} %bitcast.31, f32[2048,1024]{1,0:T(8,128)} %bitcast.32), kind=kOutput, calls=%fused_computation | convolution fusion | flops 25769803776 | bytes 20971520 | tf_op jit(solution)/shard_map/dot_general | solution.py:83
  170.5 4.2 %fusion.12 = (f32[1024,1024]{0,1:T(8,128)}, f32[1024,1024]{0,1:T(8,128)}) fusion(f32[2048,1024]{0,1:T(8,128)S(1)} %convolution_bitcast_fusion), kind=kLoop, calls=%fused_computation.32 | loop fusion | bytes 16777216 | tf_op jit(solution)/shard_map/slice | solution.py:88
  174.7 5.3 %copy.14 = f32[1024,1024]{1,0:T(8,128)} copy(f32[1024,1024]{0,1:T(8,128)} %get-tuple-element.6) | data formatting | bytes 8388608 | tf_op jit(solution)/shard_map/slice | solution.py:87
  180.1 5.4 %copy.15 = f32[1024,1024]{1,0:T(8,128)} copy(f32[1024,1024]{0,1:T(8,128)} %get-tuple-element.5) | data formatting | bytes 8388608 | tf_op jit(solution)/shard_map/slice | solution.py:88
  185.5 4.4 %broadcast_select_fusion = f32[2,8,64,1,1024]{4,2,1,0,3:T(8,128)S(1)} fusion(f32[2,8,64,1,1024]{4,2,1,0,3:T(8,128)} %bitcast.26, f32[2,8,64,1,1024]{4,2,1,0,3:T(8,128)} %bitcast.27, pred[1024]{0:T(1024)(128)(4,1)S(1)} %fusion.5), kind=kLoop, calls=%fused_computation.10 | loop fusion | flops 1048576 | bytes 12583936 | tf_op jit(solution)/shard_map/jit(_where)/select_n | solution.py:89
  189.9 0.6 copy.16
  190.5 98.4 %all_to_all.30 = f32[2,8,64,1,1024]{4,2,0,3,1:T(8,128)S(1)} all-to-all(f32[2,8,64,1,1024]{4,2,0,3,1:T(8,128)S(1)} %copy.16), channel_id=1, replica_groups=mesh['rad'=8,'ang'=4] {'rad'}, dimensions={1} | all-to-all | bytes 8388608 | tf_op jit(solution)/shard_map/all_to_all | solution.py:106
  288.9 4.4 %copy.17 = f32[2,1,64,8,1,1024]{5,3,2,0,4,1:T(8,128)} copy(f32[2,1,64,8,1,1024]{5,2,0,3,4,1:T(8,128)S(1)} %bitcast.29) | data formatting | bytes 8388608 | tf_op jit(solution)/shard_map/all_to_all | solution.py:106
  293.3 4.9 %reshape.109 = f32[2,64,8192]{2,1,0:T(8,128)} reshape(f32[2,1,64,8,1,1024]{5,3,2,0,4,1:T(8,128)} %copy.17) | data formatting | bytes 8388608 | tf_op jit(solution)/shard_map/reshape | solution.py:109
  (1 shorter events, 0.0 us)
Async XLA Ops:
  1.1 7.1 %collective-permute-start = (bf16[2,1,8192]{2,1,0:T(2,128)(2,1)S(1)}, bf16[2,1,8192]{2,1,0:T(2,128)(2,1)S(1)}, u32[]{:S(2)}, u32[]{:S(2)}) collective-permute-start(bf16[2,1,8192]{2,1,0:T(2,128)(2,1)S(1)} %get-tuple-element.7), channel_id=1, source_target_pairs={{0,4},{4,8},{8,12},{12,16},{16,20},{20,24},{24,28},{1,5},{5,9},{9,... | collective-permute-start | bytes 98312 | tf_op jit(solution)/shard_map/ppermute | solution.py:20
  4.6 6.2 %collective-permute-start.1 = (bf16[2,1,8192]{2,1,0:T(2,128)(2,1)S(1)}, bf16[2,1,8192]{2,1,0:T(2,128)(2,1)S(1)}, u32[]{:S(2)}, u32[]{:S(2)}) collective-permute-start(bf16[2,1,8192]{2,1,0:T(2,128)(2,1)S(1)} %get-tuple-element.8), channel_id=1, source_target_pairs={{4,0},{8,4},{12,8},{16,12},{20,16},{24,20},{28,24},{5,1},{9,5},{13... | collective-permute-start | bytes 98312 | tf_op jit(solution)/shard_map/ppermute | solution.py:21
  7.9 5.1 %copy-start = (f32[2,64,8192]{2,1,0:T(8,128)S(1)}, f32[2,64,8192]{2,1,0:T(8,128)}, u32[]{:S(2)}) copy-start(f32[2,64,8192]{2,1,0:T(8,128)} %param.5) | copy-start | bytes 12582916
  17.7 95.5 %all-to-all-start = ((f32[2,64,8,1024]{3,1,0,2:T(8,128)}), f32[2,64,8,1024]{3,1,0,2:T(8,128)}, u32[]{:S(2)}, u32[]{:S(2)}) async-start(f32[2,64,8,1024]{3,1,0,2:T(8,128)} %bitcast.28), calls=%async_computation | async-start | bytes 8388608 | tf_op jit(solution)/shard_map/all_to_all | solution.py:101
where the time goes:
time: 301 us; the launch traced here: 298 us
  blocking collectives  98.4 us (33%)
  waiting for transfers between devices  91.3 us (30%)
  matrix products  54.6 us (18%)
  local copies, waits for them, and re-layouts  31.3 us (10%)
  starting transfers between devices  12.9 us (4%)
  other arithmetic  8.96 us (3%)
    all_to_all x1, blocking collectives, local(): lax.all_to_all(solved.reshape(2, groups, levels, 1, width), 'rad', split_...  98.4 us
    all_to_all x1, waiting for transfers between devices, local(): lax.all_to_all(right_side.reshape(2, levels, groups, width), 'rad', split...  88.6 us
    dot_general x1, matrix products, apply_inverse(): jnp.dot(stacked, flattened, precision=lax.Precision.HIGHEST, preferred_el...  54.6 us
    slice x2, local copies, waits for them, and re-layouts, apply_inverse(): upper_part = both_parts[1]  9.59 us
    all_to_all x1, starting transfers between devices, local(): lax.all_to_all(right_side.reshape(2, levels, groups, width), 'rad', split...  6.17 us
  transfers between devices with their start and end apart: 3, of which 3 were waited for; matrix products, arithmetic and copies ran while one was open for 0% of the time, Pallas kernels for 0%

commit v1 on v0

v1 whole, which is shorter than its diff:
```python
import functools
import math

import jax
import jax.numpy as jnp
import numpy as np
from jax import lax
from jax.experimental import pallas as pl
from jax.experimental.pallas import tpu as pltpu
from jax.sharding import PartitionSpec as P

inner_radius = 0.35
outer_radius = 1.0
blend_weight = 0.5

LANES = 128
TILE = 16
CHUNKS = 2
TOP = 32700.0
FINE = 128.0
MIB = 1024 * 1024


def radius_at(level_index, total_levels):
    scaled = level_index / (total_levels - 1.0)
    stretch = (1.0 - blend_weight) * scaled + blend_weight * (1.0 - np.cos(math.pi * scaled)) / 2.0
    return inner_radius + (outer_radius - inner_radius) * stretch


def stencil_table(total_levels):
    k = np.arange(total_levels, dtype=np.float64)
    radius = radius_at(k, total_levels)
    below = radius - radius_at(k - 1.0, total_levels)
    above = radius_at(k + 1.0, total_levels) - radius
    at_inner, at_outer = k == 0, k == total_levels - 1
    weight_below = np.where(at_inner, 0.0, np.where(at_outer, -1.0 / below, -above / (below * (below + above))))
    weight_here = np.where(
        at_inner, -1.0 / above, np.where(at_outer, 1.0 / below, (above - below) / (below * above))
    )
    weight_above = np.where(at_inner, 1.0 / above, np.where(at_outer, 0.0, below / (above * (below + above))))
    time_step = 0.5 * (outer_radius - inner_radius) / (total_levels - 1.0)
    table = np.zeros((total_levels, LANES), np.float32)
    table[:, 0] = time_step * weight_below
    table[:, 1] = time_step * (weight_here + 2.0 / radius)
    table[:, 2] = time_step * weight_above
    return table


def scale_code(values):
    largest = jnp.maximum(jnp.max(jnp.abs(values), axis=0, keepdims=True), 1e-30)
    return jnp.ceil(jnp.log2(largest) * FINE)


def encode(values, code):
    scaled = values * (jnp.exp2(code * (-1.0 / FINE)) * TOP)
    scaled = jnp.clip(jnp.round(scaled), -32767.0, 32767.0)
    return scaled.astype(jnp.int32).astype(jnp.int16)


def scale_of(codes):
    return jnp.exp2(codes.astype(jnp.int32).astype(jnp.float32) * (1.0 / FINE)) * (1.0 / TOP)


def pack_codes(codes):
    rows = codes + [jnp.zeros_like(codes[0])] * (TILE - len(codes))
    return jnp.concatenate(rows, axis=0).astype(jnp.int32).astype(jnp.int16)


def right_side_kernel(groups, slabs, where, n_ref, s_ref, before_ref, after_ref, tab_ref, *rest):
    outs, buffer = rest[:groups], rest[groups]
    levels = n_ref.shape[1]
    rows = 2 * levels
    step = pl.program_id(0)
    tab = tab_ref[...]
    below, here, above = (jnp.broadcast_to(tab[:, i : i + 1], (levels, LANES)) for i in range(3))
    row = lax.broadcasted_iota(jnp.int32, (levels, LANES), 0)
    codes = []
    for slab in range(slabs):
        cols = slice(slab * LANES, (slab + 1) * LANES)
        fields = []
        for f in range(2):
            n = n_ref[f, :, cols].astype(jnp.float32)
            prev = jnp.where(row == 0, before_ref[f, :, cols].astype(jnp.float32), pltpu.roll(n, 1, 0))
            succ = jnp.where(
                row == levels - 1, after_ref[f, :, cols].astype(jnp.float32), pltpu.roll(n, levels - 1, 0)
            )
            fields.append(s_ref[f, :, cols] + (below * prev + here * n + above * succ))
        both = jnp.concatenate(fields, axis=0)
        code = scale_code(both)
        codes.append(code)
        buffer[slab * rows : (slab + 1) * rows, :] = encode(both, code)
    buffer[slabs * rows :, :] = pack_codes(codes)
    for k in range(groups):

        @pl.when(step == k)
        def _():
            outs[k][...] = buffer[...]


def split_kernel(a_ref, hi_ref, lo_ref):
    a = a_ref[...]
    hi = a.astype(jnp.bfloat16)
    hi_ref[...] = hi
    lo_ref[...] = (a - hi.astype(jnp.float32)).astype(jnp.bfloat16)


def product_kernel(groups, slabs, lower_slabs, first_col, half_cols, where, *refs):
    ins, (hi_ref, lo_ref), outs = refs[:groups], refs[groups : groups + 2], refs[groups + 2 : 2 * groups + 2]
    v_hi, v_lo, y = refs[2 * groups + 2 :]
    size = y.shape[0]
    levels = size // (2 * groups)
    rows = 2 * levels
    me = where[0]
    pair = where[1]
    for k in range(groups):
        peer = lax.bitwise_xor(me, k)
        scales = scale_of(ins[k][slabs * rows :, :])
        for slab in range(slabs):
            cols = slice(slab * LANES, (slab + 1) * LANES)
            for f in range(2):
                at = slab * rows + f * levels
                v = ins[k][at : at + levels, :].astype(jnp.int32).astype(jnp.float32) * scales[slab : slab + 1, :]
                to = pl.ds(pl.multiple_of(f * (size // 2) + peer * levels, levels), levels)
                hi = v.astype(jnp.bfloat16)
                v_hi[to, cols] = hi
                v_lo[to, cols] = (v - hi.astype(jnp.float32)).astype(jnp.bfloat16)

    def product(which, cols):
        dot = functools.partial(jnp.dot, preferred_element_type=jnp.float32)
        return (
            dot(lo_ref[which], v_hi[:, cols])
            + dot(hi_ref[which], v_lo[:, cols])
            + dot(hi_ref[which], v_hi[:, cols])
        )

    wide = min(2 * LANES, slabs * LANES)
    for at in range(0, slabs * LANES, wide):
        y[:, at : at + wide] = product(1, slice(at, at + wide))
    for slab in range(slabs):
        first = first_col + slab * LANES
        if first % half_cols < lower_slabs * LANES:
            cols = slice(slab * LANES, (slab + 1) * LANES)
            column = first % half_cols + lax.broadcasted_iota(jnp.int32, (size, LANES), 1)
            bound = pair + 1 if first < half_cols else pair
            y[:, cols] = jnp.where(column < bound, product(0, cols), y[:, cols])

    for k in range(groups):
        peer = lax.bitwise_xor(me, k)
        codes = []
        for slab in range(slabs):
            cols = slice(slab * LANES, (slab + 1) * LANES)
            both = jnp.concatenate(
                [
                    y[pl.ds(pl.multiple_of(f * (size // 2) + peer * levels, levels), levels), cols]
                    for f in range(2)
                ],
                axis=0,
            )
            code = scale_code(both)
            codes.append(code)
            outs[k][slab * rows : (slab + 1) * rows, :] = encode(both, code)
        outs[k][slabs * rows :, :] = pack_codes(codes)


def result_kernel(groups, slabs, where, *refs):
    ins, out_ref = refs[:groups], refs[-1]
    levels = out_ref.shape[1]
    rows = 2 * levels
    step = pl.program_id(0)
    for k in range(groups):

        @pl.when(step == k)
        def _():
            scales = scale_of(ins[k][slabs * rows :, :])
            for slab in range(slabs):
                for f in range(2):
                    at = slab * rows + f * levels
                    v = ins[k][at : at + levels, :].astype(jnp.int32).astype(jnp.float32)
                    out_ref[f, :, slab * LANES : (slab + 1) * LANES] = v * scales[slab : slab + 1, :]


def exchange(messages, groups):
    got = list(messages)
    for k in reversed(range(1, groups)):
        got[k] = lax.ppermute(messages[k], "rad", [(i, i ^ k) for i in range(groups)])
    return got


def neighbours(nonlin, groups):
    up = [(i, i + 1) for i in range(groups - 1)]
    down = [(j, i) for i, j in up]
    before = lax.ppermute(nonlin[:, -1:, :], "rad", up)
    after = lax.ppermute(nonlin[:, :1, :], "rad", down)
    return before, after


def local(slots, nonlin, state, inverse, pair_of_slot):
    levels = nonlin.shape[1]
    groups = lax.axis_size("rad")
    width = nonlin.shape[2] // groups
    size = inverse.shape[-1]
    span = width // CHUNKS
    slabs = span // LANES
    rows = 2 * levels
    lower_slabs = -(-slots // LANES)
    me = lax.axis_index("rad").astype(jnp.int32)
    where = jnp.stack([me, pair_of_slot[0].astype(jnp.int32)])
    table = jnp.asarray(stencil_table(levels * groups))
    message = jax.ShapeDtypeStruct((slabs * rows + TILE, LANES), jnp.int16)
    whole = pl.BlockSpec(message.shape, lambda *_: (0, 0))
    vmem = pl.BlockSpec(memory_space=pltpu.VMEM)
    before, after = neighbours(nonlin, groups)

    def right_side(chunk):
        def at(k, w):
            return (0, 0, lax.bitwise_xor(w[0], k) * CHUNKS + chunk)

        return pl.pallas_call(
            functools.partial(right_side_kernel, groups, slabs),
            out_shape=[message] * groups,
            grid_spec=pltpu.PrefetchScalarGridSpec(
                num_scalar_prefetch=1,
                grid=(groups,),
                in_specs=[
                    pl.BlockSpec((2, levels, span), at),
                    pl.BlockSpec((2, levels, span), at),
                    pl.BlockSpec((2, 1, span), at),
                    pl.BlockSpec((2, 1, span), at),
                    pl.BlockSpec((levels, LANES), lambda k, w: (w[0], 0)),
                ],
                out_specs=[whole] * groups,
                scratch_shapes=[pltpu.VMEM(message.shape, jnp.int16)],
            ),
            compiler_params=pltpu.CompilerParams(vmem_limit_bytes=16 * MIB),
            cost_estimate=pl.CostEstimate(flops=4 * MIB, bytes_accessed=4 * MIB, transcendentals=0),
            name="right_side",
        )(where, nonlin, state, before, after, table)

    def split():
        block = pl.BlockSpec((1, size // 4, size), lambda i, j: (i, j, 0))
        half = jax.ShapeDtypeStruct((2, size, size), jnp.bfloat16)
        return pl.pallas_call(
            split_kernel,
            out_shape=[half, half],
            grid=(2, 4),
            in_specs=[block],
            out_specs=[block, block],
            compiler_params=pltpu.CompilerParams(vmem_limit_bytes=16 * MIB),
            cost_estimate=pl.CostEstimate(flops=4 * MIB, bytes_accessed=16 * MIB, transcendentals=0),
            name="split_inverse",
        )(inverse[0])

    def product(chunk, messages, hi, lo):
        return pl.pallas_call(
            functools.partial(product_kernel, groups, slabs, lower_slabs, chunk * span, width // 2),
            out_shape=[message] * groups,
            grid_spec=pltpu.PrefetchScalarGridSpec(
                num_scalar_prefetch=1,
                grid=(),
                in_specs=[vmem] * (groups + 2),
                out_specs=[vmem] * groups,
                scratch_shapes=[
                    pltpu.VMEM((size, span), jnp.bfloat16),
                    pltpu.VMEM((size, span), jnp.bfloat16),
                    pltpu.VMEM((size, span), jnp.float32),
                ],
            ),
            compiler_params=pltpu.CompilerParams(vmem_limit_bytes=32 * MIB),
            cost_estimate=pl.CostEstimate(
                flops=6 * size * size * span, bytes_accessed=10 * MIB, transcendentals=0
            ),
            name="product",
        )(where, *messages, hi, lo)

    def result(chunk, messages, previous):
        def at(k, w):
            return (0, 0, lax.bitwise_xor(w[0], k) * CHUNKS + chunk)

        out_shape = jax.ShapeDtypeStruct(state.shape, jnp.float32)
        carried = [] if previous is None else [previous]
        return pl.pallas_call(
            functools.partial(result_kernel, groups, slabs),
            out_shape=out_shape,
            grid_spec=pltpu.PrefetchScalarGridSpec(
                num_scalar_prefetch=1,
                grid=(groups,),
                in_specs=[whole] * groups + [pl.BlockSpec(memory_space=pl.ANY)] * len(carried),
                out_specs=pl.BlockSpec((2, levels, span), at),
            ),
            input_output_aliases={} if previous is None else {groups + 1: 0},
            compiler_params=pltpu.CompilerParams(vmem_limit_bytes=16 * MIB),
            cost_estimate=pl.CostEstimate(flops=MIB, bytes_accessed=3 * MIB, transcendentals=0),
            name="result",
        )(where, *messages, *carried)

    sent = [exchange(right_side(c), groups) for c in range(CHUNKS)]
    hi, lo = split()
    back = [exchange(product(c, sent[c], hi, lo), groups) for c in range(CHUNKS)]
    out = None
    for c in range(CHUNKS):
        out = result(c, back[c], out)
    return out


def solution(mesh):
    placed = (
        P(None, "rad", "ang"),
        P(None, "rad", "ang"),
        P(("ang", "rad"), None, None, None),
        P(("ang", "rad")),
    )
    slots = mesh.shape["rad"] * mesh.shape["ang"]
    return jax.shard_map(
        functools.partial(local, slots),
        mesh=mesh,
        in_specs=placed,
        out_specs=P(None, "rad", "ang"),
        check_vma=False,
    )
```

time: 301 us -> 132 us (0.44)
  blocking collectives: 98.4 us -> 0 us
  matrix products: 54.6 us -> 0 us
  waiting for transfers between devices: 91.3 us -> 44.5 us
  starting transfers between devices: 12.9 us -> 52 us
  Pallas kernels: 0 us -> 28.3 us
  local copies, waits for them, and re-layouts: 31.3 us -> 5.86 us
  other arithmetic: 8.96 us -> 0.08 us
    all_to_all x1 -> x0, blocking collectives: 98.4 us -> none  [local(): lax.all_to_all(solved.reshape(2, groups, levels, 1, width), 'rad', split_...]
    all_to_all x1 -> x0, waiting for transfers between devices: 88.6 us -> none  [local(): lax.all_to_all(right_side.reshape(2, levels, groups, width), 'rad', split...]
    dot_general x1 -> x0, matrix products: 54.6 us -> none  [apply_inverse(): jnp.dot(stacked, flattened, precision=lax.Precision.HIGHEST, preferred_el...]
    ppermute x2 -> x30, starting transfers between devices: 6.74 us -> 52 us  [the longest x28 45.3 us: exchange(): lax.ppermute(messages[k], 'rad', [(i, i ^ k) for i in range(groups)])]
    ppermute x2 -> x30, waiting for transfers between devices: 2.66 us -> 44.5 us  [the longest x28 42.4 us: exchange(): lax.ppermute(messages[k], 'rad', [(i, i ^ k) for i in range(groups)])]
    pallas_call x0 -> x7, Pallas kernels: none -> 28.3 us  [the longest x2 13.3 us: product(): pl.pallas_call(functools.partial(product_kernel, groups, slabs, lower_sla...]
    slice x4 -> x1, local copies, waits for them, and re-layouts: 16.1 us -> 1.13 us  [neighbours(): after = lax.ppermute(nonlin[:, :1, :], 'rad', down)]
    reshape x2 -> x0, local copies, waits for them, and re-layouts: 7.48 us -> none  [the longest x1 4.94 us: local(): return returned.reshape(2, levels, groups * width)]
  transfers between devices with their start and end apart: 3 -> 30, of which waited for: 3 -> 12; matrix products, arithmetic and copies ran while one was open for 0% -> 0% of each run, Pallas kernels for 0% -> 16%
where the time goes in v1:
time: 132 us
  starting transfers between devices  52 us (39%)
  waiting for transfers between devices  44.5 us (34%)
  Pallas kernels  28.3 us (21%)
  local copies, waits for them, and re-layouts  5.86 us (4%)
    ppermute x28, starting transfers between devices, exchange(): lax.ppermute(messages[k], 'rad', [(i, i ^ k) for i in range(groups)])  45.3 us
    ppermute x28, waiting for transfers between devices, exchange(): lax.ppermute(messages[k], 'rad', [(i, i ^ k) for i in range(groups)])  42.4 us
    pallas_call x2, Pallas kernels, product(): pl.pallas_call(functools.partial(product_kernel, groups, slabs, lower_sla...  13.3 us
    pallas_call x2, Pallas kernels, result(): pl.pallas_call(functools.partial(result_kernel, groups, slabs), out_shape...  7.34 us
    pallas_call x2, Pallas kernels, right_side(): pl.pallas_call(functools.partial(right_side_kernel, groups, slabs), out_s...  6.46 us
    unnamed x8, local copies, waits for them, and re-layouts  4.73 us
    ppermute x1, starting transfers between devices, neighbours(): before = lax.ppermute(nonlin[:, -1:, :], 'rad', up)  3.43 us
    ppermute x1, starting transfers between devices, neighbours(): after = lax.ppermute(nonlin[:, :1, :], 'rad', down)  3.31 us
  transfers between devices with their start and end apart: 30, of which 12 were waited for; matrix products, arithmetic and copies ran while one was open for 0% of the time, Pallas kernels for 16%

profile of v1, /device:TPU:8, one launch (start us, length us, event | category | flops | bytes accessed | tf_op | source)
XLA Modules:
  0.0 131.5 jit_solution(14524501873534284595)
XLA Ops:
  1.1 3.4 %collective-permute-start = (bf16[2,1,8192]{2,1,0:T(2,128)(2,1)S(1)}, bf16[2,1,8192]{2,1,0:T(2,128)(2,1)S(1)}, u32[]{:S(2)}, u32[]{:S(2)}) collective-permute-start(bf16[2,1,8192]{2,1,0:T(2,128)(2,1)S(1)} %get-tuple-element.74), channel_id=1, source_target_pairs={{0,4},{4,8},{8,12},{12,16},{16,20},{20,24},{24,28},{1,5},{5,9},{9,... | collective-permute-start | bytes 98312 | tf_op jit(solution)/shard_map/ppermute | solution.py:192
  4.6 3.3 %collective-permute-start.1 = (bf16[2,1,8192]{2,1,0:T(2,128)(2,1)S(1)}, bf16[2,1,8192]{2,1,0:T(2,128)(2,1)S(1)}, u32[]{:S(2)}, u32[]{:S(2)}) collective-permute-start(bf16[2,1,8192]{2,1,0:T(2,128)(2,1)S(1)} %get-tuple-element.73), channel_id=1, source_target_pairs={{4,0},{8,4},{12,8},{16,12},{20,16},{24,20},{28,24},{5,1},{9,5},{13... | collective-permute-start | bytes 98312 | tf_op jit(solution)/shard_map/ppermute | solution.py:193
  10.7 2.2 %copy-done = f32[2,64,8192]{2,1,0:T(8,128)S(1)} copy-done((f32[2,64,8192]{2,1,0:T(8,128)S(1)}, f32[2,64,8192]{2,1,0:T(8,128)}, u32[]{:S(2)}) %copy-start) | copy-done | bytes 4194328
  15.5 3.2 %right_side.2 = (s16[528,128]{1,0:T(8,128)(2,1)S(1)}, s16[528,128]{1,0:T(8,128)(2,1)S(1)}, s16[528,128]{1,0:T(8,128)(2,1)S(1)}, s16[528,128]{1,0:T(8,128)(2,1)S(...) custom-call(s32[2]{0:T(128)S(1)} %pad_add_fusion.where, ...), custom_call_target="tpu_custom_call" | custom-call | flops 4194304 | bytes 4194304 | tf_op jit(solution)/shard_map/right_side/pallas_call | solution.py:218
  18.7 2.5 %collective-permute-start.2 = (s16[528,128]{1,0:T(8,128)(2,1)S(1)}, s16[528,128]{1,0:T(8,128)(2,1)S(1)}, u32[]{:S(2)}, u32[]{:S(2)}) collective-permute-start(s16[528,128]{1,0:T(8,128)(2,1)S(1)} %get-tuple-element.40), channel_id=1, source_target_pairs={{0,4},{4,0},{8,12},{12,8},{16,20},{20,16},{24,28},{28,24},{1,5},{5... | collective-permute-start | bytes 405512 | tf_op jit(solution)/shard_map/ppermute | solution.py:185
  22.7 2.1 %collective-permute-start.5 = (s16[528,128]{1,0:T(8,128)(2,1)S(1)}, s16[528,128]{1,0:T(8,128)(2,1)S(1)}, u32[]{:S(2)}, u32[]{:S(2)}) collective-permute-start(s16[528,128]{1,0:T(8,128)(2,1)S(1)} %get-tuple-element.43), channel_id=1, source_target_pairs={{0,16},{4,20},{8,24},{12,28},{16,0},{20,4},{24,8},{28,12},{1,17},{... | collective-permute-start | bytes 405512 | tf_op jit(solution)/shard_map/ppermute | solution.py:185
  24.9 2.2 %collective-permute-start.6 = (s16[528,128]{1,0:T(8,128)(2,1)S(1)}, s16[528,128]{1,0:T(8,128)(2,1)S(1)}, u32[]{:S(2)}, u32[]{:S(2)}) collective-permute-start(s16[528,128]{1,0:T(8,128)(2,1)S(1)} %get-tuple-element.44), channel_id=1, source_target_pairs={{0,20},{4,16},{8,28},{12,24},{16,4},{20,0},{24,12},{28,8},{1,21},{... | collective-permute-start | bytes 405512 | tf_op jit(solution)/shard_map/ppermute | solution.py:185
  27.1 3.2 %right_side.3 = (s16[528,128]{1,0:T(8,128)(2,1)S(1)}, s16[528,128]{1,0:T(8,128)(2,1)S(1)}, s16[528,128]{1,0:T(8,128)(2,1)S(1)}, s16[528,128]{1,0:T(8,128)(2,1)S(...) custom-call(s32[2]{0:T(128)S(1)} %pad_add_fusion.where, ...), custom_call_target="tpu_custom_call" | custom-call | flops 4194304 | bytes 4194304 | tf_op jit(solution)/shard_map/right_side/pallas_call | solution.py:218
  33.9 2.8 %collective-permute-done.5.refs_4_ = s16[528,128]{1,0:T(8,128)(2,1)S(1)} collective-permute-done((s16[528,128]{1,0:T(8,128)(2,1)S(1)}, s16[528,128]{1,0:T(8,128)(2,1)S(1)}, u32[]{:S(2)}, u32[]{:S(2)}) %collective-permute-start.5) | collective-permute-done | bytes 135200 | tf_op jit(solution)/shard_map/ppermute | solution.py:185
  37.9 4.2 %collective-permute-done.6.refs_5_ = s16[528,128]{1,0:T(8,128)(2,1)S(1)} collective-permute-done((s16[528,128]{1,0:T(8,128)(2,1)S(1)}, s16[528,128]{1,0:T(8,128)(2,1)S(1)}, u32[]{:S(2)}, u32[]{:S(2)}) %collective-permute-start.6) | collective-permute-done | bytes 135200 | tf_op jit(solution)/shard_map/ppermute | solution.py:185
  42.1 3.6 %collective-permute-start.18 = (s16[528,128]{1,0:T(8,128)(2,1)S(1)}, s16[528,128]{1,0:T(8,128)(2,1)S(1)}, u32[]{:S(2)}, u32[]{:S(2)}) collective-permute-start(s16[528,128]{1,0:T(8,128)(2,1)S(1)} %get-tuple-element.60), channel_id=1, source_target_pairs={{0,12},{4,8},{8,4},{12,0},{16,28},{20,24},{24,20},{28,16},{1,13},{... | collective-permute-start | bytes 405512 | tf_op jit(solution)/shard_map/ppermute | solution.py:185
  46.6 10.7 %collective-permute-done.8.refs_7_ = s16[528,128]{1,0:T(8,128)(2,1)S(1)} collective-permute-done((s16[528,128]{1,0:T(8,128)(2,1)S(1)}, s16[528,128]{1,0:T(8,128)(2,1)S(1)}, u32[]{:S(2)}, u32[]{:S(2)}) %collective-permute-start.8) | collective-permute-done | bytes 135200 | tf_op jit(solution)/shard_map/ppermute | solution.py:185
  58.7 6.6 %product.2 = (s16[528,128]{1,0:T(8,128)(2,1)S(1)}, s16[528,128]{1,0:T(8,128)(2,1)S(1)}, s16[528,128]{1,0:T(8,128)(2,1)S(1)}, s16[528,128]{1,0:T(8,128)(2,1)S(1)}...) custom-call(s32[2]{0:T(128)S(1)} %pad_add_fusion.where, ...), custom_call_target="tpu_custom_call" | custom-call | flops 3221225472 | bytes 10485760 | tf_op jit(solution)/shard_map/product/pallas_call | solution.py:254
  67.5 4.6 %collective-permute-start.10 = (s16[528,128]{1,0:T(8,128)(2,1)S(1)}, s16[528,128]{1,0:T(8,128)(2,1)S(1)}, u32[]{:S(2)}, u32[]{:S(2)}) collective-permute-start(s16[528,128]{1,0:T(8,128)(2,1)S(1)} %get-tuple-element.51), channel_id=1, source_target_pairs={{0,8},{4,12},{8,0},{12,4},{16,24},{20,28},{24,16},{28,20},{1,9},{5... | collective-permute-start | bytes 405512 | tf_op jit(solution)/shard_map/ppermute | solution.py:185
  72.1 6.6 %product.3 = (s16[528,128]{1,0:T(8,128)(2,1)S(1)}, s16[528,128]{1,0:T(8,128)(2,1)S(1)}, s16[528,128]{1,0:T(8,128)(2,1)S(1)}, s16[528,128]{1,0:T(8,128)(2,1)S(1)}...) custom-call(s32[2]{0:T(128)S(1)} %pad_add_fusion.where, ...), custom_call_target="tpu_custom_call" | custom-call | flops 3221225472 | bytes 10485760 | tf_op jit(solution)/shard_map/product/pallas_call | solution.py:254
  79.9 2.4 %collective-permute-start.25 = (s16[528,128]{1,0:T(8,128)(2,1)S(1)}, s16[528,128]{1,0:T(8,128)(2,1)S(1)}, u32[]{:S(2)}, u32[]{:S(2)}) collective-permute-start(s16[528,128]{1,0:T(8,128)(2,1)S(1)} %get-tuple-element.68), channel_id=1, source_target_pairs={{0,12},{4,8},{8,4},{12,0},{16,28},{20,24},{24,20},{28,16},{1,13},{... | collective-permute-start | bytes 405512 | tf_op jit(solution)/shard_map/ppermute | solution.py:185
  82.4 3.4 %collective-permute-start.27 = (s16[528,128]{1,0:T(8,128)(2,1)S(1)}, s16[528,128]{1,0:T(8,128)(2,1)S(1)}, u32[]{:S(2)}, u32[]{:S(2)}) collective-permute-start(s16[528,128]{1,0:T(8,128)(2,1)S(1)} %get-tuple-element.70), channel_id=1, source_target_pairs={{0,20},{4,16},{8,28},{12,24},{16,4},{20,0},{24,12},{28,8},{1,21},{... | collective-permute-start | bytes 405512 | tf_op jit(solution)/shard_map/ppermute | solution.py:185
  92.7 3.4 %collective-permute-start.12 = (s16[528,128]{1,0:T(8,128)(2,1)S(1)}, s16[528,128]{1,0:T(8,128)(2,1)S(1)}, u32[]{:S(2)}, u32[]{:S(2)}) collective-permute-start(s16[528,128]{1,0:T(8,128)(2,1)S(1)} %get-tuple-element.53), channel_id=1, source_target_pairs={{0,16},{4,20},{8,24},{12,28},{16,0},{20,4},{24,8},{28,12},{1,17},{... | collective-permute-start | bytes 405512 | tf_op jit(solution)/shard_map/ppermute | solution.py:185
  96.0 10.2 %collective-permute-done.27.refs_5_ = s16[528,128]{1,0:T(8,128)(2,1)S(1)} collective-permute-done((s16[528,128]{1,0:T(8,128)(2,1)S(1)}, s16[528,128]{1,0:T(8,128)(2,1)S(1)}, u32[]{:S(2)}, u32[]{:S(2)}) %collective-permute-start.27) | collective-permute-done | bytes 135200 | tf_op jit(solution)/shard_map/ppermute | solution.py:185
  106.3 4.4 %collective-permute-start.13 = (s16[528,128]{1,0:T(8,128)(2,1)S(1)}, s16[528,128]{1,0:T(8,128)(2,1)S(1)}, u32[]{:S(2)}, u32[]{:S(2)}) collective-permute-start(s16[528,128]{1,0:T(8,128)(2,1)S(1)} %get-tuple-element.54), channel_id=1, source_target_pairs={{0,20},{4,16},{8,28},{12,24},{16,4},{20,0},{24,12},{28,8},{1,21},{... | collective-permute-start | bytes 405512 | tf_op jit(solution)/shard_map/ppermute | solution.py:185
  111.8 6.9 %collective-permute-done.29.refs_7_ = s16[528,128]{1,0:T(8,128)(2,1)S(1)} collective-permute-done((s16[528,128]{1,0:T(8,128)(2,1)S(1)}, s16[528,128]{1,0:T(8,128)(2,1)S(1)}, u32[]{:S(2)}, u32[]{:S(2)}) %collective-permute-start.29) | collective-permute-done | bytes 135200 | tf_op jit(solution)/shard_map/ppermute | solution.py:185
  119.9 3.7 %result.2.refs_8_ = f32[2,64,8192]{2,1,0:T(8,128)} custom-call(s32[2]{0:T(128)S(1)} %pad_add_fusion.where, s16[528,128]{1,0:T(8,128)(2,1)S(1)} %get-tuple-element.65.refs_0_, s16[528,128]{1,0:T(8,128)(2,1)S(1)} %collective-permute-done.23.refs_1_, s16[528,128]{1,0:T(8,128)(2,1)S(1)} %collective-permute-done.24.refs_2_, ...), custom_call_target="tpu_custom_call" | custom-call | flops 1048576 | bytes 3145728 | tf_op jit(solution)/shard_map/result/pallas_call | solution.py:281
  123.6 2.4 %collective-permute-done.14.refs_6_ = s16[528,128]{1,0:T(8,128)(2,1)S(1)} collective-permute-done((s16[528,128]{1,0:T(8,128)(2,1)S(1)}, s16[528,128]{1,0:T(8,128)(2,1)S(1)}, u32[]{:S(2)}, u32[]{:S(2)}) %collective-permute-start.14) | collective-permute-done | bytes 135200 | tf_op jit(solution)/shard_map/ppermute | solution.py:185
  127.8 3.7 %result.3 = f32[2,64,8192]{2,1,0:T(8,128)} custom-call(s32[2]{0:T(128)S(1)} %pad_add_fusion.where, s16[528,128]{1,0:T(8,128)(2,1)S(1)} %get-tuple-element.49.refs_0_, s16[528,128]{1,0:T(8,128)(2,1)S(1)} %collective-permute-done.9.refs_1_, s16[528,128]{1,0:T(8,128)(2,1)S(1)} %collective-permute-done.10.refs_2_, ...), custom_call_target="tpu_custom_call", output_to_operand_aliasing={{}: (9, {})} | custom-call | flops 1048576 | bytes 3145728 | tf_op jit(solution)/shard_map/result/pallas_call | solution.py:281
  (53 shorter events, 29.0 us)
Async XLA Ops:
  18.7 11.6 %collective-permute-start.2 = (s16[528,128]{1,0:T(8,128)(2,1)S(1)}, s16[528,128]{1,0:T(8,128)(2,1)S(1)}, u32[]{:S(2)}, u32[]{:S(2)}) collective-permute-start(s16[528,128]{1,0:T(8,128)(2,1)S(1)} %get-tuple-element.40), channel_id=1, source_target_pairs={{0,4},{4,0},{8,12},{12,8},{16,20},{20,16},{24,28},{28,24},{1,5},{5... | collective-permute-start | bytes 405512 | tf_op jit(solution)/shard_map/ppermute | solution.py:185
  21.2 10.7 %collective-permute-start.3 = (s16[528,128]{1,0:T(8,128)(2,1)S(1)}, s16[528,128]{1,0:T(8,128)(2,1)S(1)}, u32[]{:S(2)}, u32[]{:S(2)}) collective-permute-start(s16[528,128]{1,0:T(8,128)(2,1)S(1)} %get-tuple-element.41), channel_id=1, source_target_pairs={{0,8},{4,12},{8,0},{12,4},{16,24},{20,28},{24,16},{28,20},{1,9},{5... | collective-permute-start | bytes 405512 | tf_op jit(solution)/shard_map/ppermute | solution.py:185
  21.7 10.3 %collective-permute-start.4 = (s16[528,128]{1,0:T(8,128)(2,1)S(1)}, s16[528,128]{1,0:T(8,128)(2,1)S(1)}, u32[]{:S(2)}, u32[]{:S(2)}) collective-permute-start(s16[528,128]{1,0:T(8,128)(2,1)S(1)} %get-tuple-element.42), channel_id=1, source_target_pairs={{0,12},{4,8},{8,4},{12,0},{16,28},{20,24},{24,20},{28,16},{1,13},{... | collective-permute-start | bytes 405512 | tf_op jit(solution)/shard_map/ppermute | solution.py:185
  22.7 13.9 %collective-permute-start.5 = (s16[528,128]{1,0:T(8,128)(2,1)S(1)}, s16[528,128]{1,0:T(8,128)(2,1)S(1)}, u32[]{:S(2)}, u32[]{:S(2)}) collective-permute-start(s16[528,128]{1,0:T(8,128)(2,1)S(1)} %get-tuple-element.43), channel_id=1, source_target_pairs={{0,16},{4,20},{8,24},{12,28},{16,0},{20,4},{24,8},{28,12},{1,17},{... | collective-permute-start | bytes 405512 | tf_op jit(solution)/shard_map/ppermute | solution.py:185
  24.9 17.2 %collective-permute-start.6 = (s16[528,128]{1,0:T(8,128)(2,1)S(1)}, s16[528,128]{1,0:T(8,128)(2,1)S(1)}, u32[]{:S(2)}, u32[]{:S(2)}) collective-permute-start(s16[528,128]{1,0:T(8,128)(2,1)S(1)} %get-tuple-element.44), channel_id=1, source_target_pairs={{0,20},{4,16},{8,28},{12,24},{16,4},{20,0},{24,12},{28,8},{1,21},{... | collective-permute-start | bytes 405512 | tf_op jit(solution)/shard_map/ppermute | solution.py:185
  30.3 15.9 %collective-permute-start.7 = (s16[528,128]{1,0:T(8,128)(2,1)S(1)}, s16[528,128]{1,0:T(8,128)(2,1)S(1)}, u32[]{:S(2)}, u32[]{:S(2)}) collective-permute-start(s16[528,128]{1,0:T(8,128)(2,1)S(1)} %get-tuple-element.45), channel_id=1, source_target_pairs={{0,24},{4,28},{8,16},{12,20},{16,8},{20,12},{24,0},{28,4},{1,25},{... | collective-permute-start | bytes 405512 | tf_op jit(solution)/shard_map/ppermute | solution.py:185
  31.9 25.3 %collective-permute-start.8 = (s16[528,128]{1,0:T(8,128)(2,1)S(1)}, s16[528,128]{1,0:T(8,128)(2,1)S(1)}, u32[]{:S(2)}, u32[]{:S(2)}) collective-permute-start(s16[528,128]{1,0:T(8,128)(2,1)S(1)} %get-tuple-element.46), channel_id=1, source_target_pairs={{0,28},{4,24},{8,20},{12,16},{16,12},{20,8},{24,4},{28,0},{1,29},{... | collective-permute-start | bytes 405512 | tf_op jit(solution)/shard_map/ppermute | solution.py:185
  31.9 25.3 %collective-permute-start.16 = (s16[528,128]{1,0:T(8,128)(2,1)S(1)}, s16[528,128]{1,0:T(8,128)(2,1)S(1)}, u32[]{:S(2)}, u32[]{:S(2)}) collective-permute-start(s16[528,128]{1,0:T(8,128)(2,1)S(1)} %get-tuple-element.58), channel_id=1, source_target_pairs={{0,4},{4,0},{8,12},{12,8},{16,20},{20,16},{24,28},{28,24},{1,5},{5... | collective-permute-start | bytes 405512 | tf_op jit(solution)/shard_map/ppermute | solution.py:185
  36.6 21.6 %collective-permute-start.17 = (s16[528,128]{1,0:T(8,128)(2,1)S(1)}, s16[528,128]{1,0:T(8,128)(2,1)S(1)}, u32[]{:S(2)}, u32[]{:S(2)}) collective-permute-start(s16[528,128]{1,0:T(8,128)(2,1)S(1)} %get-tuple-element.59), channel_id=1, source_target_pairs={{0,8},{4,12},{8,0},{12,4},{16,24},{20,28},{24,16},{28,20},{1,9},{5... | collective-permute-start | bytes 405512 | tf_op jit(solution)/shard_map/ppermute | solution.py:185
  42.1 23.3 %collective-permute-start.18 = (s16[528,128]{1,0:T(8,128)(2,1)S(1)}, s16[528,128]{1,0:T(8,128)(2,1)S(1)}, u32[]{:S(2)}, u32[]{:S(2)}) collective-permute-start(s16[528,128]{1,0:T(8,128)(2,1)S(1)} %get-tuple-element.60), channel_id=1, source_target_pairs={{0,12},{4,8},{8,4},{12,0},{16,28},{20,24},{24,20},{28,16},{1,13},{... | collective-permute-start | bytes 405512 | tf_op jit(solution)/shard_map/ppermute | solution.py:185
  46.2 21.2 %collective-permute-start.19 = (s16[528,128]{1,0:T(8,128)(2,1)S(1)}, s16[528,128]{1,0:T(8,128)(2,1)S(1)}, u32[]{:S(2)}, u32[]{:S(2)}) collective-permute-start(s16[528,128]{1,0:T(8,128)(2,1)S(1)} %get-tuple-element.61), channel_id=1, source_target_pairs={{0,16},{4,20},{8,24},{12,28},{16,0},{20,4},{24,8},{28,12},{1,17},{... | collective-permute-start | bytes 405512 | tf_op jit(solution)/shard_map/ppermute | solution.py:185
  57.2 14.9 %collective-permute-start.20 = (s16[528,128]{1,0:T(8,128)(2,1)S(1)}, s16[528,128]{1,0:T(8,128)(2,1)S(1)}, u32[]{:S(2)}, u32[]{:S(2)}) collective-permute-start(s16[528,128]{1,0:T(8,128)(2,1)S(1)} %get-tuple-element.62), channel_id=1, source_target_pairs={{0,20},{4,16},{8,28},{12,24},{16,4},{20,0},{24,12},{28,8},{1,21},{... | collective-permute-start | bytes 405512 | tf_op jit(solution)/shard_map/ppermute | solution.py:185
  57.2 14.9 %collective-permute-start.21 = (s16[528,128]{1,0:T(8,128)(2,1)S(1)}, s16[528,128]{1,0:T(8,128)(2,1)S(1)}, u32[]{:S(2)}, u32[]{:S(2)}) collective-permute-start(s16[528,128]{1,0:T(8,128)(2,1)S(1)} %get-tuple-element.63), channel_id=1, source_target_pairs={{0,24},{4,28},{8,16},{12,20},{16,8},{20,12},{24,0},{28,4},{1,25},{... | collective-permute-start | bytes 405512 | tf_op jit(solution)/shard_map/ppermute | solution.py:185
  58.3 13.8 %collective-permute-start.22 = (s16[528,128]{1,0:T(8,128)(2,1)S(1)}, s16[528,128]{1,0:T(8,128)(2,1)S(1)}, u32[]{:S(2)}, u32[]{:S(2)}) collective-permute-start(s16[528,128]{1,0:T(8,128)(2,1)S(1)} %get-tuple-element.64), channel_id=1, source_target_pairs={{0,28},{4,24},{8,20},{12,16},{16,12},{20,8},{24,4},{28,0},{1,29},{... | collective-permute-start | bytes 405512 | tf_op jit(solution)/shard_map/ppermute | solution.py:185
  65.4 17.0 %collective-permute-start.9 = (s16[528,128]{1,0:T(8,128)(2,1)S(1)}, s16[528,128]{1,0:T(8,128)(2,1)S(1)}, u32[]{:S(2)}, u32[]{:S(2)}) collective-permute-start(s16[528,128]{1,0:T(8,128)(2,1)S(1)} %get-tuple-element.50), channel_id=1, source_target_pairs={{0,4},{4,0},{8,12},{12,8},{16,20},{20,16},{24,28},{28,24},{1,5},{5... | collective-permute-start | bytes 405512 | tf_op jit(solution)/shard_map/ppermute | solution.py:185
  67.5 14.9 %collective-permute-start.10 = (s16[528,128]{1,0:T(8,128)(2,1)S(1)}, s16[528,128]{1,0:T(8,128)(2,1)S(1)}, u32[]{:S(2)}, u32[]{:S(2)}) collective-permute-start(s16[528,128]{1,0:T(8,128)(2,1)S(1)} %get-tuple-element.51), channel_id=1, source_target_pairs={{0,8},{4,12},{8,0},{12,4},{16,24},{20,28},{24,16},{28,20},{1,9},{5... | collective-permute-start | bytes 405512 | tf_op jit(solution)/shard_map/ppermute | solution.py:185
  82.3 10.4 %collective-permute-start.26 = (s16[528,128]{1,0:T(8,128)(2,1)S(1)}, s16[528,128]{1,0:T(8,128)(2,1)S(1)}, u32[]{:S(2)}, u32[]{:S(2)}) collective-permute-start(s16[528,128]{1,0:T(8,128)(2,1)S(1)} %get-tuple-element.69), channel_id=1, source_target_pairs={{0,16},{4,20},{8,24},{12,28},{16,0},{20,4},{24,8},{28,12},{1,17},{... | collective-permute-start | bytes 405512 | tf_op jit(solution)/shard_map/ppermute | solution.py:185
  82.4 23.9 %collective-permute-start.27 = (s16[528,128]{1,0:T(8,128)(2,1)S(1)}, s16[528,128]{1,0:T(8,128)(2,1)S(1)}, u32[]{:S(2)}, u32[]{:S(2)}) collective-permute-start(s16[528,128]{1,0:T(8,128)(2,1)S(1)} %get-tuple-element.70), channel_id=1, source_target_pairs={{0,20},{4,16},{8,28},{12,24},{16,4},{20,0},{24,12},{28,8},{1,21},{... | collective-permute-start | bytes 405512 | tf_op jit(solution)/shard_map/ppermute | solution.py:185
  85.8 25.1 %collective-permute-start.28 = (s16[528,128]{1,0:T(8,128)(2,1)S(1)}, s16[528,128]{1,0:T(8,128)(2,1)S(1)}, u32[]{:S(2)}, u32[]{:S(2)}) collective-permute-start(s16[528,128]{1,0:T(8,128)(2,1)S(1)} %get-tuple-element.71), channel_id=1, source_target_pairs={{0,24},{4,28},{8,16},{12,20},{16,8},{20,12},{24,0},{28,4},{1,25},{... | collective-permute-start | bytes 405512 | tf_op jit(solution)/shard_map/ppermute | solution.py:185
  86.8 31.9 %collective-permute-start.29 = (s16[528,128]{1,0:T(8,128)(2,1)S(1)}, s16[528,128]{1,0:T(8,128)(2,1)S(1)}, u32[]{:S(2)}, u32[]{:S(2)}) collective-permute-start(s16[528,128]{1,0:T(8,128)(2,1)S(1)} %get-tuple-element.72), channel_id=1, source_target_pairs={{0,28},{4,24},{8,20},{12,16},{16,12},{20,8},{24,4},{28,0},{1,29},{... | collective-permute-start | bytes 405512 | tf_op jit(solution)/shard_map/ppermute | solution.py:185
  89.7 33.9 %collective-permute-start.11 = (s16[528,128]{1,0:T(8,128)(2,1)S(1)}, s16[528,128]{1,0:T(8,128)(2,1)S(1)}, u32[]{:S(2)}, u32[]{:S(2)}) collective-permute-start(s16[528,128]{1,0:T(8,128)(2,1)S(1)} %get-tuple-element.52), channel_id=1, source_target_pairs={{0,12},{4,8},{8,4},{12,0},{16,28},{20,24},{24,20},{28,16},{1,13},{... | collective-permute-start | bytes 405512 | tf_op jit(solution)/shard_map/ppermute | solution.py:185
  92.7 30.9 %collective-permute-start.12 = (s16[528,128]{1,0:T(8,128)(2,1)S(1)}, s16[528,128]{1,0:T(8,128)(2,1)S(1)}, u32[]{:S(2)}, u32[]{:S(2)}) collective-permute-start(s16[528,128]{1,0:T(8,128)(2,1)S(1)} %get-tuple-element.53), channel_id=1, source_target_pairs={{0,16},{4,20},{8,24},{12,28},{16,0},{20,4},{24,8},{28,12},{1,17},{... | collective-permute-start | bytes 405512 | tf_op jit(solution)/shard_map/ppermute | solution.py:185
  106.3 17.3 %collective-permute-start.13 = (s16[528,128]{1,0:T(8,128)(2,1)S(1)}, s16[528,128]{1,0:T(8,128)(2,1)S(1)}, u32[]{:S(2)}, u32[]{:S(2)}) collective-permute-start(s16[528,128]{1,0:T(8,128)(2,1)S(1)} %get-tuple-element.54), channel_id=1, source_target_pairs={{0,20},{4,16},{8,28},{12,24},{16,4},{20,0},{24,12},{28,8},{1,21},{... | collective-permute-start | bytes 405512 | tf_op jit(solution)/shard_map/ppermute | solution.py:185
  110.8 15.2 %collective-permute-start.14 = (s16[528,128]{1,0:T(8,128)(2,1)S(1)}, s16[528,128]{1,0:T(8,128)(2,1)S(1)}, u32[]{:S(2)}, u32[]{:S(2)}) collective-permute-start(s16[528,128]{1,0:T(8,128)(2,1)S(1)} %get-tuple-element.55), channel_id=1, source_target_pairs={{0,24},{4,28},{8,16},{12,20},{16,8},{20,12},{24,0},{28,4},{1,25},{... | collective-permute-start | bytes 405512 | tf_op jit(solution)/shard_map/ppermute | solution.py:185
  (10 other events, 72.4 us)

commit v2 on v1

v2 whole, which is shorter than its diff:
```python
import functools
import math

import jax
import jax.numpy as jnp
import numpy as np
from jax import lax
from jax.experimental import pallas as pl
from jax.experimental.pallas import tpu as pltpu
from jax.sharding import PartitionSpec as P

inner_radius = 0.35
outer_radius = 1.0
blend_weight = 0.5

LANES = 128
TILE = 16
CHUNKS = 2
TOP = 32700.0
EDGE_TOP = 16384.0
FINE = 128.0
MIB = 1024 * 1024


def radius_at(level_index, total_levels):
    scaled = level_index / (total_levels - 1.0)
    stretch = (1.0 - blend_weight) * scaled + blend_weight * (1.0 - np.cos(math.pi * scaled)) / 2.0
    return inner_radius + (outer_radius - inner_radius) * stretch


def stencil_table(total_levels):
    k = np.arange(total_levels, dtype=np.float64)
    radius = radius_at(k, total_levels)
    below = radius - radius_at(k - 1.0, total_levels)
    above = radius_at(k + 1.0, total_levels) - radius
    at_inner, at_outer = k == 0, k == total_levels - 1
    weight_below = np.where(at_inner, 0.0, np.where(at_outer, -1.0 / below, -above / (below * (below + above))))
    weight_here = np.where(
        at_inner, -1.0 / above, np.where(at_outer, 1.0 / below, (above - below) / (below * above))
    )
    weight_above = np.where(at_inner, 1.0 / above, np.where(at_outer, 0.0, below / (above * (below + above))))
    time_step = 0.5 * (outer_radius - inner_radius) / (total_levels - 1.0)
    table = np.zeros((total_levels, LANES), np.float32)
    table[:, 0] = time_step * weight_below
    table[:, 1] = time_step * (weight_here + 2.0 / radius)
    table[:, 2] = time_step * weight_above
    return table


def scale_code(values, per_octave):
    largest = jnp.maximum(jnp.max(jnp.abs(values), axis=0, keepdims=True), 1e-30)
    return jnp.ceil(jnp.log2(largest) * per_octave) * (FINE / per_octave)


def encode(values, code, top):
    scaled = values * (jnp.exp2(code * (-1.0 / FINE)) * top)
    return jnp.clip(jnp.round(scaled), -32767.0, 32767.0)


def to_int16(values):
    return values.astype(jnp.int32).astype(jnp.int16)


def to_float(codes):
    return codes.astype(jnp.int32).astype(jnp.float32)


def scale_of(codes, top):
    return jnp.exp2(to_float(codes) * (1.0 / FINE)) * (1.0 / top)


def padded_rows(parts, rows):
    used = sum(p.shape[0] for p in parts)
    return jnp.concatenate(parts + [jnp.zeros((rows - used, LANES), jnp.float32)], axis=0)


def tile_rows(rows):
    return -(-rows // TILE) * TILE


def right_side_kernel(partners, parts, slabs, where, n_ref, s_ref, tab_ref, *outs):
    levels = n_ref.shape[1]
    rows = 2 * levels
    step = pl.program_id(0)
    tab = tab_ref[...]
    below, here, above = (jnp.broadcast_to(tab[:, i : i + 1], (levels, LANES)) for i in range(3))
    row = lax.broadcasted_iota(jnp.int32, (levels, LANES), 0)
    for at, _ in enumerate(partners):

        @pl.when(step == at)
        def _():
            for part in range(parts):
                codes, edge_codes, edges = [], [], []
                for slab in range(slabs):
                    cols = slice((part * slabs + slab) * LANES, (part * slabs + slab + 1) * LANES)
                    fields, ends = [], []
                    for f in range(2):
                        n = n_ref[f, :, cols].astype(jnp.float32)
                        prev = jnp.where(row == 0, n, pltpu.roll(n, 1, 0))
                        succ = jnp.where(row == levels - 1, n, pltpu.roll(n, levels - 1, 0))
                        fields.append(s_ref[f, :, cols] + (below * prev + here * n + above * succ))
                        ends += [n[:1], n[levels - 1 :]]
                    both = jnp.concatenate(fields, axis=0)
                    code = scale_code(both, FINE)
                    codes.append(code)
                    outs[at][part, slab * rows : (slab + 1) * rows, :] = to_int16(encode(both, code, TOP))
                    ends = jnp.concatenate(ends, axis=0)
                    code = scale_code(ends, 1.0)
                    edge_codes.append(code)
                    edges.append(encode(ends, code, EDGE_TOP))
                extra = outs[at].shape[1] - slabs * rows
                outs[at][part, slabs * rows :, :] = to_int16(padded_rows(edges + edge_codes + codes, extra))


def split_kernel(a_ref, hi_ref, lo_ref):
    a = a_ref[...]
    hi = a.astype(jnp.bfloat16)
    hi_ref[...] = hi
    lo_ref[...] = (a - hi.astype(jnp.float32)).astype(jnp.bfloat16)


def product_kernel(groups, slabs, lower_slabs, first_col, half_cols, places, carried, outs_at, where, edge_weight, *refs):
    ins, (hi_ref, lo_ref), refs = refs[:groups], refs[groups : groups + 2], refs[groups + 2 :]
    earlier, refs = refs[: len(carried)], refs[len(carried) :]
    outs, (v_hi, v_lo, y, edges) = refs[:groups], refs[groups:]
    size = y.shape[0]
    levels = size // (2 * groups)
    rows = 2 * levels
    me = where[0]
    pair = where[1]
    peers = [lax.bitwise_xor(me, k) for k in range(groups)]
    for k, ref in zip(carried, earlier):
        outs[k][: outs_at[k]] = ref[...]

    extra = []
    for k in range(groups):
        extra.append(ins[k][places[k], slabs * rows :, :])
        for slab in range(slabs):
            code = extra[k][4 * slabs + slab : 4 * slabs + slab + 1]
            edges[peers[k], :, slab * LANES : (slab + 1) * LANES] = to_float(
                extra[k][4 * slab : 4 * slab + 4]
            ) * scale_of(code, EDGE_TOP)
    near = lax.broadcasted_iota(jnp.int32, (8, LANES), 0)
    for k in range(groups):
        peer = peers[k]
        before, after = jnp.maximum(peer - 1, 0), jnp.minimum(peer + 1, groups - 1)
        weight_before, weight_after = edge_weight[peer], edge_weight[groups + peer]
        for slab in range(slabs):
            cols = slice(slab * LANES, (slab + 1) * LANES)
            scale = scale_of(extra[k][5 * slabs + slab : 5 * slabs + slab + 1], TOP)
            here = edges[peer, :, cols]
            low = weight_before * (edges[before, :, cols] - here_shifted(here))
            high = weight_after * (edges[after, :, cols] - here_shifted(here))
            for f in range(2):
                at = slab * rows + f * levels
                v = to_float(ins[k][places[k], at : at + levels, :]) * scale
                first = v[:8] + jnp.where(near == 0, low[2 * f + 1 : 2 * f + 2], 0.0)
                last = v[levels - 8 :] + jnp.where(near == 7, high[2 * f : 2 * f + 1], 0.0)
                middle = [v[8 : levels - 8]] if levels > 16 else []
                v = jnp.concatenate([first] + middle + [last], axis=0)
                to = pl.ds(pl.multiple_of(f * (size // 2) + peer * levels, levels), levels)
                hi = v.astype(jnp.bfloat16)
                v_hi[to, cols] = hi
                v_lo[to, cols] = (v - hi.astype(jnp.float32)).astype(jnp.bfloat16)

    def product(which, cols):
        dot = functools.partial(jnp.dot, preferred_element_type=jnp.float32)
        return (
            dot(lo_ref[which], v_hi[:, cols])
            + dot(hi_ref[which], v_lo[:, cols])
            + dot(hi_ref[which], v_hi[:, cols])
        )

    wide = min(2 * LANES, slabs * LANES)
    for at in range(0, slabs * LANES, wide):
        y[:, at : at + wide] = product(1, slice(at, at + wide))
    for slab in range(slabs):
        first = first_col + slab * LANES
        if first % half_cols < lower_slabs * LANES:
            cols = slice(slab * LANES, (slab + 1) * LANES)
            column = first % half_cols + lax.broadcasted_iota(jnp.int32, (size, LANES), 1)
            bound = pair + 1 if first < half_cols else pair
            y[:, cols] = jnp.where(column < bound, product(0, cols), y[:, cols])

    for k in range(groups):
        codes = []
        for slab in range(slabs):
            cols = slice(slab * LANES, (slab + 1) * LANES)
            both = jnp.concatenate(
                [
                    y[pl.ds(pl.multiple_of(f * (size // 2) + peers[k] * levels, levels), levels), cols]
                    for f in range(2)
                ],
                axis=0,
            )
            code = scale_code(both, FINE)
            codes.append(code)
            outs[k][outs_at[k], slab * rows : (slab + 1) * rows, :] = to_int16(encode(both, code, TOP))
        extra_rows = outs[k].shape[1] - slabs * rows
        outs[k][outs_at[k], slabs * rows :, :] = to_int16(padded_rows(codes, extra_rows))


def here_shifted(edges):
    return jnp.concatenate([edges[1:2], edges[0:1], edges[3:4], edges[2:3]], axis=0)


def result_kernel(count, parts, slabs, where, *refs):
    ins, out_ref = refs[:count], refs[-1]
    levels = out_ref.shape[1]
    rows = 2 * levels
    step = pl.program_id(0)
    for at in range(count):

        @pl.when(step == at)
        def _():
            for part in range(parts):
                scales = scale_of(ins[at][part, slabs * rows :, :], TOP)
                for slab in range(slabs):
                    for f in range(2):
                        first = slab * rows + f * levels
                        v = to_float(ins[at][part, first : first + levels, :]) * scales[slab : slab + 1, :]
                        out_ref[f, :, (part * slabs + slab) * LANES : (part * slabs + slab + 1) * LANES] = v


def send(message, k, groups):
    return message if k == 0 else lax.ppermute(message, "rad", [(i, i ^ k) for i in range(groups)])


def xor_block(ks, chunks, first_chunk):
    def at(step, w):
        k = jnp.int32(ks[-1])
        for i, value in enumerate(ks[:-1]):
            k = jnp.where(step == i, value, k)
        return (0, 0, lax.bitwise_xor(w[0], k) * chunks + first_chunk)

    return at


def local(slots, nonlin, state, inverse, pair_of_slot):
    levels = nonlin.shape[1]
    groups = lax.axis_size("rad")
    width = nonlin.shape[2] // groups
    size = inverse.shape[-1]
    span = width // CHUNKS
    slabs = span // LANES
    rows = 2 * levels
    lower_slabs = -(-slots // LANES)
    me = lax.axis_index("rad").astype(jnp.int32)
    where = jnp.stack([me, pair_of_slot[0].astype(jnp.int32)])
    weights = stencil_table(levels * groups)
    table = jnp.asarray(weights)
    edge_weight = jnp.asarray(np.concatenate([weights[::levels, 0], weights[levels - 1 :: levels, 2]]))
    out_rows = slabs * rows + tile_rows(6 * slabs)
    back_rows = slabs * rows + tile_rows(slabs)
    vmem = pl.BlockSpec(memory_space=pltpu.VMEM)
    hbm = pl.BlockSpec(memory_space=pl.ANY)
    far = list(range(groups // 2, groups))
    near = list(range(groups // 2))

    def right_side(ks, parts, first):
        at = xor_block(ks, CHUNKS // parts, first)
        shape = (parts, out_rows, LANES)
        return pl.pallas_call(
            functools.partial(right_side_kernel, ks, parts, slabs),
            out_shape=[jax.ShapeDtypeStruct(shape, jnp.int16)] * len(ks),
            grid_spec=pltpu.PrefetchScalarGridSpec(
                num_scalar_prefetch=1,
                grid=(len(ks),),
                in_specs=[
                    pl.BlockSpec((2, levels, parts * span), at),
                    pl.BlockSpec((2, levels, parts * span), at),
                    pl.BlockSpec((levels, LANES), lambda k, w: (w[0], 0)),
                ],
                out_specs=[pl.BlockSpec(shape, lambda k, w: (0, 0, 0))] * len(ks),
            ),
            compiler_params=pltpu.CompilerParams(vmem_limit_bytes=56 * MIB),
            cost_estimate=pl.CostEstimate(flops=4 * MIB, bytes_accessed=4 * MIB, transcendentals=0),
            name="right_side",
        )(where, nonlin, state, table)

    def split():
        block = pl.BlockSpec((1, size // 4, size), lambda i, j: (i, j, 0))
        half = jax.ShapeDtypeStruct((2, size, size), jnp.bfloat16)
        return pl.pallas_call(
            split_kernel,
            out_shape=[half, half],
            grid=(2, 4),
            in_specs=[block],
            out_specs=[block, block],
            compiler_params=pltpu.CompilerParams(vmem_limit_bytes=16 * MIB),
            cost_estimate=pl.CostEstimate(flops=4 * MIB, bytes_accessed=16 * MIB, transcendentals=0),
            name="split_inverse",
        )(inverse[0])

    def product(chunk, messages, places, hi, lo, carried, outs_at):
        shapes = [
            jax.ShapeDtypeStruct((outs_at[k] + 1, back_rows, LANES), jnp.int16) for k in range(groups)
        ]
        return pl.pallas_call(
            functools.partial(
                product_kernel,
                groups,
                slabs,
                lower_slabs,
                chunk * span,
                width // 2,
                places,
                tuple(carried),
                outs_at,
            ),
            out_shape=shapes,
            grid_spec=pltpu.PrefetchScalarGridSpec(
                num_scalar_prefetch=1,
                grid=(),
                in_specs=[pl.BlockSpec(memory_space=pltpu.SMEM)] + [vmem] * (groups + 2 + len(carried)),
                out_specs=[vmem] * groups,
                scratch_shapes=[
                    pltpu.VMEM((size, span), jnp.bfloat16),
                    pltpu.VMEM((size, span), jnp.bfloat16),
                    pltpu.VMEM((size, span), jnp.float32),
                    pltpu.VMEM((groups, 4, span), jnp.float32),
                ],
            ),
            compiler_params=pltpu.CompilerParams(vmem_limit_bytes=32 * MIB),
            cost_estimate=pl.CostEstimate(
                flops=6 * size * size * span, bytes_accessed=10 * MIB, transcendentals=0
            ),
            name="product",
        )(where, edge_weight, *messages, hi, lo, *carried.values())

    def result(ks, parts, first, messages, previous):
        at = xor_block(ks, CHUNKS // parts, first)
        out_shape = jax.ShapeDtypeStruct(state.shape, jnp.float32)
        carried = [] if previous is None else [previous]
        whole = [pl.BlockSpec(m.shape, lambda k, w: (0, 0, 0)) for m in messages]
        return pl.pallas_call(
            functools.partial(result_kernel, len(ks), parts, slabs),
            out_shape=out_shape,
            grid_spec=pltpu.PrefetchScalarGridSpec(
                num_scalar_prefetch=1,
                grid=(len(ks),),
                in_specs=whole + [hbm] * len(carried),
                out_specs=pl.BlockSpec((2, levels, parts * span), at),
            ),
            input_output_aliases={} if previous is None else {len(ks) + 1: 0},
            compiler_params=pltpu.CompilerParams(vmem_limit_bytes=16 * MIB),
            cost_estimate=pl.CostEstimate(flops=MIB, bytes_accessed=3 * MIB, transcendentals=0),
            name="result",
        )(where, *messages, *carried)

    plan = [(far, 1, 0), (near, CHUNKS, 0)] + [(far, 1, c) for c in range(1, CHUNKS)]
    got = {}
    for ks, parts, first in plan:
        for k, message in zip(ks, right_side(ks, parts, first)):
            arrived = send(message, k, groups)
            for c in range(first, first + parts):
                got[k, c] = (arrived, c - first)
    hi, lo = split()
    back, made = {}, {}
    for c in range(CHUNKS):
        messages, places = zip(*[got[k, c] for k in range(groups)])
        outs_at = [c if k in near else 0 for k in range(groups)]
        carried = {k: made[k] for k in near} if c else {}
        made = dict(enumerate(product(c, messages, places, hi, lo, carried, outs_at)))
        back.update({(k, c): send(made[k], k, groups) for k in far})
    back.update({(k, 0): send(made[k], k, groups) for k in near})
    out = None
    for ks, parts, first in [(far, 1, c) for c in range(CHUNKS - 1)] + [(near, CHUNKS, 0), (far, 1, CHUNKS - 1)]:
        out = result(ks, parts, first, [back[k, first] for k in ks], out)
    return out


def solution(mesh):
    placed = (
        P(None, "rad", "ang"),
        P(None, "rad", "ang"),
        P(("ang", "rad"), None, None, None),
        P(("ang", "rad")),
    )
    slots = mesh.shape["rad"] * mesh.shape["ang"]
    return jax.shard_map(
        functools.partial(local, slots),
        mesh=mesh,
        in_specs=placed,
        out_specs=P(None, "rad", "ang"),
        check_vma=False,
    )
```

time: 132 us -> 119 us (0.902)
  waiting for transfers between devices: 44.5 us -> 26.5 us
  Pallas kernels: 28.3 us -> 37.3 us
  local copies, waits for them, and re-layouts: 5.86 us -> 3.42 us
  starting transfers between devices: 52 us -> 49.7 us
    ppermute x30 -> x22, waiting for transfers between devices: 44.5 us -> 26.5 us  [send(): lax.ppermute(message, 'rad', [(i, i ^ k) for i in range(groups)])]
    pallas_call x4 -> x6, Pallas kernels: 13.8 us -> 21.3 us  [the longest x3 14.5 us: right_side(): pl.pallas_call(functools.partial(right_side_kernel, ks, parts, slabs), ou...]
    ppermute x30 -> x22, starting transfers between devices: 52 us -> 49.7 us  [send(): lax.ppermute(message, 'rad', [(i, i ^ k) for i in range(groups)])]
    pallas_call x2, Pallas kernels: 13.3 us -> 14.6 us  [product(): pl.pallas_call(functools.partial(product_kernel, groups, slabs, lower_sla...]
    unnamed x8 -> x20, local copies, waits for them, and re-layouts: 4.73 us -> 3.42 us
  transfers between devices with their start and end apart: 30 -> 22, of which waited for: 12 -> 9; matrix products, arithmetic and copies ran while one was open for 0% -> 0% of each run, Pallas kernels for 16% -> 26%
where the time goes in v2:
time: 119 us; the launch traced here: 118 us
  starting transfers between devices  49.7 us (42%)
  Pallas kernels  37.3 us (31%)
  waiting for transfers between devices  26.5 us (22%)
  local copies, waits for them, and re-layouts  3.42 us (3%)
    ppermute x22, starting transfers between devices, send(): lax.ppermute(message, 'rad', [(i, i ^ k) for i in range(groups)])  49.7 us
    ppermute x22, waiting for transfers between devices, send(): lax.ppermute(message, 'rad', [(i, i ^ k) for i in range(groups)])  26.5 us
    pallas_call x2, Pallas kernels, product(): pl.pallas_call(functools.partial(product_kernel, groups, slabs, lower_sla...  14.6 us
    pallas_call x3, Pallas kernels, right_side(): pl.pallas_call(functools.partial(right_side_kernel, ks, parts, slabs), ou...  14.5 us
    pallas_call x3, Pallas kernels, result(): pl.pallas_call(functools.partial(result_kernel, len(ks), parts, slabs), o...  6.79 us
    unnamed x20, local copies, waits for them, and re-layouts  3.42 us
  transfers between devices with their start and end apart: 22, of which 9 were waited for; matrix products, arithmetic and copies ran while one was open for 0% of the time, Pallas kernels for 26%

profile of v2, /device:TPU:8, one launch (start us, length us, event | category | flops | bytes accessed | tf_op | source)
XLA Modules:
  0.0 118.3 jit_solution(10471882887530257669)
XLA Ops:
  1.2 4.5 %right_side.5 = (s16[1,544,128]{2,1,0:T(8,128)(2,1)}, s16[1,544,128]{2,1,0:T(8,128)(2,1)}, s16[1,544,128]{2,1,0:T(8,128)(2,1)}, s16[1,544,128]{2,1,0:T(8,128)(2,1)}) custom-call(s32[2]{0:T(128)} %pad_add_fusion.where, bf16[2,64,8192]{2,1,0:T(8,128)(2,1)} %n_ref.5, f32[2,64,8192]{2,1,0:T(8,128)} %s_ref.5, f32[512,128]{1,0:T(8,128)} %constant.10.clone.tab_ref), custom_call_target="tpu_custom_call" | custom-call | flops 4194304 | bytes 4194304 | tf_op jit(solution)/shard_map/right_side/pallas_call | solution.py:263
  5.7 2.6 %collective-permute-start.7 = (s16[1,544,128]{2,1,0:T(8,128)(2,1)}, s16[1,544,128]{2,1,0:T(8,128)(2,1)S(1)}, u32[]{:S(2)}, u32[]{:S(2)}) collective-permute-start(s16[1,544,128]{2,1,0:T(8,128)(2,1)} %get-tuple-element.45), channel_id=1, source_target_pairs={{0,16},{4,20},{8,24},{12,28},{16,0},{20,4},{24,8},{28,12},{1,17},{... | collective-permute-start | bytes 417800 | tf_op jit(solution)/shard_map/ppermute | solution.py:226
  9.7 5.4 %right_side.3 = (s16[2,544,128]{2,1,0:T(8,128)(2,1)}, s16[2,544,128]{2,1,0:T(8,128)(2,1)}, s16[2,544,128]{2,1,0:T(8,128)(2,1)}, s16[2,544,128]{2,1,0:T(8,128)(2,1)}) custom-call(s32[2]{0:T(128)} %pad_add_fusion.where, bf16[2,64,8192]{2,1,0:T(8,128)(2,1)} %n_ref.5, f32[2,64,8192]{2,1,0:T(8,128)} %s_ref.5, f32[512,128]{1,0:T(8,128)} %constant.10.clone.tab_ref), custom_call_target="tpu_custom_call" | custom-call | flops 4194304 | bytes 4194304 | tf_op jit(solution)/shard_map/right_side/pallas_call | solution.py:263
  15.8 2.8 %collective-permute-start.2 = (s16[2,544,128]{2,1,0:T(8,128)(2,1)}, s16[2,544,128]{2,1,0:T(8,128)(2,1)S(1)}, u32[]{:S(2)}, u32[]{:S(2)}) collective-permute-start(s16[2,544,128]{2,1,0:T(8,128)(2,1)} %get-tuple-element.38), channel_id=1, source_target_pairs={{0,12},{4,8},{8,4},{12,0},{16,28},{20,24},{24,20},{28,16},{1,13},{... | collective-permute-start | bytes 835592 | tf_op jit(solution)/shard_map/ppermute | solution.py:226
  21.0 4.5 %right_side.4 = (s16[1,544,128]{2,1,0:T(8,128)(2,1)}, s16[1,544,128]{2,1,0:T(8,128)(2,1)}, s16[1,544,128]{2,1,0:T(8,128)(2,1)}, s16[1,544,128]{2,1,0:T(8,128)(2,1)}) custom-call(s32[2]{0:T(128)} %pad_add_fusion.where, bf16[2,64,8192]{2,1,0:T(8,128)(2,1)} %n_ref.5, f32[2,64,8192]{2,1,0:T(8,128)} %s_ref.5, f32[512,128]{1,0:T(8,128)} %constant.10.clone.tab_ref), custom_call_target="tpu_custom_call" | custom-call | flops 4194304 | bytes 4194304 | tf_op jit(solution)/shard_map/right_side/pallas_call | solution.py:263
  25.6 3.4 %copy-done = f32[1,2,1024,1024]{3,2,1,0:T(8,128)S(1)} copy-done((f32[1,2,1024,1024]{3,2,1,0:T(8,128)S(1)}, f32[1,2,1024,1024]{3,2,1,0:T(8,128)}, u32[]{:S(2)}) %copy-start) | copy-done | bytes 8388632
  30.5 7.3 %collective-permute-start.3 = (s16[1,544,128]{2,1,0:T(8,128)(2,1)S(1)}, s16[1,544,128]{2,1,0:T(8,128)(2,1)S(1)}, u32[]{:S(2)}, u32[]{:S(2)}) collective-permute-start(s16[1,544,128]{2,1,0:T(8,128)(2,1)S(1)} %copy-done.7), channel_id=1, source_target_pairs={{0,16},{4,20},{8,24},{12,28},{16,0},{20,4},{24,8},{28,12},{1,17},{... | collective-permute-start | bytes 417800 | tf_op jit(solution)/shard_map/ppermute | solution.py:226
  37.8 2.9 %collective-permute-start.4 = (s16[1,544,128]{2,1,0:T(8,128)(2,1)S(1)}, s16[1,544,128]{2,1,0:T(8,128)(2,1)S(1)}, u32[]{:S(2)}, u32[]{:S(2)}) collective-permute-start(s16[1,544,128]{2,1,0:T(8,128)(2,1)S(1)} %copy-done.6), channel_id=1, source_target_pairs={{0,20},{4,16},{8,28},{12,24},{16,4},{20,0},{24,12},{28,8},{1,21},{... | collective-permute-start | bytes 417800 | tf_op jit(solution)/shard_map/ppermute | solution.py:226
  40.7 2.1 %collective-permute-start.5 = (s16[1,544,128]{2,1,0:T(8,128)(2,1)S(1)}, s16[1,544,128]{2,1,0:T(8,128)(2,1)S(1)}, u32[]{:S(2)}, u32[]{:S(2)}) collective-permute-start(s16[1,544,128]{2,1,0:T(8,128)(2,1)S(1)} %copy-done.5), channel_id=1, source_target_pairs={{0,24},{4,28},{8,16},{12,20},{16,8},{20,12},{24,0},{28,4},{1,25},{... | collective-permute-start | bytes 417800 | tf_op jit(solution)/shard_map/ppermute | solution.py:226
  44.8 7.3 %product.2 = (s16[1,528,128]{2,1,0:T(8,128)(2,1)S(1)}, s16[1,528,128]{2,1,0:T(8,128)(2,1)S(1)}, s16[1,528,128]{2,1,0:T(8,128)(2,1)S(1)}, s16[1,528,128]{2,1,0:T(...) custom-call(s32[2]{0:T(128)S(1)} %copy-done.1, ...), custom_call_target="tpu_custom_call" | custom-call | flops 3221225472 | bytes 10485760 | tf_op jit(solution)/shard_map/product/pallas_call | solution.py:299
  53.3 3.5 %collective-permute-start.19 = (s16[1,528,128]{2,1,0:T(8,128)(2,1)S(1)}, s16[1,528,128]{2,1,0:T(8,128)(2,1)S(1)}, u32[]{:S(2)}, u32[]{:S(2)}) collective-permute-start(s16[1,528,128]{2,1,0:T(8,128)(2,1)S(1)} %get-tuple-element.62), channel_id=1, source_target_pairs={{0,20},{4,16},{8,28},{12,24},{16,4},{20,0},{24,12},{28,8},{1,21},{... | collective-permute-start | bytes 405512 | tf_op jit(solution)/shard_map/ppermute | solution.py:226
  56.8 3.7 %collective-permute-done.4.refs_5_ = s16[1,544,128]{2,1,0:T(8,128)(2,1)S(1)} collective-permute-done((s16[1,544,128]{2,1,0:T(8,128)(2,1)S(1)}, s16[1,544,128]{2,1,0:T(8,128)(2,1)S(1)}, u32[]{:S(2)}, u32[]{:S(2)}) %collective-permute-start.4) | collective-permute-done | bytes 139296 | tf_op jit(solution)/shard_map/ppermute | solution.py:226
  60.5 3.7 %collective-permute-done.5.refs_6_ = s16[1,544,128]{2,1,0:T(8,128)(2,1)S(1)} collective-permute-done((s16[1,544,128]{2,1,0:T(8,128)(2,1)S(1)}, s16[1,544,128]{2,1,0:T(8,128)(2,1)S(1)}, u32[]{:S(2)}, u32[]{:S(2)}) %collective-permute-start.5) | collective-permute-done | bytes 139296 | tf_op jit(solution)/shard_map/ppermute | solution.py:226
  64.2 4.2 %collective-permute-done.6.refs_7_ = s16[1,544,128]{2,1,0:T(8,128)(2,1)S(1)} collective-permute-done((s16[1,544,128]{2,1,0:T(8,128)(2,1)S(1)}, s16[1,544,128]{2,1,0:T(8,128)(2,1)S(1)}, u32[]{:S(2)}, u32[]{:S(2)}) %collective-permute-start.6) | collective-permute-done | bytes 139296 | tf_op jit(solution)/shard_map/ppermute | solution.py:226
  68.4 7.3 %product.3 = (s16[2,528,128]{2,1,0:T(8,128)(2,1)S(1)}, s16[2,528,128]{2,1,0:T(8,128)(2,1)S(1)}, s16[2,528,128]{2,1,0:T(8,128)(2,1)S(1)}, s16[2,528,128]{2,1,0:T(...) custom-call(s32[2]{0:T(128)S(1)} %copy-done.1, ...), custom_call_target="tpu_custom_call" | custom-call | flops 3221225472 | bytes 10485760 | tf_op jit(solution)/shard_map/product/pallas_call | solution.py:299
  79.3 3.5 %collective-permute-start.17 = (s16[2,528,128]{2,1,0:T(8,128)(2,1)S(1)}, s16[2,528,128]{2,1,0:T(8,128)(2,1)S(1)}, u32[]{:S(2)}, u32[]{:S(2)}) collective-permute-start(s16[2,528,128]{2,1,0:T(8,128)(2,1)S(1)} %get-tuple-element.60), channel_id=1, source_target_pairs={{0,12},{4,8},{8,4},{12,0},{16,28},{20,24},{24,20},{28,16},{1,13},{... | collective-permute-start | bytes 811016 | tf_op jit(solution)/shard_map/ppermute | solution.py:226
  83.0 7.7 %collective-permute-start.11 = (s16[1,528,128]{2,1,0:T(8,128)(2,1)S(1)}, s16[1,528,128]{2,1,0:T(8,128)(2,1)S(1)}, u32[]{:S(2)}, u32[]{:S(2)}) collective-permute-start(s16[1,528,128]{2,1,0:T(8,128)(2,1)S(1)} %get-tuple-element.53), channel_id=1, source_target_pairs={{0,16},{4,20},{8,24},{12,28},{16,0},{20,4},{24,8},{28,12},{1,17},{... | collective-permute-start | bytes 405512 | tf_op jit(solution)/shard_map/ppermute | solution.py:226
  90.8 3.7 %collective-permute-start.12 = (s16[1,528,128]{2,1,0:T(8,128)(2,1)S(1)}, s16[1,528,128]{2,1,0:T(8,128)(2,1)S(1)}, u32[]{:S(2)}, u32[]{:S(2)}) collective-permute-start(s16[1,528,128]{2,1,0:T(8,128)(2,1)S(1)} %get-tuple-element.54), channel_id=1, source_target_pairs={{0,20},{4,16},{8,28},{12,24},{16,4},{20,0},{24,12},{28,8},{1,21},{... | collective-permute-start | bytes 405512 | tf_op jit(solution)/shard_map/ppermute | solution.py:226
  97.8 2.1 %result.3.refs_4_ = f32[2,64,8192]{2,1,0:T(8,128)} custom-call(s32[2]{0:T(128)S(1)} %copy-done.1, s16[1,528,128]{2,1,0:T(8,128)(2,1)S(1)} %collective-permute-done.18.refs_0_, s16[1,528,128]{2,1,0:T(8,128)(2,1)S(1)} %collective-permute-done.19.refs_1_, s16[1,528,128]{2,1,0:T(8,128)(2,1)S(1)} %collective-permute-done.20.refs_2_, ...), custom_call_target="tpu_custom_call" | custom-call | flops 1048576 | bytes 3145728 | tf_op jit(solution)/shard_map/result/pallas_call | solution.py:336
  99.9 2.5 %result.4.refs_4_ = f32[2,64,8192]{2,1,0:T(8,128)} custom-call(s32[2]{0:T(128)S(1)} %copy-done.1, s16[2,528,128]{2,1,0:T(8,128)(2,1)S(1)} %get-tuple-element.57.refs_0_, s16[2,528,128]{2,1,0:T(8,128)(2,1)S(1)} %collective-permute-done.15.refs_1_, s16[2,528,128]{2,1,0:T(8,128)(2,1)S(1)} %collective-permute-done.16.refs_2_, ...), custom_call_target="tpu_custom_call", output_to_operand_aliasing={{}: (5, {})} | custom-call | flops 1048576 | bytes 3145728 | tf_op jit(solution)/shard_map/result/pallas_call | solution.py:336
  102.4 6.7 %collective-permute-done.12.refs_1_ = s16[1,528,128]{2,1,0:T(8,128)(2,1)S(1)} collective-permute-done((s16[1,528,128]{2,1,0:T(8,128)(2,1)S(1)}, s16[1,528,128]{2,1,0:T(8,128)(2,1)S(1)}, u32[]{:S(2)}, u32[]{:S(2)}) %collective-permute-start.12) | collective-permute-done | bytes 135200 | tf_op jit(solution)/shard_map/ppermute | solution.py:226
  109.1 3.5 %collective-permute-done.13.refs_2_ = s16[1,528,128]{2,1,0:T(8,128)(2,1)S(1)} collective-permute-done((s16[1,528,128]{2,1,0:T(8,128)(2,1)S(1)}, s16[1,528,128]{2,1,0:T(8,128)(2,1)S(1)}, u32[]{:S(2)}, u32[]{:S(2)}) %collective-permute-start.13) | collective-permute-done | bytes 135200 | tf_op jit(solution)/shard_map/ppermute | solution.py:226
  112.7 3.4 %collective-permute-done.14.refs_3_ = s16[1,528,128]{2,1,0:T(8,128)(2,1)S(1)} collective-permute-done((s16[1,528,128]{2,1,0:T(8,128)(2,1)S(1)}, s16[1,528,128]{2,1,0:T(8,128)(2,1)S(1)}, u32[]{:S(2)}, u32[]{:S(2)}) %collective-permute-start.14) | collective-permute-done | bytes 135200 | tf_op jit(solution)/shard_map/ppermute | solution.py:226
  116.1 2.1 %result.5 = f32[2,64,8192]{2,1,0:T(8,128)} custom-call(s32[2]{0:T(128)S(1)} %copy-done.1, s16[1,528,128]{2,1,0:T(8,128)(2,1)S(1)} %collective-permute-done.11.refs_0_, s16[1,528,128]{2,1,0:T(8,128)(2,1)S(1)} %collective-permute-done.12.refs_1_, s16[1,528,128]{2,1,0:T(8,128)(2,1)S(1)} %collective-permute-done.13.refs_2_, ...), custom_call_target="tpu_custom_call", output_to_operand_aliasing={{}: (5, {})} | custom-call | flops 1048576 | bytes 3145728 | tf_op jit(solution)/shard_map/result/pallas_call | solution.py:336
  (50 shorter events, 16.8 us)
Async XLA Ops:
  5.7 12.9 %collective-permute-start.7 = (s16[1,544,128]{2,1,0:T(8,128)(2,1)}, s16[1,544,128]{2,1,0:T(8,128)(2,1)S(1)}, u32[]{:S(2)}, u32[]{:S(2)}) collective-permute-start(s16[1,544,128]{2,1,0:T(8,128)(2,1)} %get-tuple-element.45), channel_id=1, source_target_pairs={{0,16},{4,20},{8,24},{12,28},{16,0},{20,4},{24,8},{28,12},{1,17},{... | collective-permute-start | bytes 417800 | tf_op jit(solution)/shard_map/ppermute | solution.py:226
  8.4 12.3 %collective-permute-start.8 = (s16[1,544,128]{2,1,0:T(8,128)(2,1)}, s16[1,544,128]{2,1,0:T(8,128)(2,1)S(1)}, u32[]{:S(2)}, u32[]{:S(2)}) collective-permute-start(s16[1,544,128]{2,1,0:T(8,128)(2,1)} %get-tuple-element.46), channel_id=1, source_target_pairs={{0,20},{4,16},{8,28},{12,24},{16,4},{20,0},{24,12},{28,8},{1,21},{... | collective-permute-start | bytes 417800 | tf_op jit(solution)/shard_map/ppermute | solution.py:226
  15.1 25.6 %collective-permute-start = (s16[2,544,128]{2,1,0:T(8,128)(2,1)}, s16[2,544,128]{2,1,0:T(8,128)(2,1)S(1)}, u32[]{:S(2)}, u32[]{:S(2)}) collective-permute-start(s16[2,544,128]{2,1,0:T(8,128)(2,1)} %get-tuple-element.36), channel_id=1, source_target_pairs={{0,4},{4,0},{8,12},{12,8},{16,20},{20,16},{24,28},{28,24},{1,5},{5... | collective-permute-start | bytes 835592 | tf_op jit(solution)/shard_map/ppermute | solution.py:226
  15.6 27.2 %collective-permute-start.1 = (s16[2,544,128]{2,1,0:T(8,128)(2,1)}, s16[2,544,128]{2,1,0:T(8,128)(2,1)S(1)}, u32[]{:S(2)}, u32[]{:S(2)}) collective-permute-start(s16[2,544,128]{2,1,0:T(8,128)(2,1)} %get-tuple-element.37), channel_id=1, source_target_pairs={{0,8},{4,12},{8,0},{12,4},{16,24},{20,28},{24,16},{28,20},{1,9},{5... | collective-permute-start | bytes 835592 | tf_op jit(solution)/shard_map/ppermute | solution.py:226
  15.8 29.0 %collective-permute-start.2 = (s16[2,544,128]{2,1,0:T(8,128)(2,1)}, s16[2,544,128]{2,1,0:T(8,128)(2,1)S(1)}, u32[]{:S(2)}, u32[]{:S(2)}) collective-permute-start(s16[2,544,128]{2,1,0:T(8,128)(2,1)} %get-tuple-element.38), channel_id=1, source_target_pairs={{0,12},{4,8},{8,4},{12,0},{16,28},{20,24},{24,20},{28,16},{1,13},{... | collective-permute-start | bytes 835592 | tf_op jit(solution)/shard_map/ppermute | solution.py:226
  18.6 11.9 %collective-permute-start.9 = (s16[1,544,128]{2,1,0:T(8,128)(2,1)S(1)}, s16[1,544,128]{2,1,0:T(8,128)(2,1)S(1)}, u32[]{:S(2)}, u32[]{:S(2)}) collective-permute-start(s16[1,544,128]{2,1,0:T(8,128)(2,1)S(1)} %copy-done.9), channel_id=1, source_target_pairs={{0,24},{4,28},{8,16},{12,20},{16,8},{20,12},{24,0},{28,4},{1,25},{... | collective-permute-start | bytes 417800 | tf_op jit(solution)/shard_map/ppermute | solution.py:226
  20.7 17.1 %collective-permute-start.10 = (s16[1,544,128]{2,1,0:T(8,128)(2,1)S(1)}, s16[1,544,128]{2,1,0:T(8,128)(2,1)S(1)}, u32[]{:S(2)}, u32[]{:S(2)}) collective-permute-start(s16[1,544,128]{2,1,0:T(8,128)(2,1)S(1)} %copy-done.8), channel_id=1, source_target_pairs={{0,28},{4,24},{8,20},{12,16},{16,12},{20,8},{24,4},{28,0},{1,29},{... | collective-permute-start | bytes 417800 | tf_op jit(solution)/shard_map/ppermute | solution.py:226
  29.0 15.8 %copy-start.1 = (s32[2]{0:T(128)S(1)}, s32[2]{0:T(128)}, u32[]{:S(2)}) copy-start(s32[2]{0:T(128)} %pad_add_fusion.where) | copy-start | bytes 28
  29.0 15.8 %copy-start.2 = (s16[2,544,128]{2,1,0:T(8,128)(2,1)S(1)}, s16[2,544,128]{2,1,0:T(8,128)(2,1)}, u32[]{:S(2)}) copy-start(s16[2,544,128]{2,1,0:T(8,128)(2,1)} %get-tuple-element.35.refs_0_) | copy-start | bytes 835588
  30.5 22.8 %collective-permute-start.3 = (s16[1,544,128]{2,1,0:T(8,128)(2,1)S(1)}, s16[1,544,128]{2,1,0:T(8,128)(2,1)S(1)}, u32[]{:S(2)}, u32[]{:S(2)}) collective-permute-start(s16[1,544,128]{2,1,0:T(8,128)(2,1)S(1)} %copy-done.7), channel_id=1, source_target_pairs={{0,16},{4,20},{8,24},{12,28},{16,0},{20,4},{24,8},{28,12},{1,17},{... | collective-permute-start | bytes 417800 | tf_op jit(solution)/shard_map/ppermute | solution.py:226
  37.8 22.7 %collective-permute-start.4 = (s16[1,544,128]{2,1,0:T(8,128)(2,1)S(1)}, s16[1,544,128]{2,1,0:T(8,128)(2,1)S(1)}, u32[]{:S(2)}, u32[]{:S(2)}) collective-permute-start(s16[1,544,128]{2,1,0:T(8,128)(2,1)S(1)} %copy-done.6), channel_id=1, source_target_pairs={{0,20},{4,16},{8,28},{12,24},{16,4},{20,0},{24,12},{28,8},{1,21},{... | collective-permute-start | bytes 417800 | tf_op jit(solution)/shard_map/ppermute | solution.py:226
  40.7 23.5 %collective-permute-start.5 = (s16[1,544,128]{2,1,0:T(8,128)(2,1)S(1)}, s16[1,544,128]{2,1,0:T(8,128)(2,1)S(1)}, u32[]{:S(2)}, u32[]{:S(2)}) collective-permute-start(s16[1,544,128]{2,1,0:T(8,128)(2,1)S(1)} %copy-done.5), channel_id=1, source_target_pairs={{0,24},{4,28},{8,16},{12,20},{16,8},{20,12},{24,0},{28,4},{1,25},{... | collective-permute-start | bytes 417800 | tf_op jit(solution)/shard_map/ppermute | solution.py:226
  42.8 25.7 %collective-permute-start.6 = (s16[1,544,128]{2,1,0:T(8,128)(2,1)S(1)}, s16[1,544,128]{2,1,0:T(8,128)(2,1)S(1)}, u32[]{:S(2)}, u32[]{:S(2)}) collective-permute-start(s16[1,544,128]{2,1,0:T(8,128)(2,1)S(1)} %copy-done.4), channel_id=1, source_target_pairs={{0,28},{4,24},{8,20},{12,16},{16,12},{20,8},{24,4},{28,0},{1,29},{... | collective-permute-start | bytes 417800 | tf_op jit(solution)/shard_map/ppermute | solution.py:226
  52.1 25.8 %collective-permute-start.18 = (s16[1,528,128]{2,1,0:T(8,128)(2,1)S(1)}, s16[1,528,128]{2,1,0:T(8,128)(2,1)S(1)}, u32[]{:S(2)}, u32[]{:S(2)}) collective-permute-start(s16[1,528,128]{2,1,0:T(8,128)(2,1)S(1)} %get-tuple-element.61), channel_id=1, source_target_pairs={{0,16},{4,20},{8,24},{12,28},{16,0},{20,4},{24,8},{28,12},{1,17},{... | collective-permute-start | bytes 405512 | tf_op jit(solution)/shard_map/ppermute | solution.py:226
  53.3 26.1 %collective-permute-start.19 = (s16[1,528,128]{2,1,0:T(8,128)(2,1)S(1)}, s16[1,528,128]{2,1,0:T(8,128)(2,1)S(1)}, u32[]{:S(2)}, u32[]{:S(2)}) collective-permute-start(s16[1,528,128]{2,1,0:T(8,128)(2,1)S(1)} %get-tuple-element.62), channel_id=1, source_target_pairs={{0,20},{4,16},{8,28},{12,24},{16,4},{20,0},{24,12},{28,8},{1,21},{... | collective-permute-start | bytes 405512 | tf_op jit(solution)/shard_map/ppermute | solution.py:226
  75.8 18.7 %collective-permute-start.15 = (s16[2,528,128]{2,1,0:T(8,128)(2,1)S(1)}, s16[2,528,128]{2,1,0:T(8,128)(2,1)S(1)}, u32[]{:S(2)}, u32[]{:S(2)}) collective-permute-start(s16[2,528,128]{2,1,0:T(8,128)(2,1)S(1)} %get-tuple-element.58), channel_id=1, source_target_pairs={{0,4},{4,0},{8,12},{12,8},{16,20},{20,16},{24,28},{28,24},{1,5},{5... | collective-permute-start | bytes 811016 | tf_op jit(solution)/shard_map/ppermute | solution.py:226
  76.0 20.4 %collective-permute-start.16 = (s16[2,528,128]{2,1,0:T(8,128)(2,1)S(1)}, s16[2,528,128]{2,1,0:T(8,128)(2,1)S(1)}, u32[]{:S(2)}, u32[]{:S(2)}) collective-permute-start(s16[2,528,128]{2,1,0:T(8,128)(2,1)S(1)} %get-tuple-element.59), channel_id=1, source_target_pairs={{0,8},{4,12},{8,0},{12,4},{16,24},{20,28},{24,16},{28,20},{1,9},{5... | collective-permute-start | bytes 811016 | tf_op jit(solution)/shard_map/ppermute | solution.py:226
  76.0 7.0 %collective-permute-start.20 = (s16[1,528,128]{2,1,0:T(8,128)(2,1)S(1)}, s16[1,528,128]{2,1,0:T(8,128)(2,1)S(1)}, u32[]{:S(2)}, u32[]{:S(2)}) collective-permute-start(s16[1,528,128]{2,1,0:T(8,128)(2,1)S(1)} %get-tuple-element.63), channel_id=1, source_target_pairs={{0,24},{4,28},{8,16},{12,20},{16,8},{20,12},{24,0},{28,4},{1,25},{... | collective-permute-start | bytes 405512 | tf_op jit(solution)/shard_map/ppermute | solution.py:226
  77.9 12.9 %collective-permute-start.21 = (s16[1,528,128]{2,1,0:T(8,128)(2,1)S(1)}, s16[1,528,128]{2,1,0:T(8,128)(2,1)S(1)}, u32[]{:S(2)}, u32[]{:S(2)}) collective-permute-start(s16[1,528,128]{2,1,0:T(8,128)(2,1)S(1)} %get-tuple-element.64), channel_id=1, source_target_pairs={{0,28},{4,24},{8,20},{12,16},{16,12},{20,8},{24,4},{28,0},{1,29},{... | collective-permute-start | bytes 405512 | tf_op jit(solution)/shard_map/ppermute | solution.py:226
  79.3 20.6 %collective-permute-start.17 = (s16[2,528,128]{2,1,0:T(8,128)(2,1)S(1)}, s16[2,528,128]{2,1,0:T(8,128)(2,1)S(1)}, u32[]{:S(2)}, u32[]{:S(2)}) collective-permute-start(s16[2,528,128]{2,1,0:T(8,128)(2,1)S(1)} %get-tuple-element.60), channel_id=1, source_target_pairs={{0,12},{4,8},{8,4},{12,0},{16,28},{20,24},{24,20},{28,16},{1,13},{... | collective-permute-start | bytes 811016 | tf_op jit(solution)/shard_map/ppermute | solution.py:226
  83.0 19.4 %collective-permute-start.11 = (s16[1,528,128]{2,1,0:T(8,128)(2,1)S(1)}, s16[1,528,128]{2,1,0:T(8,128)(2,1)S(1)}, u32[]{:S(2)}, u32[]{:S(2)}) collective-permute-start(s16[1,528,128]{2,1,0:T(8,128)(2,1)S(1)} %get-tuple-element.53), channel_id=1, source_target_pairs={{0,16},{4,20},{8,24},{12,28},{16,0},{20,4},{24,8},{28,12},{1,17},{... | collective-permute-start | bytes 405512 | tf_op jit(solution)/shard_map/ppermute | solution.py:226
  90.8 18.4 %collective-permute-start.12 = (s16[1,528,128]{2,1,0:T(8,128)(2,1)S(1)}, s16[1,528,128]{2,1,0:T(8,128)(2,1)S(1)}, u32[]{:S(2)}, u32[]{:S(2)}) collective-permute-start(s16[1,528,128]{2,1,0:T(8,128)(2,1)S(1)} %get-tuple-element.54), channel_id=1, source_target_pairs={{0,20},{4,16},{8,28},{12,24},{16,4},{20,0},{24,12},{28,8},{1,21},{... | collective-permute-start | bytes 405512 | tf_op jit(solution)/shard_map/ppermute | solution.py:226
  94.5 18.2 %collective-permute-start.13 = (s16[1,528,128]{2,1,0:T(8,128)(2,1)S(1)}, s16[1,528,128]{2,1,0:T(8,128)(2,1)S(1)}, u32[]{:S(2)}, u32[]{:S(2)}) collective-permute-start(s16[1,528,128]{2,1,0:T(8,128)(2,1)S(1)} %get-tuple-element.55), channel_id=1, source_target_pairs={{0,24},{4,28},{8,16},{12,20},{16,8},{20,12},{24,0},{28,4},{1,25},{... | collective-permute-start | bytes 405512 | tf_op jit(solution)/shard_map/ppermute | solution.py:226
  96.4 19.7 %collective-permute-start.14 = (s16[1,528,128]{2,1,0:T(8,128)(2,1)S(1)}, s16[1,528,128]{2,1,0:T(8,128)(2,1)S(1)}, u32[]{:S(2)}, u32[]{:S(2)}) collective-permute-start(s16[1,528,128]{2,1,0:T(8,128)(2,1)S(1)} %get-tuple-element.56), channel_id=1, source_target_pairs={{0,28},{4,24},{8,20},{12,16},{16,12},{20,8},{24,4},{28,0},{1,29},{... | collective-permute-start | bytes 405512 | tf_op jit(solution)/shard_map/ppermute | solution.py:226
  (8 other events, 82.8 us)

commit v3 on v1

v3 whole, which is shorter than its diff:
```python
import functools
import math

import jax
import jax.numpy as jnp
import numpy as np
from jax import lax
from jax.experimental import pallas as pl
from jax.experimental.pallas import tpu as pltpu
from jax.sharding import PartitionSpec as P

inner_radius = 0.35
outer_radius = 1.0
blend_weight = 0.5

LANES = 128
TILE = 16
EXTRA = 8
SHARES = ((0, 4), (4, 4))
TOP = 32700.0
EDGE_TOP = 16384.0
FINE = 128.0
MIB = 1024 * 1024


def radius_at(level_index, total_levels):
    scaled = level_index / (total_levels - 1.0)
    stretch = (1.0 - blend_weight) * scaled + blend_weight * (1.0 - np.cos(math.pi * scaled)) / 2.0
    return inner_radius + (outer_radius - inner_radius) * stretch


def stencil_table(total_levels):
    k = np.arange(total_levels, dtype=np.float64)
    radius = radius_at(k, total_levels)
    below = radius - radius_at(k - 1.0, total_levels)
    above = radius_at(k + 1.0, total_levels) - radius
    at_inner, at_outer = k == 0, k == total_levels - 1
    weight_below = np.where(at_inner, 0.0, np.where(at_outer, -1.0 / below, -above / (below * (below + above))))
    weight_here = np.where(
        at_inner, -1.0 / above, np.where(at_outer, 1.0 / below, (above - below) / (below * above))
    )
    weight_above = np.where(at_inner, 1.0 / above, np.where(at_outer, 0.0, below / (above * (below + above))))
    time_step = 0.5 * (outer_radius - inner_radius) / (total_levels - 1.0)
    table = np.zeros((total_levels, LANES), np.float32)
    table[:, 0] = time_step * weight_below
    table[:, 1] = time_step * (weight_here + 2.0 / radius)
    table[:, 2] = time_step * weight_above
    return table


def scale_code(largest, per_octave):
    return jnp.ceil(jnp.log2(jnp.maximum(largest, 1e-30)) * per_octave) * (FINE / per_octave)


def encode_factor(code, top):
    return jnp.exp2(code * (-1.0 / FINE)) * top


def to_int16(values):
    return values.astype(jnp.int32).astype(jnp.int16)


def to_float(codes):
    return codes.astype(jnp.int32).astype(jnp.float32)


def scale_of(codes, top):
    return jnp.exp2(codes * (1.0 / FINE)) * (1.0 / top)


def lanes_of(slab):
    return pl.ds(pl.multiple_of(slab * LANES, LANES), LANES)


def right_side_kernel(slabs, partners, where, n_ref, s_ref, tab_ref, *refs):
    outs, (buffer, values, tops, extra) = refs[-4 - partners : -4], refs[-4:]
    levels = n_ref.shape[1]
    rows = 2 * levels
    tab = tab_ref[...]
    below, here, above = (jnp.broadcast_to(tab[:, i : i + 1], (levels, LANES)) for i in range(3))
    row = lax.broadcasted_iota(jnp.int32, (levels, LANES), 0)

    def rows_of(slab):
        return pl.ds(pl.multiple_of(slab * rows, rows), rows)

    def compute(slab, _):
        ends, top = [], jnp.zeros((8, LANES), jnp.float32)
        for f in range(2):
            n = n_ref[f, :, lanes_of(slab)].astype(jnp.float32)
            prev = jnp.where(row == 0, n, pltpu.roll(n, 1, 0))
            succ = jnp.where(row == levels - 1, n, pltpu.roll(n, levels - 1, 0))
            v = s_ref[f, :, lanes_of(slab)] + (below * prev + here * n + above * succ)
            values[pl.ds(pl.multiple_of(slab * rows + f * levels, levels), levels), :] = v
            top = jnp.maximum(top, jnp.max(jnp.abs(v).reshape(levels // 8, 8, LANES), axis=0))
            ends += [n[:1], n[levels - 1 :]]
        tops[slab] = top
        extra[slab] = jnp.concatenate(ends + [jnp.zeros((4, LANES), jnp.float32)], axis=0)
        return 0

    lax.fori_loop(0, slabs, compute, 0, unroll=2)
    ends = extra[...]
    code = scale_code(jnp.max(tops[...], axis=1), FINE)
    factor = encode_factor(code, TOP)
    edge_code = scale_code(jnp.max(jnp.abs(ends), axis=1), 1.0)
    edge_factor = encode_factor(edge_code, EDGE_TOP)
    at_row = lax.broadcasted_iota(jnp.int32, ends.shape, 1)
    ends = jnp.round(ends * edge_factor[:, None, :])
    ends = jnp.where(at_row == 4, edge_code[:, None, :], jnp.where(at_row == 5, code[:, None, :], ends))
    buffer[slabs * rows :, :] = to_int16(ends.reshape(slabs * EXTRA, LANES))
    tops[:, 0, :] = factor

    def code_slab(slab, _):
        buffer[rows_of(slab), :] = to_int16(jnp.round(values[rows_of(slab), :] * tops[slab, 0:1, :]))
        return 0

    lax.fori_loop(0, slabs, code_slab, 0, unroll=2)
    step = pl.program_id(0)
    for at, out in enumerate(outs):

        @pl.when(step == at)
        def _():
            out[...] = buffer[...]


def split_kernel(a_ref, hi_ref, lo_ref):
    a = a_ref[...]
    hi = a.astype(jnp.bfloat16)
    hi_ref[...] = hi
    lo_ref[...] = (a - hi.astype(jnp.float32)).astype(jnp.bfloat16)


def swapped(edges):
    return jnp.concatenate([edges[1:2], edges[0:1], edges[3:4], edges[2:3]], axis=0)


def product_kernel(order, held, first_slab, slabs, lower_slabs, half_cols, where, edge_weight, *refs):
    groups = len(order)
    ins, (hi_ref, lo_ref) = refs[:groups], refs[groups : groups + 2]
    outs, (v_hi, v_lo, y, edges, codes, all_codes) = refs[-6 - groups : -6], refs[-6:]
    size = y.shape[0]
    levels = size // (2 * groups)
    rows = 2 * levels
    me = where[0]
    pair = where[1]
    peers = [lax.bitwise_xor(me, k) for k in order]
    near = lax.broadcasted_iota(jnp.int32, (8, LANES), 0)

    def place(f, peer):
        return pl.ds(pl.multiple_of(f * (size // 2) + peer * levels, levels), levels)

    def one_tile(t, _):
        extras = []
        for ref, peer, (all_slabs, skipped) in zip(ins, peers, held):
            at = all_slabs * rows + (skipped + t * 2) * EXTRA
            two = to_float(ref[pl.ds(pl.multiple_of(at, TILE), TILE), :])
            power = jnp.exp2(two * (1.0 / FINE))
            extras.append(power)
            for j in range(2):
                at = j * EXTRA
                edges[peer, :, j * LANES : (j + 1) * LANES] = two[at : at + 4] * (
                    power[at + 4 : at + 5] * (1.0 / EDGE_TOP)
                )
        for ref, peer, power, (_, skipped) in zip(ins, peers, extras, held):
            before, after = jnp.maximum(peer - 1, 0), jnp.minimum(peer + 1, groups - 1)
            weight_before, weight_after = edge_weight[peer], edge_weight[groups + peer]
            for j in range(2):
                cols = slice(j * LANES, (j + 1) * LANES)
                scale = power[j * EXTRA + 5 : j * EXTRA + 6] * (1.0 / TOP)
                here = swapped(edges[peer, :, cols])
                low = weight_before * (edges[before, :, cols] - here)
                high = weight_after * (edges[after, :, cols] - here)
                start = (skipped + t * 2 + j) * rows
                for f in range(2):
                    v = to_float(ref[pl.ds(pl.multiple_of(start + f * levels, TILE), levels), :]) * scale
                    first = v[:8] + jnp.where(near == 0, low[2 * f + 1 : 2 * f + 2], 0.0)
                    last = v[levels - 8 :] + jnp.where(near == 7, high[2 * f : 2 * f + 1], 0.0)
                    middle = [v[8 : levels - 8]] if levels > 16 else []
                    v = jnp.concatenate([first] + middle + [last], axis=0)
                    hi = v.astype(jnp.bfloat16)
                    v_hi[place(f, peer), cols] = hi
                    v_lo[place(f, peer), cols] = (v - hi.astype(jnp.float32)).astype(jnp.bfloat16)

        def product(which, cols):
            dot = functools.partial(jnp.dot, preferred_element_type=jnp.float32)
            return (
                dot(lo_ref[which], v_hi[:, cols])
                + dot(hi_ref[which], v_lo[:, cols])
                + dot(hi_ref[which], v_hi[:, cols])
            )

        y[...] = product(1, slice(0, 2 * LANES))
        for tile in range(slabs // 2):
            for j in range(2):
                first_col = (first_slab + tile * 2 + j) * LANES
                if first_col % half_cols < lower_slabs * LANES:

                    @pl.when(t == tile)
                    def _():
                        cols = slice(j * LANES, (j + 1) * LANES)
                        column = first_col % half_cols + lax.broadcasted_iota(jnp.int32, (size, LANES), 1)
                        bound = pair + 1 if first_col < half_cols else pair
                        y[:, cols] = jnp.where(column < bound, product(0, cols), y[:, cols])

        def results(peer, j):
            return jnp.concatenate([y[place(f, peer), j * LANES : (j + 1) * LANES] for f in range(2)], axis=0)

        for i, peer in enumerate(peers):
            for j in range(2):
                v = jnp.abs(results(peer, j))
                codes[j, i] = jnp.max(v.reshape(rows // 8, 8, LANES), axis=0)
        code = scale_code(jnp.max(codes[...], axis=2), FINE)
        factor = encode_factor(code, TOP)
        for i, (out, peer) in enumerate(zip(outs, peers)):
            for j in range(2):
                start = (t * 2 + j) * rows
                out[pl.ds(pl.multiple_of(start, TILE), rows), :] = to_int16(
                    jnp.round(results(peer, j) * factor[j, i : i + 1])
                )
                all_codes[i, pl.ds(t * 2 + j, 1), :] = code[j, i : i + 1]
        return 0

    all_codes[...] = jnp.zeros_like(all_codes)
    lax.fori_loop(0, slabs // 2, one_tile, 0)
    for i, out in enumerate(outs):
        out[slabs * rows :, :] = to_int16(all_codes[i])


def result_kernel(count, slabs, where, *refs):
    ins, out_ref, buffer = refs[:count], refs[-2], refs[-1]
    levels = out_ref.shape[1]
    rows = 2 * levels
    step = pl.program_id(0)
    for at in range(count):

        @pl.when(step == at)
        def _():
            buffer[...] = ins[at][...]

    scales = scale_of(to_float(buffer[slabs * rows :, :]), TOP)
    for slab in range(slabs):
        for f in range(2):
            start = slab * rows + f * levels
            v = to_float(buffer[start : start + levels, :])
            out_ref[f, :, slab * LANES : (slab + 1) * LANES] = v * scales[slab : slab + 1, :]


def send(message, k, groups):
    return message if k == 0 else lax.ppermute(message, "rad", [(i, i ^ k) for i in range(groups)])


def columns_of(ks, width, first):
    def at(step, w):
        k = jnp.int32(ks[-1])
        for i, value in enumerate(ks[:-1]):
            k = jnp.where(step == i, value, k)
        return (0, 0, pl.multiple_of(lax.bitwise_xor(w[0], k) * width + first, LANES))

    return at


def columns_block(levels, count, index_map):
    return pl.BlockSpec((pl.Element(2), pl.Element(levels), pl.Element(count)), index_map)


def local(slots, nonlin, state, inverse, pair_of_slot):
    levels = nonlin.shape[1]
    groups = lax.axis_size("rad")
    width = nonlin.shape[2] // groups
    size = inverse.shape[-1]
    all_slabs = width // LANES
    shares = [(first * all_slabs // 8, count * all_slabs // 8) for first, count in SHARES]
    rows = 2 * levels
    lower_slabs = -(-slots // LANES)
    me = lax.axis_index("rad").astype(jnp.int32)
    where = jnp.stack([me, pair_of_slot[0].astype(jnp.int32)])
    weights = stencil_table(levels * groups)
    table = jnp.asarray(weights)
    edge_weight = jnp.asarray(np.concatenate([weights[::levels, 0], weights[levels - 1 :: levels, 2]]))
    vmem = pl.BlockSpec(memory_space=pltpu.VMEM)
    hbm = pl.BlockSpec(memory_space=pl.ANY)
    far = list(range(groups // 2, groups))
    near = list(range(groups // 2))
    others = near[1:]
    order = []
    for i, k in enumerate(far):
        order += [k] + others[2 * i : 2 * i + 2]
    order += near[:1]

    def call(kernel, name, flops, moved, vmem_mib, **kwargs):
        return pl.pallas_call(
            kernel,
            name=name,
            compiler_params=pltpu.CompilerParams(vmem_limit_bytes=vmem_mib * MIB),
            cost_estimate=pl.CostEstimate(flops=flops, bytes_accessed=moved, transcendentals=0),
            **kwargs,
        )

    def right_side(ks, cut, *earlier):
        first, held = cut
        block = columns_block(levels, held * LANES, columns_of(ks, width, first * LANES))
        out_rows = held * (rows + EXTRA)
        return call(
            functools.partial(right_side_kernel, held, len(ks)),
            "right_side",
            MIB * len(ks),
            MIB * len(ks),
            56,
            out_shape=[jax.ShapeDtypeStruct((out_rows, LANES), jnp.int16)] * len(ks),
            grid_spec=pltpu.PrefetchScalarGridSpec(
                num_scalar_prefetch=1,
                grid=(len(ks),),
                in_specs=[block, block, pl.BlockSpec((levels, LANES), lambda k, w: (w[0], 0)), *[hbm for _ in earlier]],
                out_specs=[pl.BlockSpec((out_rows, LANES), lambda k, w: (0, 0))] * len(ks),
                scratch_shapes=[
                    pltpu.VMEM((out_rows, LANES), jnp.int16),
                    pltpu.VMEM((held * rows, LANES), jnp.float32),
                    pltpu.VMEM((held, 8, LANES), jnp.float32),
                    pltpu.VMEM((held, EXTRA, LANES), jnp.float32),
                ],
            ),
        )(where, nonlin, state, table, *earlier)

    def split():
        block = pl.BlockSpec((1, size // 4, size), lambda i, j: (i, j, 0))
        half = jax.ShapeDtypeStruct((2, size, size), jnp.bfloat16)
        return call(
            split_kernel,
            "split_inverse",
            4 * MIB,
            16 * MIB,
            16,
            out_shape=[half, half],
            grid=(2, 4),
            in_specs=[block],
            out_specs=[block, block],
        )(inverse[0])

    def product(cut, messages, held, hi, lo, *earlier):
        first, slabs = cut
        return call(
            functools.partial(product_kernel, order, held, first, slabs, lower_slabs, width // 2),
            "product",
            6 * size * size * slabs * LANES,
            10 * MIB,
            32,
            out_shape=[jax.ShapeDtypeStruct((slabs * rows + TILE, LANES), jnp.int16)] * groups,
            grid_spec=pltpu.PrefetchScalarGridSpec(
                num_scalar_prefetch=1,
                grid=(),
                in_specs=[pl.BlockSpec(memory_space=pltpu.SMEM)]
                + [vmem] * (groups + 2)
                + [hbm for _ in earlier],
                out_specs=[vmem] * groups,
                scratch_shapes=[
                    pltpu.VMEM((size, 2 * LANES), jnp.bfloat16),
                    pltpu.VMEM((size, 2 * LANES), jnp.bfloat16),
                    pltpu.VMEM((size, 2 * LANES), jnp.float32),
                    pltpu.VMEM((groups, 4, 2 * LANES), jnp.float32),
                    pltpu.VMEM((2, groups, 8, LANES), jnp.float32),
                    pltpu.VMEM((groups, TILE, LANES), jnp.float32),
                ],
            ),
        )(where, edge_weight, *messages, hi, lo, *earlier)

    def result(ks, cut, messages, previous):
        first, slabs = cut
        carried = [] if previous is None else [previous]
        return call(
            functools.partial(result_kernel, len(ks), slabs),
            "result",
            MIB,
            2 * MIB,
            16,
            out_shape=jax.ShapeDtypeStruct(state.shape, jnp.float32),
            grid_spec=pltpu.PrefetchScalarGridSpec(
                num_scalar_prefetch=1,
                grid=(len(ks),),
                in_specs=[pl.BlockSpec(m.shape, lambda k, w: (0, 0)) for m in messages] + [hbm] * len(carried),
                out_specs=columns_block(levels, slabs * LANES, columns_of(ks, width, first * LANES)),
                scratch_shapes=[pltpu.VMEM(messages[0].shape, jnp.int16)],
            ),
            input_output_aliases={} if previous is None else {len(ks) + 1: 0},
        )(where, *messages, *carried)

    made, got = [], {}
    for ks, cut in ((far[:2], shares[0]), (near, shares[0]), (far[2:], shares[0]), (far, shares[1]), (near, shares[1])):
        made = right_side(ks, cut, *made[-1:])
        got.update({(k, cut): send(m, k, groups) for k, m in zip(ks, made)})
    hi, lo = split()
    back, made = [], []
    for first, count in shares:
        messages, held = [], []
        for k in order:
            cut = next(c for j, c in got if j == k and c[0] <= first < sum(c))
            messages.append(got[k, cut])
            held.append((cut[1], first - cut[0]))
        made = product((first, count), messages, tuple(held), hi, lo, *made[-1:])
        back.append({k: send(m, k, groups) for k, m in zip(order, made)})
    out = None
    for i, (cut, came) in enumerate(zip(shares, back)):
        for ks in [order] if i < len(shares) - 1 else [order[:4] + order[-1:], order[4:-1]]:
            out = result(ks, cut, [came[k] for k in ks], out)
    return out


def solution(mesh):
    placed = (
        P(None, "rad", "ang"),
        P(None, "rad", "ang"),
        P(("ang", "rad"), None, None, None),
        P(("ang", "rad")),
    )
    slots = mesh.shape["rad"] * mesh.shape["ang"]
    return jax.shard_map(
        functools.partial(local, slots),
        mesh=mesh,
        in_specs=placed,
        out_specs=P(None, "rad", "ang"),
        check_vma=False,
    )
```

time: 132 us -> 114 us (0.86); the launches traced: 132 us -> 112 us
  waiting for transfers between devices: 44.5 us -> 18.2 us
  Pallas kernels: 28.3 us -> 45.3 us
  starting transfers between devices: 52 us -> 43.4 us
  local copies, waits for them, and re-layouts: 5.86 us -> 3.42 us
    ppermute x30 -> x28, waiting for transfers between devices: 44.5 us -> 18.2 us  [send(): lax.ppermute(message, 'rad', [(i, i ^ k) for i in range(groups)])]
    pallas_call x7 -> x11, Pallas kernels: 28.3 us -> 45.3 us  [the longest x5 20 us: right_side(): call(functools.partial(right_side_kernel, held, len(ks)), 'right_side', M...]
    ppermute x30 -> x28, starting transfers between devices: 52 us -> 43.4 us  [send(): lax.ppermute(message, 'rad', [(i, i ^ k) for i in range(groups)])]
    unnamed x8 -> x22, local copies, waits for them, and re-layouts: 4.73 us -> 3.42 us
  transfers between devices with their start and end apart: 30 -> 28, of which waited for: 12 -> 5; matrix products, arithmetic and copies ran while one was open for 0% -> 0% of each run, Pallas kernels for 16% -> 36%
where the time goes in v3:
time: 114 us; the launch traced here: 112 us
  Pallas kernels  45.3 us (40%)
  starting transfers between devices  43.4 us (38%)
  waiting for transfers between devices  18.2 us (16%)
  local copies, waits for them, and re-layouts  3.42 us (3%)
    ppermute x28, starting transfers between devices, send(): lax.ppermute(message, 'rad', [(i, i ^ k) for i in range(groups)])  43.4 us
    pallas_call x5, Pallas kernels, right_side(): call(functools.partial(right_side_kernel, held, len(ks)), 'right_side', M...  20 us
    ppermute x28, waiting for transfers between devices, send(): lax.ppermute(message, 'rad', [(i, i ^ k) for i in range(groups)])  18.2 us
    pallas_call x2, Pallas kernels, product(): call(functools.partial(product_kernel, order, held, first, slabs, lower_s...  15.2 us
    pallas_call x3, Pallas kernels, result(): call(functools.partial(result_kernel, len(ks), slabs), 'result', MIB, 2 *...  8.73 us
    unnamed x22, local copies, waits for them, and re-layouts  3.42 us
  transfers between devices with their start and end apart: 28, of which 5 were waited for; matrix products, arithmetic and copies ran while one was open for 0% of the time, Pallas kernels for 36%

profile of v3, /device:TPU:8, one launch (start us, length us, event | category | flops | bytes accessed | tf_op | source)
XLA Modules:
  0.0 111.7 jit_solution(5776025399326262894)
XLA Ops:
  1.3 3.1 %right_side.5 = (s16[544,128]{1,0:T(8,128)(2,1)}, s16[544,128]{1,0:T(8,128)(2,1)}) custom-call(s32[2]{0:T(128)} %pad_add_fusion.where, bf16[2,64,8192]{2,1,0:T(8,128)(2,1)} %n_ref.9, f32[2,64,8192]{2,1,0:T(8,128)} %s_ref.9, f32[512,128]{1,0:T(8,128)} %constant.10.clone.tab_ref), custom_call_target="tpu_custom_call" | custom-call | flops 2097152 | bytes 2097152 | tf_op jit(solution)/shard_map/right_side/pallas_call | solution.py:302
  4.4 2.6 %collective-permute-start.7 = (s16[544,128]{1,0:T(8,128)(2,1)}, s16[544,128]{1,0:T(8,128)(2,1)S(1)}, u32[]{:S(2)}, u32[]{:S(2)}) collective-permute-start(s16[544,128]{1,0:T(8,128)(2,1)} %get-tuple-element.52), channel_id=1, source_target_pairs={{0,16},{4,20},{8,24},{12,28},{16,0},{20,4},{24,8},{28,12},{1,17},{... | collective-permute-start | bytes 417800 | tf_op jit(solution)/shard_map/ppermute | solution.py:248
  8.3 4.6 %right_side.6 = (s16[544,128]{1,0:T(8,128)(2,1)}, s16[544,128]{1,0:T(8,128)(2,1)}, s16[544,128]{1,0:T(8,128)(2,1)}, s16[544,128]{1,0:T(8,128)(2,1)}) custom-call(s32[2]{0:T(128)} %pad_add_fusion.where, bf16[2,64,8192]{2,1,0:T(8,128)(2,1)} %n_ref.9, f32[2,64,8192]{2,1,0:T(8,128)} %s_ref.9, f32[512,128]{1,0:T(8,128)} %constant.10.clone.tab_ref, ...), custom_call_target="tpu_custom_call" | custom-call | flops 4194304 | bytes 4194304 | tf_op jit(solution)/shard_map/right_side/pallas_call | solution.py:302
  13.6 2.8 %collective-permute-start.11 = (s16[544,128]{1,0:T(8,128)(2,1)}, s16[544,128]{1,0:T(8,128)(2,1)S(1)}, u32[]{:S(2)}, u32[]{:S(2)}) collective-permute-start(s16[544,128]{1,0:T(8,128)(2,1)} %get-tuple-element.40.refs_0_), channel_id=1, source_target_pairs={{0,12},{4,8},{8,4},{12,0},{16,28},{20,24},{24,20},{28,16},{1,13},{... | collective-permute-start | bytes 417800 | tf_op jit(solution)/shard_map/ppermute | solution.py:248
  16.4 3.1 %right_side.7 = (s16[544,128]{1,0:T(8,128)(2,1)}, s16[544,128]{1,0:T(8,128)(2,1)}) custom-call(s32[2]{0:T(128)} %pad_add_fusion.where, bf16[2,64,8192]{2,1,0:T(8,128)(2,1)} %n_ref.9, f32[2,64,8192]{2,1,0:T(8,128)} %s_ref.9, f32[512,128]{1,0:T(8,128)} %constant.10.clone.tab_ref, s16[544,128]{1,0:T(8,128)(2,1)} %get-tuple-element.40.refs_0_), custom_call_target="tpu_custom_call" | custom-call | flops 2097152 | bytes 2097152 | tf_op jit(solution)/shard_map/right_side/pallas_call | solution.py:302
  21.1 4.6 %right_side.8 = (s16[544,128]{1,0:T(8,128)(2,1)}, s16[544,128]{1,0:T(8,128)(2,1)}, s16[544,128]{1,0:T(8,128)(2,1)}, s16[544,128]{1,0:T(8,128)(2,1)}) custom-call(s32[2]{0:T(128)} %pad_add_fusion.where, bf16[2,64,8192]{2,1,0:T(8,128)(2,1)} %n_ref.9, f32[2,64,8192]{2,1,0:T(8,128)} %s_ref.9, f32[512,128]{1,0:T(8,128)} %constant.10.clone.tab_ref, ...), custom_call_target="tpu_custom_call" | custom-call | flops 4194304 | bytes 4194304 | tf_op jit(solution)/shard_map/right_side/pallas_call | solution.py:302
  26.2 4.4 %collective-permute-start = (s16[544,128]{1,0:T(8,128)(2,1)}, s16[544,128]{1,0:T(8,128)(2,1)S(1)}, u32[]{:S(2)}, u32[]{:S(2)}) collective-permute-start(s16[544,128]{1,0:T(8,128)(2,1)} %get-tuple-element.42), channel_id=1, source_target_pairs={{0,16},{4,20},{8,24},{12,28},{16,0},{20,4},{24,8},{28,12},{1,17},{... | collective-permute-start | bytes 417800 | tf_op jit(solution)/shard_map/ppermute | solution.py:248
  31.6 4.6 %right_side.9 = (s16[544,128]{1,0:T(8,128)(2,1)}, s16[544,128]{1,0:T(8,128)(2,1)}, s16[544,128]{1,0:T(8,128)(2,1)}, s16[544,128]{1,0:T(8,128)(2,1)}) custom-call(s32[2]{0:T(128)} %pad_add_fusion.where, bf16[2,64,8192]{2,1,0:T(8,128)(2,1)} %n_ref.9, f32[2,64,8192]{2,1,0:T(8,128)} %s_ref.9, f32[512,128]{1,0:T(8,128)} %constant.10.clone.tab_ref, ...), custom_call_target="tpu_custom_call" | custom-call | flops 4194304 | bytes 4194304 | tf_op jit(solution)/shard_map/right_side/pallas_call | solution.py:302
  36.3 3.4 %copy-done = f32[1,2,1024,1024]{3,2,1,0:T(8,128)S(1)} copy-done((f32[1,2,1024,1024]{3,2,1,0:T(8,128)S(1)}, f32[1,2,1024,1024]{3,2,1,0:T(8,128)}, u32[]{:S(2)}) %copy-start) | copy-done | bytes 8388632
  41.1 1.9 %collective-permute-start.5 = (s16[544,128]{1,0:T(8,128)(2,1)S(1)}, s16[544,128]{1,0:T(8,128)(2,1)S(1)}, u32[]{:S(2)}, u32[]{:S(2)}) collective-permute-start(s16[544,128]{1,0:T(8,128)(2,1)S(1)} %copy-done.8), channel_id=1, source_target_pairs={{0,24},{4,28},{8,16},{12,20},{16,8},{20,12},{24,0},{28,4},{1,25},{... | collective-permute-start | bytes 417800 | tf_op jit(solution)/shard_map/ppermute | solution.py:248
  44.5 5.6 %collective-permute-start.2 = (s16[544,128]{1,0:T(8,128)(2,1)S(1)}, s16[544,128]{1,0:T(8,128)(2,1)S(1)}, u32[]{:S(2)}, u32[]{:S(2)}) collective-permute-start(s16[544,128]{1,0:T(8,128)(2,1)S(1)} %copy-done.9), channel_id=1, source_target_pairs={{0,8},{4,12},{8,0},{12,4},{16,24},{20,28},{24,16},{28,20},{1,9},{5... | collective-permute-start | bytes 417800 | tf_op jit(solution)/shard_map/ppermute | solution.py:248
  50.1 5.4 %collective-permute-start.4 = (s16[544,128]{1,0:T(8,128)(2,1)S(1)}, s16[544,128]{1,0:T(8,128)(2,1)S(1)}, u32[]{:S(2)}, u32[]{:S(2)}) collective-permute-start(s16[544,128]{1,0:T(8,128)(2,1)S(1)} %copy-done.7), channel_id=1, source_target_pairs={{0,12},{4,8},{8,4},{12,0},{16,28},{20,24},{24,20},{28,16},{1,13},{... | collective-permute-start | bytes 417800 | tf_op jit(solution)/shard_map/ppermute | solution.py:248
  55.5 7.6 %product.2 = (s16[528,128]{1,0:T(8,128)(2,1)S(1)}, s16[528,128]{1,0:T(8,128)(2,1)S(1)}, s16[528,128]{1,0:T(8,128)(2,1)S(1)}, s16[528,128]{1,0:T(8,128)(2,1)S(1)}...) custom-call(s32[2]{0:T(128)S(1)} %copy-done.1, ...), custom_call_target="tpu_custom_call" | custom-call | flops 3221225472 | bytes 10485760 | tf_op jit(solution)/shard_map/product/pallas_call | solution.py:340
  67.7 2.9 %collective-permute-start.25 = (s16[528,128]{1,0:T(8,128)(2,1)S(1)}, s16[528,128]{1,0:T(8,128)(2,1)S(1)}, u32[]{:S(2)}, u32[]{:S(2)}) collective-permute-start(s16[528,128]{1,0:T(8,128)(2,1)S(1)} %get-tuple-element.70), channel_id=1, source_target_pairs={{0,12},{4,8},{8,4},{12,0},{16,28},{20,24},{24,20},{28,16},{1,13},{... | collective-permute-start | bytes 405512 | tf_op jit(solution)/shard_map/ppermute | solution.py:248
  70.6 7.6 %product.3 = (s16[528,128]{1,0:T(8,128)(2,1)S(1)}, s16[528,128]{1,0:T(8,128)(2,1)S(1)}, s16[528,128]{1,0:T(8,128)(2,1)S(1)}, s16[528,128]{1,0:T(8,128)(2,1)S(1)}...) custom-call(s32[2]{0:T(128)S(1)} %copy-done.1, ...), custom_call_target="tpu_custom_call" | custom-call | flops 3221225472 | bytes 10485760 | tf_op jit(solution)/shard_map/product/pallas_call | solution.py:340
  80.3 1.9 %collective-permute-start.17 = (s16[528,128]{1,0:T(8,128)(2,1)S(1)}, s16[528,128]{1,0:T(8,128)(2,1)S(1)}, u32[]{:S(2)}, u32[]{:S(2)}) collective-permute-start(s16[528,128]{1,0:T(8,128)(2,1)S(1)} %get-tuple-element.61), channel_id=1, source_target_pairs={{0,16},{4,20},{8,24},{12,28},{16,0},{20,4},{24,8},{28,12},{1,17},{... | collective-permute-start | bytes 405512 | tf_op jit(solution)/shard_map/ppermute | solution.py:248
  83.8 6.9 %collective-permute-done.26.refs_5_ = s16[528,128]{1,0:T(8,128)(2,1)S(1)} collective-permute-done((s16[528,128]{1,0:T(8,128)(2,1)S(1)}, s16[528,128]{1,0:T(8,128)(2,1)S(1)}, u32[]{:S(2)}, u32[]{:S(2)}) %collective-permute-start.26) | collective-permute-done | bytes 135200 | tf_op jit(solution)/shard_map/ppermute | solution.py:248
  90.6 3.4 %collective-permute-done.27.refs_6_ = s16[528,128]{1,0:T(8,128)(2,1)S(1)} collective-permute-done((s16[528,128]{1,0:T(8,128)(2,1)S(1)}, s16[528,128]{1,0:T(8,128)(2,1)S(1)}, u32[]{:S(2)}, u32[]{:S(2)}) %collective-permute-start.27) | collective-permute-done | bytes 135200 | tf_op jit(solution)/shard_map/ppermute | solution.py:248
  94.1 2.7 %collective-permute-done.17.refs_0_ = s16[528,128]{1,0:T(8,128)(2,1)S(1)} collective-permute-done((s16[528,128]{1,0:T(8,128)(2,1)S(1)}, s16[528,128]{1,0:T(8,128)(2,1)S(1)}, u32[]{:S(2)}, u32[]{:S(2)}) %collective-permute-start.17) | collective-permute-done | bytes 135200 | tf_op jit(solution)/shard_map/ppermute | solution.py:248
  97.9 3.8 %result.3.refs_5_ = f32[2,64,8192]{2,1,0:T(8,128)} custom-call(s32[2]{0:T(128)S(1)} %copy-done.1, s16[528,128]{1,0:T(8,128)(2,1)S(1)} %collective-permute-done.21.refs_0_, s16[528,128]{1,0:T(8,128)(2,1)S(1)} %collective-permute-done.22.refs_1_, s16[528,128]{1,0:T(8,128)(2,1)S(1)} %collective-permute-done.23.refs_2_, ...), custom_call_target="tpu_custom_call" | custom-call | flops 1048576 | bytes 2097152 | tf_op jit(solution)/shard_map/result/pallas_call | solution.py:368
  101.6 2.9 %result.4.refs_3_ = f32[2,64,8192]{2,1,0:T(8,128)} custom-call(s32[2]{0:T(128)S(1)} %copy-done.1, s16[528,128]{1,0:T(8,128)(2,1)S(1)} %collective-permute-done.17.refs_0_, s16[528,128]{1,0:T(8,128)(2,1)S(1)} %collective-permute-done.18.refs_1_, s16[528,128]{1,0:T(8,128)(2,1)S(1)} %collective-permute-done.19.refs_2_, ...), custom_call_target="tpu_custom_call", output_to_operand_aliasing={{}: (6, {})} | custom-call | flops 1048576 | bytes 2097152 | tf_op jit(solution)/shard_map/result/pallas_call | solution.py:368
  104.5 2.6 %collective-permute-done.15.refs_1_ = s16[528,128]{1,0:T(8,128)(2,1)S(1)} collective-permute-done((s16[528,128]{1,0:T(8,128)(2,1)S(1)}, s16[528,128]{1,0:T(8,128)(2,1)S(1)}, u32[]{:S(2)}, u32[]{:S(2)}) %collective-permute-start.15) | collective-permute-done | bytes 135200 | tf_op jit(solution)/shard_map/ppermute | solution.py:248
  107.1 2.6 %collective-permute-done.16.refs_2_ = s16[528,128]{1,0:T(8,128)(2,1)S(1)} collective-permute-done((s16[528,128]{1,0:T(8,128)(2,1)S(1)}, s16[528,128]{1,0:T(8,128)(2,1)S(1)}, u32[]{:S(2)}, u32[]{:S(2)}) %collective-permute-start.16) | collective-permute-done | bytes 135200 | tf_op jit(solution)/shard_map/ppermute | solution.py:248
  109.7 2.1 %result.5 = f32[2,64,8192]{2,1,0:T(8,128)} custom-call(s32[2]{0:T(128)S(1)} %copy-done.1, s16[528,128]{1,0:T(8,128)(2,1)S(1)} %collective-permute-done.14.refs_0_, s16[528,128]{1,0:T(8,128)(2,1)S(1)} %collective-permute-done.15.refs_1_, s16[528,128]{1,0:T(8,128)(2,1)S(1)} %collective-permute-done.16.refs_2_, ...), custom_call_target="tpu_custom_call", output_to_operand_aliasing={{}: (4, {})} | custom-call | flops 1048576 | bytes 2097152 | tf_op jit(solution)/shard_map/result/pallas_call | solution.py:368
  (66 shorter events, 17.8 us)
Async XLA Ops:
  4.4 15.1 %collective-permute-start.7 = (s16[544,128]{1,0:T(8,128)(2,1)}, s16[544,128]{1,0:T(8,128)(2,1)S(1)}, u32[]{:S(2)}, u32[]{:S(2)}) collective-permute-start(s16[544,128]{1,0:T(8,128)(2,1)} %get-tuple-element.52), channel_id=1, source_target_pairs={{0,16},{4,20},{8,24},{12,28},{16,0},{20,4},{24,8},{28,12},{1,17},{... | collective-permute-start | bytes 417800 | tf_op jit(solution)/shard_map/ppermute | solution.py:248
  7.0 18.8 %collective-permute-start.10 = (s16[544,128]{1,0:T(8,128)(2,1)}, s16[544,128]{1,0:T(8,128)(2,1)S(1)}, u32[]{:S(2)}, u32[]{:S(2)}) collective-permute-start(s16[544,128]{1,0:T(8,128)(2,1)} %get-tuple-element.39.refs_0_), channel_id=1, source_target_pairs={{0,20},{4,16},{8,28},{12,24},{16,4},{20,0},{24,12},{28,8},{1,21},{... | collective-permute-start | bytes 417800 | tf_op jit(solution)/shard_map/ppermute | solution.py:248
  12.9 13.3 %collective-permute-start.8 = (s16[544,128]{1,0:T(8,128)(2,1)}, s16[544,128]{1,0:T(8,128)(2,1)S(1)}, u32[]{:S(2)}, u32[]{:S(2)}) collective-permute-start(s16[544,128]{1,0:T(8,128)(2,1)} %get-tuple-element.53), channel_id=1, source_target_pairs={{0,4},{4,0},{8,12},{12,8},{16,20},{20,16},{24,28},{28,24},{1,5},{5... | collective-permute-start | bytes 417800 | tf_op jit(solution)/shard_map/ppermute | solution.py:248
  13.4 17.2 %collective-permute-start.9 = (s16[544,128]{1,0:T(8,128)(2,1)}, s16[544,128]{1,0:T(8,128)(2,1)S(1)}, u32[]{:S(2)}, u32[]{:S(2)}) collective-permute-start(s16[544,128]{1,0:T(8,128)(2,1)} %get-tuple-element.54), channel_id=1, source_target_pairs={{0,8},{4,12},{8,0},{12,4},{16,24},{20,28},{24,16},{28,20},{1,9},{5... | collective-permute-start | bytes 417800 | tf_op jit(solution)/shard_map/ppermute | solution.py:248
  13.6 27.4 %collective-permute-start.11 = (s16[544,128]{1,0:T(8,128)(2,1)}, s16[544,128]{1,0:T(8,128)(2,1)S(1)}, u32[]{:S(2)}, u32[]{:S(2)}) collective-permute-start(s16[544,128]{1,0:T(8,128)(2,1)} %get-tuple-element.40.refs_0_), channel_id=1, source_target_pairs={{0,12},{4,8},{8,4},{12,0},{16,28},{20,24},{24,20},{28,16},{1,13},{... | collective-permute-start | bytes 417800 | tf_op jit(solution)/shard_map/ppermute | solution.py:248
  19.5 21.5 %collective-permute-start.12 = (s16[544,128]{1,0:T(8,128)(2,1)}, s16[544,128]{1,0:T(8,128)(2,1)S(1)}, u32[]{:S(2)}, u32[]{:S(2)}) collective-permute-start(s16[544,128]{1,0:T(8,128)(2,1)} %get-tuple-element.55), channel_id=1, source_target_pairs={{0,24},{4,28},{8,16},{12,20},{16,8},{20,12},{24,0},{28,4},{1,25},{... | collective-permute-start | bytes 417800 | tf_op jit(solution)/shard_map/ppermute | solution.py:248
  25.8 17.3 %collective-permute-start.13 = (s16[544,128]{1,0:T(8,128)(2,1)S(1)}, s16[544,128]{1,0:T(8,128)(2,1)S(1)}, u32[]{:S(2)}, u32[]{:S(2)}) collective-permute-start(s16[544,128]{1,0:T(8,128)(2,1)S(1)} %copy-done.6), channel_id=1, source_target_pairs={{0,28},{4,24},{8,20},{12,16},{16,12},{20,8},{24,4},{28,0},{1,29},{... | collective-permute-start | bytes 417800 | tf_op jit(solution)/shard_map/ppermute | solution.py:248
  26.2 18.3 %collective-permute-start = (s16[544,128]{1,0:T(8,128)(2,1)}, s16[544,128]{1,0:T(8,128)(2,1)S(1)}, u32[]{:S(2)}, u32[]{:S(2)}) collective-permute-start(s16[544,128]{1,0:T(8,128)(2,1)} %get-tuple-element.42), channel_id=1, source_target_pairs={{0,16},{4,20},{8,24},{12,28},{16,0},{20,4},{24,8},{28,12},{1,17},{... | collective-permute-start | bytes 417800 | tf_op jit(solution)/shard_map/ppermute | solution.py:248
  30.6 19.5 %collective-permute-start.3 = (s16[544,128]{1,0:T(8,128)(2,1)}, s16[544,128]{1,0:T(8,128)(2,1)S(1)}, u32[]{:S(2)}, u32[]{:S(2)}) collective-permute-start(s16[544,128]{1,0:T(8,128)(2,1)} %get-tuple-element.46), channel_id=1, source_target_pairs={{0,20},{4,16},{8,28},{12,24},{16,4},{20,0},{24,12},{28,8},{1,21},{... | collective-permute-start | bytes 417800 | tf_op jit(solution)/shard_map/ppermute | solution.py:248
  41.0 22.3 %collective-permute-start.6 = (s16[544,128]{1,0:T(8,128)(2,1)S(1)}, s16[544,128]{1,0:T(8,128)(2,1)S(1)}, u32[]{:S(2)}, u32[]{:S(2)}) collective-permute-start(s16[544,128]{1,0:T(8,128)(2,1)S(1)} %copy-done.5), channel_id=1, source_target_pairs={{0,28},{4,24},{8,20},{12,16},{16,12},{20,8},{24,4},{28,0},{1,29},{... | collective-permute-start | bytes 417800 | tf_op jit(solution)/shard_map/ppermute | solution.py:248
  41.1 22.1 %collective-permute-start.5 = (s16[544,128]{1,0:T(8,128)(2,1)S(1)}, s16[544,128]{1,0:T(8,128)(2,1)S(1)}, u32[]{:S(2)}, u32[]{:S(2)}) collective-permute-start(s16[544,128]{1,0:T(8,128)(2,1)S(1)} %copy-done.8), channel_id=1, source_target_pairs={{0,24},{4,28},{8,16},{12,20},{16,8},{20,12},{24,0},{28,4},{1,25},{... | collective-permute-start | bytes 417800 | tf_op jit(solution)/shard_map/ppermute | solution.py:248
  43.0 21.8 %collective-permute-start.1 = (s16[544,128]{1,0:T(8,128)(2,1)S(1)}, s16[544,128]{1,0:T(8,128)(2,1)S(1)}, u32[]{:S(2)}, u32[]{:S(2)}) collective-permute-start(s16[544,128]{1,0:T(8,128)(2,1)S(1)} %copy-done.10), channel_id=1, source_target_pairs={{0,4},{4,0},{8,12},{12,8},{16,20},{20,16},{24,28},{28,24},{1,5},{5... | collective-permute-start | bytes 417800 | tf_op jit(solution)/shard_map/ppermute | solution.py:248
  44.5 21.3 %collective-permute-start.2 = (s16[544,128]{1,0:T(8,128)(2,1)S(1)}, s16[544,128]{1,0:T(8,128)(2,1)S(1)}, u32[]{:S(2)}, u32[]{:S(2)}) collective-permute-start(s16[544,128]{1,0:T(8,128)(2,1)S(1)} %copy-done.9), channel_id=1, source_target_pairs={{0,8},{4,12},{8,0},{12,4},{16,24},{20,28},{24,16},{28,20},{1,9},{5... | collective-permute-start | bytes 417800 | tf_op jit(solution)/shard_map/ppermute | solution.py:248
  50.1 17.6 %collective-permute-start.4 = (s16[544,128]{1,0:T(8,128)(2,1)S(1)}, s16[544,128]{1,0:T(8,128)(2,1)S(1)}, u32[]{:S(2)}, u32[]{:S(2)}) collective-permute-start(s16[544,128]{1,0:T(8,128)(2,1)S(1)} %copy-done.7), channel_id=1, source_target_pairs={{0,12},{4,8},{8,4},{12,0},{16,28},{20,24},{24,20},{28,16},{1,13},{... | collective-permute-start | bytes 417800 | tf_op jit(solution)/shard_map/ppermute | solution.py:248
  63.2 15.1 %collective-permute-start.21 = (s16[528,128]{1,0:T(8,128)(2,1)S(1)}, s16[528,128]{1,0:T(8,128)(2,1)S(1)}, u32[]{:S(2)}, u32[]{:S(2)}) collective-permute-start(s16[528,128]{1,0:T(8,128)(2,1)S(1)} %get-tuple-element.66), channel_id=1, source_target_pairs={{0,16},{4,20},{8,24},{12,28},{16,0},{20,4},{24,8},{28,12},{1,17},{... | collective-permute-start | bytes 405512 | tf_op jit(solution)/shard_map/ppermute | solution.py:248
  63.2 15.1 %collective-permute-start.22 = (s16[528,128]{1,0:T(8,128)(2,1)S(1)}, s16[528,128]{1,0:T(8,128)(2,1)S(1)}, u32[]{:S(2)}, u32[]{:S(2)}) collective-permute-start(s16[528,128]{1,0:T(8,128)(2,1)S(1)} %get-tuple-element.67), channel_id=1, source_target_pairs={{0,4},{4,0},{8,12},{12,8},{16,20},{20,16},{24,28},{28,24},{1,5},{5... | collective-permute-start | bytes 405512 | tf_op jit(solution)/shard_map/ppermute | solution.py:248
  64.9 15.4 %collective-permute-start.23 = (s16[528,128]{1,0:T(8,128)(2,1)S(1)}, s16[528,128]{1,0:T(8,128)(2,1)S(1)}, u32[]{:S(2)}, u32[]{:S(2)}) collective-permute-start(s16[528,128]{1,0:T(8,128)(2,1)S(1)} %get-tuple-element.68), channel_id=1, source_target_pairs={{0,8},{4,12},{8,0},{12,4},{16,24},{20,28},{24,16},{28,20},{1,9},{5... | collective-permute-start | bytes 405512 | tf_op jit(solution)/shard_map/ppermute | solution.py:248
  65.8 16.4 %collective-permute-start.24 = (s16[528,128]{1,0:T(8,128)(2,1)S(1)}, s16[528,128]{1,0:T(8,128)(2,1)S(1)}, u32[]{:S(2)}, u32[]{:S(2)}) collective-permute-start(s16[528,128]{1,0:T(8,128)(2,1)S(1)} %get-tuple-element.69), channel_id=1, source_target_pairs={{0,20},{4,16},{8,28},{12,24},{16,4},{20,0},{24,12},{28,8},{1,21},{... | collective-permute-start | bytes 405512 | tf_op jit(solution)/shard_map/ppermute | solution.py:248
  67.7 16.0 %collective-permute-start.25 = (s16[528,128]{1,0:T(8,128)(2,1)S(1)}, s16[528,128]{1,0:T(8,128)(2,1)S(1)}, u32[]{:S(2)}, u32[]{:S(2)}) collective-permute-start(s16[528,128]{1,0:T(8,128)(2,1)S(1)} %get-tuple-element.70), channel_id=1, source_target_pairs={{0,12},{4,8},{8,4},{12,0},{16,28},{20,24},{24,20},{28,16},{1,13},{... | collective-permute-start | bytes 405512 | tf_op jit(solution)/shard_map/ppermute | solution.py:248
  78.3 12.4 %collective-permute-start.26 = (s16[528,128]{1,0:T(8,128)(2,1)S(1)}, s16[528,128]{1,0:T(8,128)(2,1)S(1)}, u32[]{:S(2)}, u32[]{:S(2)}) collective-permute-start(s16[528,128]{1,0:T(8,128)(2,1)S(1)} %get-tuple-element.71), channel_id=1, source_target_pairs={{0,24},{4,28},{8,16},{12,20},{16,8},{20,12},{24,0},{28,4},{1,25},{... | collective-permute-start | bytes 405512 | tf_op jit(solution)/shard_map/ppermute | solution.py:248
  78.3 15.7 %collective-permute-start.27 = (s16[528,128]{1,0:T(8,128)(2,1)S(1)}, s16[528,128]{1,0:T(8,128)(2,1)S(1)}, u32[]{:S(2)}, u32[]{:S(2)}) collective-permute-start(s16[528,128]{1,0:T(8,128)(2,1)S(1)} %get-tuple-element.72), channel_id=1, source_target_pairs={{0,28},{4,24},{8,20},{12,16},{16,12},{20,8},{24,4},{28,0},{1,29},{... | collective-permute-start | bytes 405512 | tf_op jit(solution)/shard_map/ppermute | solution.py:248
  80.3 16.5 %collective-permute-start.17 = (s16[528,128]{1,0:T(8,128)(2,1)S(1)}, s16[528,128]{1,0:T(8,128)(2,1)S(1)}, u32[]{:S(2)}, u32[]{:S(2)}) collective-permute-start(s16[528,128]{1,0:T(8,128)(2,1)S(1)} %get-tuple-element.61), channel_id=1, source_target_pairs={{0,16},{4,20},{8,24},{12,28},{16,0},{20,4},{24,8},{28,12},{1,17},{... | collective-permute-start | bytes 405512 | tf_op jit(solution)/shard_map/ppermute | solution.py:248
  82.2 15.6 %collective-permute-start.18 = (s16[528,128]{1,0:T(8,128)(2,1)S(1)}, s16[528,128]{1,0:T(8,128)(2,1)S(1)}, u32[]{:S(2)}, u32[]{:S(2)}) collective-permute-start(s16[528,128]{1,0:T(8,128)(2,1)S(1)} %get-tuple-element.62), channel_id=1, source_target_pairs={{0,4},{4,0},{8,12},{12,8},{16,20},{20,16},{24,28},{28,24},{1,5},{5... | collective-permute-start | bytes 405512 | tf_op jit(solution)/shard_map/ppermute | solution.py:248
  83.7 17.9 %collective-permute-start.19 = (s16[528,128]{1,0:T(8,128)(2,1)S(1)}, s16[528,128]{1,0:T(8,128)(2,1)S(1)}, u32[]{:S(2)}, u32[]{:S(2)}) collective-permute-start(s16[528,128]{1,0:T(8,128)(2,1)S(1)} %get-tuple-element.63), channel_id=1, source_target_pairs={{0,8},{4,12},{8,0},{12,4},{16,24},{20,28},{24,16},{28,20},{1,9},{5... | collective-permute-start | bytes 405512 | tf_op jit(solution)/shard_map/ppermute | solution.py:248
  (15 other events, 137.3 us)

commit v4 on v3

v4 whole, which is shorter than its diff:
```python
import functools
import math

import jax
import jax.numpy as jnp
import numpy as np
from jax import lax
from jax.experimental import pallas as pl
from jax.experimental.pallas import tpu as pltpu
from jax.sharding import PartitionSpec as P

inner_radius = 0.35
outer_radius = 1.0
blend_weight = 0.5

LANES = 128
TILE = 16
EXTRA = 8
CHUNKS = 2
TOP = 32700.0
EDGE_TOP = 16384.0
FINE = 128.0
MIB = 1024 * 1024


def radius_at(level_index, total_levels):
    scaled = level_index / (total_levels - 1.0)
    stretch = (1.0 - blend_weight) * scaled + blend_weight * (1.0 - np.cos(math.pi * scaled)) / 2.0
    return inner_radius + (outer_radius - inner_radius) * stretch


def stencil_table(total_levels):
    k = np.arange(total_levels, dtype=np.float64)
    radius = radius_at(k, total_levels)
    below = radius - radius_at(k - 1.0, total_levels)
    above = radius_at(k + 1.0, total_levels) - radius
    at_inner, at_outer = k == 0, k == total_levels - 1
    weight_below = np.where(at_inner, 0.0, np.where(at_outer, -1.0 / below, -above / (below * (below + above))))
    weight_here = np.where(
        at_inner, -1.0 / above, np.where(at_outer, 1.0 / below, (above - below) / (below * above))
    )
    weight_above = np.where(at_inner, 1.0 / above, np.where(at_outer, 0.0, below / (above * (below + above))))
    time_step = 0.5 * (outer_radius - inner_radius) / (total_levels - 1.0)
    table = np.zeros((total_levels, LANES), np.float32)
    table[:, 0] = time_step * weight_below
    table[:, 1] = time_step * (weight_here + 2.0 / radius)
    table[:, 2] = time_step * weight_above
    return table


def scale_code(largest, per_octave):
    return jnp.ceil(jnp.log2(jnp.maximum(largest, 1e-30)) * per_octave) * (FINE / per_octave)


def encode_factor(code, top):
    return jnp.exp2(code * (-1.0 / FINE)) * top


def to_int16(values):
    return values.astype(jnp.int32).astype(jnp.int16)


def to_float(codes):
    return codes.astype(jnp.int32).astype(jnp.float32)


def scale_of(codes, top):
    return jnp.exp2(codes * (1.0 / FINE)) * (1.0 / top)


def lanes_of(slab):
    return pl.ds(pl.multiple_of(slab * LANES, LANES), LANES)


def right_side_kernel(slabs, partners, where, n_low, n_high, s_low, s_high, tab_ref, *refs):
    outs, (buffer, values, tops, extra) = refs[-4 - partners : -4], refs[-4:]
    levels = n_low.shape[1]
    rows = 2 * levels
    tab = tab_ref[...]
    below, here, above = (jnp.broadcast_to(tab[:, i : i + 1], (levels, LANES)) for i in range(3))
    row = lax.broadcasted_iota(jnp.int32, (levels, LANES), 0)

    def rows_of(slab):
        return pl.ds(pl.multiple_of(slab * rows, rows), rows)

    def compute(pair, _):
        cols = lanes_of(pair)
        for half, (n_ref, s_ref) in enumerate(((n_low, s_low), (n_high, s_high))):
            slab = pair * 2 + half
            ends, top = [], jnp.zeros((8, LANES), jnp.float32)
            for f in range(2):
                n = n_ref[f, :, cols].astype(jnp.float32)
                prev = jnp.where(row == 0, n, pltpu.roll(n, 1, 0))
                succ = jnp.where(row == levels - 1, n, pltpu.roll(n, levels - 1, 0))
                v = s_ref[f, :, cols] + (below * prev + here * n + above * succ)
                values[pl.ds(pl.multiple_of(slab * rows + f * levels, levels), levels), :] = v
                top = jnp.maximum(top, jnp.max(jnp.abs(v).reshape(levels // 8, 8, LANES), axis=0))
                ends += [n[:1], n[levels - 1 :]]
            tops[slab] = top
            extra[slab] = jnp.concatenate(ends + [jnp.zeros((4, LANES), jnp.float32)], axis=0)
        return 0

    lax.fori_loop(0, slabs // 2, compute, 0)
    ends = extra[...]
    code = scale_code(jnp.max(tops[...], axis=1), FINE)
    factor = encode_factor(code, TOP)
    edge_code = scale_code(jnp.max(jnp.abs(ends), axis=1), 1.0)
    edge_factor = encode_factor(edge_code, EDGE_TOP)
    at_row = lax.broadcasted_iota(jnp.int32, ends.shape, 1)
    ends = jnp.round(ends * edge_factor[:, None, :])
    ends = jnp.where(at_row == 4, edge_code[:, None, :], jnp.where(at_row == 5, code[:, None, :], ends))
    buffer[slabs * rows :, :] = to_int16(ends.reshape(slabs * EXTRA, LANES))
    tops[:, 0, :] = factor

    def code_slab(slab, _):
        buffer[rows_of(slab), :] = to_int16(jnp.round(values[rows_of(slab), :] * tops[slab, 0:1, :]))
        return 0

    lax.fori_loop(0, slabs, code_slab, 0, unroll=2)
    step = pl.program_id(0)
    for at, out in enumerate(outs):

        @pl.when(step == at)
        def _():
            out[...] = buffer[...]


def split_kernel(a_ref, both_ref):
    a = a_ref[...]
    size = a.shape[-1]
    hi = a.astype(jnp.bfloat16)
    both_ref[:, :, size:] = hi
    both_ref[:, :, :size] = (a - hi.astype(jnp.float32)).astype(jnp.bfloat16)


def swapped(edges):
    return jnp.concatenate([edges[1:2], edges[0:1], edges[3:4], edges[2:3]], axis=0)


def product_kernel(order, first_slab, slabs, lower_slabs, where, edge_weight, *refs):
    groups = len(order)
    ins, both_ref = refs[:groups], refs[groups]
    outs, scratch, all_codes = refs[-groups - 9 : -9], refs[-9:-1], refs[-1]
    size = both_ref.shape[1]
    levels = size // (2 * groups)
    rows = 2 * levels
    me = where[0]
    pair = where[1]
    peers = [lax.bitwise_xor(me, k) for k in order]
    near = lax.broadcasted_iota(jnp.int32, (8, LANES), 0)

    def place(f, peer):
        return pl.ds(pl.multiple_of(f * (size // 2) + peer * levels, levels), levels)

    def one_tile(t):
        v_both, y, edges, codes = scratch[t % 2 * 4 : t % 2 * 4 + 4]
        extras = []
        for ref, peer in zip(ins, peers):
            at = slabs * rows + t * TILE
            two = to_float(ref[at : at + TILE, :])
            power = jnp.exp2(two * (1.0 / FINE))
            extras.append(power)
            for j in range(2):
                at = j * EXTRA
                edges[peer, :, j * LANES : (j + 1) * LANES] = two[at : at + 4] * (
                    power[at + 4 : at + 5] * (1.0 / EDGE_TOP)
                )
        for ref, peer, power in zip(ins, peers, extras):
            before, after = jnp.maximum(peer - 1, 0), jnp.minimum(peer + 1, groups - 1)
            weight_before, weight_after = edge_weight[peer], edge_weight[groups + peer]
            for j in range(2):
                cols = slice(j * LANES, (j + 1) * LANES)
                scale = power[j * EXTRA + 5 : j * EXTRA + 6] * (1.0 / TOP)
                here = swapped(edges[peer, :, cols])
                low = weight_before * (edges[before, :, cols] - here)
                high = weight_after * (edges[after, :, cols] - here)
                start = (t * 2 + j) * rows
                for f in range(2):
                    v = to_float(ref[start + f * levels : start + (f + 1) * levels, :]) * scale
                    first = v[:8] + jnp.where(near == 0, low[2 * f + 1 : 2 * f + 2], 0.0)
                    last = v[levels - 8 :] + jnp.where(near == 7, high[2 * f : 2 * f + 1], 0.0)
                    middle = [v[8 : levels - 8]] if levels > 16 else []
                    v = jnp.concatenate([first] + middle + [last], axis=0)
                    hi = v.astype(jnp.bfloat16)
                    v_both[place(f, peer), cols] = hi
                    v_both[place(f + 2, peer), cols] = (v - hi.astype(jnp.float32)).astype(jnp.bfloat16)

        def product(which):
            dot = functools.partial(jnp.dot, preferred_element_type=jnp.float32)
            return dot(both_ref[which], v_both[...]) + dot(both_ref[which, :, size:], v_both[:size, :])

        upper = product(1)
        if first_slab + t < lower_slabs:
            lane = lax.broadcasted_iota(jnp.int32, upper.shape, 1)
            column = (first_slab + t) * LANES + jnp.where(lane < LANES, lane, lane - LANES + 1)
            y[...] = jnp.where(column < pair + 1, product(0), upper)
        else:
            y[...] = upper

        def results(peer, j):
            return jnp.concatenate([y[place(f, peer), j * LANES : (j + 1) * LANES] for f in range(2)], axis=0)

        for i, peer in enumerate(peers):
            for j in range(2):
                v = jnp.abs(results(peer, j))
                codes[j, i] = jnp.max(v.reshape(rows // 8, 8, LANES), axis=0)
        code = scale_code(jnp.max(codes[...], axis=2), FINE)
        factor = encode_factor(code, TOP)
        for i, (out, peer) in enumerate(zip(outs, peers)):
            for j in range(2):
                start = (t * 2 + j) * rows
                out[start : start + rows, :] = to_int16(
                    jnp.round(results(peer, j) * factor[j, i : i + 1])
                )
                all_codes[i, t * 2 + j : t * 2 + j + 1, :] = code[j, i : i + 1]

    all_codes[...] = jnp.zeros_like(all_codes)
    for t in range(slabs // 2):
        one_tile(t)
    for i, out in enumerate(outs):
        out[slabs * rows :, :] = to_int16(all_codes[i])


def result_kernel(ks, slabs, skipped, width, where, *refs):
    count = len(ks)
    ins, (out_ref, buffer, sems) = refs[:count], refs[-3:]
    levels = out_ref.shape[1]
    rows = 2 * levels
    span = slabs // 2 * LANES
    copies = []
    for at, (message, k) in enumerate(zip(ins, ks)):
        scales = scale_of(to_float(message[slabs * rows :, :]), TOP)
        first_col = lax.bitwise_xor(where[0], k) * width + skipped
        for half in range(2):
            for pair in range(slabs // 2):
                slab = pair * 2 + half
                for f in range(2):
                    start = slab * rows + f * levels
                    v = to_float(message[start : start + levels, :])
                    buffer[at, half, f, :, pair * LANES : (pair + 1) * LANES] = v * scales[slab : slab + 1, :]
            cols = pl.ds(pl.multiple_of(first_col + half * (width // 2), LANES), span)
            copies.append(pltpu.make_async_copy(buffer.at[at, half], out_ref.at[:, :, cols], sems.at[at, half]))
            copies[-1].start()
    for copy in copies:
        copy.wait()


def send(message, k, groups):
    return message if k == 0 else lax.ppermute(message, "rad", [(i, i ^ k) for i in range(groups)])


def columns_of(ks, width, first):
    def at(step, w):
        k = jnp.int32(ks[-1])
        for i, value in enumerate(ks[:-1]):
            k = jnp.where(step == i, value, k)
        return (0, 0, pl.multiple_of(lax.bitwise_xor(w[0], k) * width + first, LANES))

    return at


def columns_block(levels, count, index_map):
    return pl.BlockSpec((pl.Element(2), pl.Element(levels), pl.Element(count)), index_map)


def local(slots, nonlin, state, inverse, pair_of_slot):
    levels = nonlin.shape[1]
    groups = lax.axis_size("rad")
    width = nonlin.shape[2] // groups
    size = inverse.shape[-1]
    all_slabs = width // LANES
    half_cols = width // 2
    span = half_cols // CHUNKS
    slabs = 2 * span // LANES
    rows = 2 * levels
    lower_slabs = -(-slots // LANES)
    me = lax.axis_index("rad").astype(jnp.int32)
    where = jnp.stack([me, pair_of_slot[0].astype(jnp.int32)])
    weights = stencil_table(levels * groups)
    table = jnp.asarray(weights)
    edge_weight = jnp.asarray(np.concatenate([weights[::levels, 0], weights[levels - 1 :: levels, 2]]))
    vmem = pl.BlockSpec(memory_space=pltpu.VMEM)
    hbm = pl.BlockSpec(memory_space=pl.ANY)
    far = list(range(groups // 2, groups))
    near = list(range(groups // 2))
    others = near[1:]
    order = []
    for i, k in enumerate(far):
        order += [k] + others[2 * i : 2 * i + 2]
    order += near[:1]

    def call(kernel, name, flops, moved, vmem_mib, **kwargs):
        return pl.pallas_call(
            kernel,
            name=name,
            compiler_params=pltpu.CompilerParams(vmem_limit_bytes=vmem_mib * MIB),
            cost_estimate=pl.CostEstimate(flops=flops, bytes_accessed=moved, transcendentals=0),
            **kwargs,
        )

    def right_side(ks, chunk, *earlier):
        low, high = (
            columns_block(levels, span, columns_of(ks, width, first))
            for first in (chunk * span, half_cols + chunk * span)
        )
        out_rows = slabs * (rows + EXTRA)
        return call(
            functools.partial(right_side_kernel, slabs, len(ks)),
            "right_side",
            MIB * len(ks),
            MIB * len(ks),
            56,
            out_shape=[jax.ShapeDtypeStruct((out_rows, LANES), jnp.int16)] * len(ks),
            grid_spec=pltpu.PrefetchScalarGridSpec(
                num_scalar_prefetch=1,
                grid=(len(ks),),
                in_specs=[low, high, low, high, pl.BlockSpec((levels, LANES), lambda k, w: (w[0], 0))]
                + [hbm for _ in earlier],
                out_specs=[pl.BlockSpec((out_rows, LANES), lambda k, w: (0, 0))] * len(ks),
                scratch_shapes=[
                    pltpu.VMEM((out_rows, LANES), jnp.int16),
                    pltpu.VMEM((slabs * rows, LANES), jnp.float32),
                    pltpu.VMEM((slabs, 8, LANES), jnp.float32),
                    pltpu.VMEM((slabs, EXTRA, LANES), jnp.float32),
                ],
            ),
        )(where, nonlin, nonlin, state, state, table, *earlier)

    def split():
        block = pl.BlockSpec((1, size // 4, size), lambda i, j: (i, j, 0))
        return call(
            split_kernel,
            "split_inverse",
            4 * MIB,
            16 * MIB,
            16,
            out_shape=jax.ShapeDtypeStruct((2, size, 2 * size), jnp.bfloat16),
            grid=(2, 4),
            in_specs=[block],
            out_specs=pl.BlockSpec((1, size // 4, 2 * size), lambda i, j: (i, j, 0)),
        )(inverse[0])

    def product(chunk, messages, both, *earlier):
        return call(
            functools.partial(product_kernel, order, chunk * span // LANES, slabs, lower_slabs),
            "product",
            6 * size * size * slabs * LANES,
            10 * MIB,
            32,
            out_shape=[jax.ShapeDtypeStruct((slabs * rows + TILE, LANES), jnp.int16)] * groups,
            grid_spec=pltpu.PrefetchScalarGridSpec(
                num_scalar_prefetch=1,
                grid=(),
                in_specs=[pl.BlockSpec(memory_space=pltpu.SMEM)]
                + [vmem] * (groups + 1)
                + [hbm for _ in earlier],
                out_specs=[vmem] * groups,
                scratch_shapes=2
                * [
                    pltpu.VMEM((2 * size, 2 * LANES), jnp.bfloat16),
                    pltpu.VMEM((size, 2 * LANES), jnp.float32),
                    pltpu.VMEM((groups, 4, 2 * LANES), jnp.float32),
                    pltpu.VMEM((2, groups, 8, LANES), jnp.float32),
                ]
                + [pltpu.VMEM((groups, TILE, LANES), jnp.float32)],
            ),
        )(where, edge_weight, *messages, both, *earlier)

    def result(ks, chunk, messages, previous):
        carried = [] if previous is None else [previous]
        return call(
            functools.partial(result_kernel, ks, slabs, chunk * span, width),
            "result",
            MIB,
            2 * MIB,
            16,
            out_shape=jax.ShapeDtypeStruct(state.shape, jnp.float32),
            grid_spec=pltpu.PrefetchScalarGridSpec(
                num_scalar_prefetch=1,
                grid=(),
                in_specs=[vmem] * len(messages) + [hbm] * len(carried),
                out_specs=hbm,
                scratch_shapes=[
                    pltpu.VMEM((len(ks), 2, 2, levels, span), jnp.float32),
                    pltpu.SemaphoreType.DMA((len(ks), 2)),
                ],
            ),
            input_output_aliases={} if previous is None else {len(ks) + 1: 0},
        )(where, *messages, *carried)

    made, got = [], {}
    for ks, chunk in ((far[:2], 0), (near + far[2:], 0), (far + near, 1)):
        made = right_side(ks, chunk, *made[-1:])
        got.update({(k, chunk): send(m, k, groups) for k, m in zip(ks, made)})
    both = split()
    back, made = [], []
    for chunk in range(CHUNKS):
        made = product(chunk, [got[k, chunk] for k in order], both, *made[-1:])
        back.append({k: send(m, k, groups) for k, m in zip(order, made)})
    out = None
    for chunk, came in enumerate(back):
        for ks in [order] if chunk < CHUNKS - 1 else [order[:4] + order[-1:], order[4:-1]]:
            out = result(ks, chunk, [came[k] for k in ks], out)
    return out


def solution(mesh):
    placed = (
        P(None, "rad", "ang"),
        P(None, "rad", "ang"),
        P(("ang", "rad"), None, None, None),
        P(("ang", "rad")),
    )
    slots = mesh.shape["rad"] * mesh.shape["ang"]
    return jax.shard_map(
        functools.partial(local, slots),
        mesh=mesh,
        in_specs=placed,
        out_specs=P(None, "rad", "ang"),
        check_vma=False,
    )
```

time: 114 us -> 110 us (0.965)
  Pallas kernels: 45.3 us -> 36.3 us
  waiting for transfers between devices: 18.2 us -> 24.3 us
    pallas_call x11 -> x9, Pallas kernels: 45.3 us -> 36.3 us  [the longest x3 17.5 us: right_side(): call(functools.partial(right_side_kernel, slabs, len(ks)), 'right_side',...]
    ppermute x28, waiting for transfers between devices: 18.2 us -> 24.3 us  [send(): lax.ppermute(message, 'rad', [(i, i ^ k) for i in range(groups)])]
  transfers between devices with their start and end apart: 28 -> 28, of which waited for: 5 -> 9; matrix products, arithmetic and copies ran while one was open for 0% -> 0% of each run, Pallas kernels for 36% -> 29%
where the time goes in v4:
time: 110 us; the launch traced here: 109 us
  starting transfers between devices  43.2 us (39%)
  Pallas kernels  36.3 us (33%)
  waiting for transfers between devices  24.3 us (22%)
  local copies, waits for them, and re-layouts  3.42 us (3%)
    ppermute x28, starting transfers between devices, send(): lax.ppermute(message, 'rad', [(i, i ^ k) for i in range(groups)])  43.2 us
    ppermute x28, waiting for transfers between devices, send(): lax.ppermute(message, 'rad', [(i, i ^ k) for i in range(groups)])  24.3 us
    pallas_call x3, Pallas kernels, right_side(): call(functools.partial(right_side_kernel, slabs, len(ks)), 'right_side',...  17.5 us
    pallas_call x2, Pallas kernels, product(): call(functools.partial(product_kernel, order, chunk * span // LANES, slab...  12.4 us
    pallas_call x3, Pallas kernels, result(): call(functools.partial(result_kernel, ks, slabs, chunk * span, width), 'r...  5.17 us
    unnamed x22, local copies, waits for them, and re-layouts  3.42 us
  transfers between devices with their start and end apart: 28, of which 9 were waited for; matrix products, arithmetic and copies ran while one was open for 0% of the time, Pallas kernels for 29%

profile of v4, /device:TPU:8, one launch (start us, length us, event | category | flops | bytes accessed | tf_op | source)
XLA Modules:
  0.0 108.8 jit_solution(1787699918080787620)
XLA Ops:
  1.3 3.1 %right_side.3 = (s16[544,128]{1,0:T(8,128)(2,1)}, s16[544,128]{1,0:T(8,128)(2,1)}) custom-call(s32[2]{0:T(128)} %pad_add_fusion.where, bf16[2,64,8192]{2,1,0:T(8,128)(2,1)} %n_high.5, bf16[2,64,8192]{2,1,0:T(8,128)(2,1)} %n_high.5, f32[2,64,8192]{2,1,0:T(8,128)} %s_high.5, f32[2,64,8192]{2,1,0:T(8,128)} %s_high.5, f32[512,128]{1,0:T(8,128)} %constant.10.clone.tab_ref), custom_call_target="tpu_custom_call" | custom-call | flops 2097152 | bytes 2097152 | tf_op jit(solution)/shard_map/right_side/pallas_call | solution.py:307
  4.5 2.6 %collective-permute-start.7 = (s16[544,128]{1,0:T(8,128)(2,1)}, s16[544,128]{1,0:T(8,128)(2,1)S(1)}, u32[]{:S(2)}, u32[]{:S(2)}) collective-permute-start(s16[544,128]{1,0:T(8,128)(2,1)} %get-tuple-element.47), channel_id=1, source_target_pairs={{0,16},{4,20},{8,24},{12,28},{16,0},{20,4},{24,8},{28,12},{1,17},{... | collective-permute-start | bytes 417800 | tf_op jit(solution)/shard_map/ppermute | solution.py:249
  8.3 6.3 %right_side.4 = (s16[544,128]{1,0:T(8,128)(2,1)}, s16[544,128]{1,0:T(8,128)(2,1)}, s16[544,128]{1,0:T(8,128)(2,1)}, s16[544,128]{1,0:T(8,128)(2,1)}, s16[544,128]{1,0:T(8,128)(2,1)}, /*index=5*/s16[544,128]{1,0:T(8,128)(2,1)}) custom-call(s32[2]{0:T(128)} %pad_add_fusion.where, bf16[2,64,8192]{2,1,0:T(8,128)(2,1)} %n_high.5, bf16[2,64,8192]{2,1,0:T(8,128)(2,1)} %n_high.5, ...), custom_call_target="tpu_custom_call" | custom-call | flops 6291456 | bytes 6291456 | tf_op jit(solution)/shard_map/right_side/pallas_call | solution.py:307
  15.4 2.8 %collective-permute-start.11 = (s16[544,128]{1,0:T(8,128)(2,1)}, s16[544,128]{1,0:T(8,128)(2,1)S(1)}, u32[]{:S(2)}, u32[]{:S(2)}) collective-permute-start(s16[544,128]{1,0:T(8,128)(2,1)} %get-tuple-element.50), channel_id=1, source_target_pairs={{0,12},{4,8},{8,4},{12,0},{16,28},{20,24},{24,20},{28,16},{1,13},{... | collective-permute-start | bytes 417800 | tf_op jit(solution)/shard_map/ppermute | solution.py:249
  18.2 1.6 %collective-permute-start.12 = (s16[544,128]{1,0:T(8,128)(2,1)}, s16[544,128]{1,0:T(8,128)(2,1)S(1)}, u32[]{:S(2)}, u32[]{:S(2)}) collective-permute-start(s16[544,128]{1,0:T(8,128)(2,1)} %get-tuple-element.51), channel_id=1, source_target_pairs={{0,24},{4,28},{8,16},{12,20},{16,8},{20,12},{24,0},{28,4},{1,25},{... | collective-permute-start | bytes 417800 | tf_op jit(solution)/shard_map/ppermute | solution.py:249
  19.8 8.0 %right_side.5 = (s16[544,128]{1,0:T(8,128)(2,1)}, s16[544,128]{1,0:T(8,128)(2,1)}, s16[544,128]{1,0:T(8,128)(2,1)}, s16[544,128]{1,0:T(8,128)(2,1)}, s16[544,128...) custom-call(s32[2]{0:T(128)} %pad_add_fusion.where, ...), custom_call_target="tpu_custom_call" | custom-call | flops 8388608 | bytes 8388608 | tf_op jit(solution)/shard_map/right_side/pallas_call | solution.py:307
  28.2 4.4 %collective-permute-start = (s16[544,128]{1,0:T(8,128)(2,1)}, s16[544,128]{1,0:T(8,128)(2,1)S(1)}, u32[]{:S(2)}, u32[]{:S(2)}) collective-permute-start(s16[544,128]{1,0:T(8,128)(2,1)} %get-tuple-element.39), channel_id=1, source_target_pairs={{0,16},{4,20},{8,24},{12,28},{16,0},{20,4},{24,8},{28,12},{1,17},{... | collective-permute-start | bytes 417800 | tf_op jit(solution)/shard_map/ppermute | solution.py:249
  34.1 3.4 %copy-done = f32[1,2,1024,1024]{3,2,1,0:T(8,128)S(1)} copy-done((f32[1,2,1024,1024]{3,2,1,0:T(8,128)S(1)}, f32[1,2,1024,1024]{3,2,1,0:T(8,128)}, u32[]{:S(2)}) %copy-start) | copy-done | bytes 8388632
  38.9 1.7 %collective-permute-start.3 = (s16[544,128]{1,0:T(8,128)(2,1)S(1)}, s16[544,128]{1,0:T(8,128)(2,1)S(1)}, u32[]{:S(2)}, u32[]{:S(2)}) collective-permute-start(s16[544,128]{1,0:T(8,128)(2,1)S(1)} %copy-done.9), channel_id=1, source_target_pairs={{0,20},{4,16},{8,28},{12,24},{16,4},{20,0},{24,12},{28,8},{1,21},{... | collective-permute-start | bytes 417800 | tf_op jit(solution)/shard_map/ppermute | solution.py:249
  43.4 1.7 %collective-permute-start.6 = (s16[544,128]{1,0:T(8,128)(2,1)S(1)}, s16[544,128]{1,0:T(8,128)(2,1)S(1)}, u32[]{:S(2)}, u32[]{:S(2)}) collective-permute-start(s16[544,128]{1,0:T(8,128)(2,1)S(1)} %copy-done.6), channel_id=1, source_target_pairs={{0,28},{4,24},{8,20},{12,16},{16,12},{20,8},{24,4},{28,0},{1,29},{... | collective-permute-start | bytes 417800 | tf_op jit(solution)/shard_map/ppermute | solution.py:249
  45.1 7.0 %product.2 = (s16[528,128]{1,0:T(8,128)(2,1)S(1)}, s16[528,128]{1,0:T(8,128)(2,1)S(1)}, s16[528,128]{1,0:T(8,128)(2,1)S(1)}, s16[528,128]{1,0:T(8,128)(2,1)S(1)}...) custom-call(s32[2]{0:T(128)S(1)} %copy-done.1, ...), custom_call_target="tpu_custom_call" | custom-call | flops 3221225472 | bytes 10485760 | tf_op jit(solution)/shard_map/product/pallas_call | solution.py:344
  52.1 5.1 %collective-permute-start.21 = (s16[528,128]{1,0:T(8,128)(2,1)S(1)}, s16[528,128]{1,0:T(8,128)(2,1)S(1)}, u32[]{:S(2)}, u32[]{:S(2)}) collective-permute-start(s16[528,128]{1,0:T(8,128)(2,1)S(1)} %get-tuple-element.62), channel_id=1, source_target_pairs={{0,16},{4,20},{8,24},{12,28},{16,0},{20,4},{24,8},{28,12},{1,17},{... | collective-permute-start | bytes 405512 | tf_op jit(solution)/shard_map/ppermute | solution.py:249
  58.8 3.8 %collective-permute-start.24 = (s16[528,128]{1,0:T(8,128)(2,1)S(1)}, s16[528,128]{1,0:T(8,128)(2,1)S(1)}, u32[]{:S(2)}, u32[]{:S(2)}) collective-permute-start(s16[528,128]{1,0:T(8,128)(2,1)S(1)} %get-tuple-element.65), channel_id=1, source_target_pairs={{0,20},{4,16},{8,28},{12,24},{16,4},{20,0},{24,12},{28,8},{1,21},{... | collective-permute-start | bytes 405512 | tf_op jit(solution)/shard_map/ppermute | solution.py:249
  62.7 5.0 %collective-permute-done.6.refs_6_ = s16[544,128]{1,0:T(8,128)(2,1)S(1)} collective-permute-done((s16[544,128]{1,0:T(8,128)(2,1)S(1)}, s16[544,128]{1,0:T(8,128)(2,1)S(1)}, u32[]{:S(2)}, u32[]{:S(2)}) %collective-permute-start.6) | collective-permute-done | bytes 139296 | tf_op jit(solution)/shard_map/ppermute | solution.py:249
  67.7 5.4 %product.3 = (s16[528,128]{1,0:T(8,128)(2,1)S(1)}, s16[528,128]{1,0:T(8,128)(2,1)S(1)}, s16[528,128]{1,0:T(8,128)(2,1)S(1)}, s16[528,128]{1,0:T(8,128)(2,1)S(1)}...) custom-call(s32[2]{0:T(128)S(1)} %copy-done.1, ...), custom_call_target="tpu_custom_call" | custom-call | flops 3221225472 | bytes 10485760 | tf_op jit(solution)/shard_map/product/pallas_call | solution.py:344
  73.3 6.1 %collective-permute-start.17 = (s16[528,128]{1,0:T(8,128)(2,1)S(1)}, s16[528,128]{1,0:T(8,128)(2,1)S(1)}, u32[]{:S(2)}, u32[]{:S(2)}) collective-permute-start(s16[528,128]{1,0:T(8,128)(2,1)S(1)} %get-tuple-element.57), channel_id=1, source_target_pairs={{0,16},{4,20},{8,24},{12,28},{16,0},{20,4},{24,8},{28,12},{1,17},{... | collective-permute-start | bytes 405512 | tf_op jit(solution)/shard_map/ppermute | solution.py:249
  80.1 7.7 %collective-permute-done.26.refs_5_ = s16[528,128]{1,0:T(8,128)(2,1)S(1)} collective-permute-done((s16[528,128]{1,0:T(8,128)(2,1)S(1)}, s16[528,128]{1,0:T(8,128)(2,1)S(1)}, u32[]{:S(2)}, u32[]{:S(2)}) %collective-permute-start.26) | collective-permute-done | bytes 135200 | tf_op jit(solution)/shard_map/ppermute | solution.py:249
  87.8 1.6 %collective-permute-done.27.refs_6_ = s16[528,128]{1,0:T(8,128)(2,1)S(1)} collective-permute-done((s16[528,128]{1,0:T(8,128)(2,1)S(1)}, s16[528,128]{1,0:T(8,128)(2,1)S(1)}, u32[]{:S(2)}, u32[]{:S(2)}) %collective-permute-start.27) | collective-permute-done | bytes 135200 | tf_op jit(solution)/shard_map/ppermute | solution.py:249
  89.7 2.6 %collective-permute-done.17.refs_0_ = s16[528,128]{1,0:T(8,128)(2,1)S(1)} collective-permute-done((s16[528,128]{1,0:T(8,128)(2,1)S(1)}, s16[528,128]{1,0:T(8,128)(2,1)S(1)}, u32[]{:S(2)}, u32[]{:S(2)}) %collective-permute-start.17) | collective-permute-done | bytes 135200 | tf_op jit(solution)/shard_map/ppermute | solution.py:249
  92.3 5.1 %collective-permute-start.15 = (s16[528,128]{1,0:T(8,128)(2,1)S(1)}, s16[528,128]{1,0:T(8,128)(2,1)S(1)}, u32[]{:S(2)}, u32[]{:S(2)}) collective-permute-start(s16[528,128]{1,0:T(8,128)(2,1)S(1)} %get-tuple-element.55), channel_id=1, source_target_pairs={{0,24},{4,28},{8,16},{12,20},{16,8},{20,12},{24,0},{28,4},{1,25},{... | collective-permute-start | bytes 405512 | tf_op jit(solution)/shard_map/ppermute | solution.py:249
  97.5 2.0 %result.3.refs_5_ = f32[2,64,8192]{2,1,0:T(8,128)} custom-call(s32[2]{0:T(128)S(1)} %copy-done.1, s16[528,128]{1,0:T(8,128)(2,1)S(1)} %collective-permute-done.21.refs_0_, s16[528,128]{1,0:T(8,128)(2,1)S(1)} %collective-permute-done.22.refs_1_, s16[528,128]{1,0:T(8,128)(2,1)S(1)} %collective-permute-done.23.refs_2_, ...), custom_call_target="tpu_custom_call" | custom-call | flops 1048576 | bytes 2097152 | tf_op jit(solution)/shard_map/result/pallas_call | solution.py:371
  99.5 1.7 %result.4.refs_3_ = f32[2,64,8192]{2,1,0:T(8,128)} custom-call(s32[2]{0:T(128)S(1)} %copy-done.1, s16[528,128]{1,0:T(8,128)(2,1)S(1)} %collective-permute-done.17.refs_0_, s16[528,128]{1,0:T(8,128)(2,1)S(1)} %collective-permute-done.18.refs_1_, s16[528,128]{1,0:T(8,128)(2,1)S(1)} %collective-permute-done.19.refs_2_, ...), custom_call_target="tpu_custom_call", output_to_operand_aliasing={{}: (6, {})} | custom-call | flops 1048576 | bytes 2097152 | tf_op jit(solution)/shard_map/result/pallas_call | solution.py:371
  101.2 2.4 %collective-permute-done.15.refs_1_ = s16[528,128]{1,0:T(8,128)(2,1)S(1)} collective-permute-done((s16[528,128]{1,0:T(8,128)(2,1)S(1)}, s16[528,128]{1,0:T(8,128)(2,1)S(1)}, u32[]{:S(2)}, u32[]{:S(2)}) %collective-permute-start.15) | collective-permute-done | bytes 135200 | tf_op jit(solution)/shard_map/ppermute | solution.py:249
  103.6 3.7 %collective-permute-done.16.refs_2_ = s16[528,128]{1,0:T(8,128)(2,1)S(1)} collective-permute-done((s16[528,128]{1,0:T(8,128)(2,1)S(1)}, s16[528,128]{1,0:T(8,128)(2,1)S(1)}, u32[]{:S(2)}, u32[]{:S(2)}) %collective-permute-start.16) | collective-permute-done | bytes 135200 | tf_op jit(solution)/shard_map/ppermute | solution.py:249
  (64 shorter events, 12.9 us)
Async XLA Ops:
  4.5 13.7 %collective-permute-start.7 = (s16[544,128]{1,0:T(8,128)(2,1)}, s16[544,128]{1,0:T(8,128)(2,1)S(1)}, u32[]{:S(2)}, u32[]{:S(2)}) collective-permute-start(s16[544,128]{1,0:T(8,128)(2,1)} %get-tuple-element.47), channel_id=1, source_target_pairs={{0,16},{4,20},{8,24},{12,28},{16,0},{20,4},{24,8},{28,12},{1,17},{... | collective-permute-start | bytes 417800 | tf_op jit(solution)/shard_map/ppermute | solution.py:249
  7.1 20.7 %collective-permute-start.10 = (s16[544,128]{1,0:T(8,128)(2,1)}, s16[544,128]{1,0:T(8,128)(2,1)S(1)}, u32[]{:S(2)}, u32[]{:S(2)}) collective-permute-start(s16[544,128]{1,0:T(8,128)(2,1)} %get-tuple-element.37.refs_0_), channel_id=1, source_target_pairs={{0,20},{4,16},{8,28},{12,24},{16,4},{20,0},{24,12},{28,8},{1,21},{... | collective-permute-start | bytes 417800 | tf_op jit(solution)/shard_map/ppermute | solution.py:249
  14.7 13.5 %collective-permute-start.8 = (s16[544,128]{1,0:T(8,128)(2,1)}, s16[544,128]{1,0:T(8,128)(2,1)S(1)}, u32[]{:S(2)}, u32[]{:S(2)}) collective-permute-start(s16[544,128]{1,0:T(8,128)(2,1)} %get-tuple-element.48), channel_id=1, source_target_pairs={{0,4},{4,0},{8,12},{12,8},{16,20},{20,16},{24,28},{28,24},{1,5},{5... | collective-permute-start | bytes 417800 | tf_op jit(solution)/shard_map/ppermute | solution.py:249
  15.2 17.4 %collective-permute-start.9 = (s16[544,128]{1,0:T(8,128)(2,1)}, s16[544,128]{1,0:T(8,128)(2,1)S(1)}, u32[]{:S(2)}, u32[]{:S(2)}) collective-permute-start(s16[544,128]{1,0:T(8,128)(2,1)} %get-tuple-element.49), channel_id=1, source_target_pairs={{0,8},{4,12},{8,0},{12,4},{16,24},{20,28},{24,16},{28,20},{1,9},{5... | collective-permute-start | bytes 417800 | tf_op jit(solution)/shard_map/ppermute | solution.py:249
  15.4 23.5 %collective-permute-start.11 = (s16[544,128]{1,0:T(8,128)(2,1)}, s16[544,128]{1,0:T(8,128)(2,1)S(1)}, u32[]{:S(2)}, u32[]{:S(2)}) collective-permute-start(s16[544,128]{1,0:T(8,128)(2,1)} %get-tuple-element.50), channel_id=1, source_target_pairs={{0,12},{4,8},{8,4},{12,0},{16,28},{20,24},{24,20},{28,16},{1,13},{... | collective-permute-start | bytes 417800 | tf_op jit(solution)/shard_map/ppermute | solution.py:249
  18.2 20.8 %collective-permute-start.12 = (s16[544,128]{1,0:T(8,128)(2,1)}, s16[544,128]{1,0:T(8,128)(2,1)S(1)}, u32[]{:S(2)}, u32[]{:S(2)}) collective-permute-start(s16[544,128]{1,0:T(8,128)(2,1)} %get-tuple-element.51), channel_id=1, source_target_pairs={{0,24},{4,28},{8,16},{12,20},{16,8},{20,12},{24,0},{28,4},{1,25},{... | collective-permute-start | bytes 417800 | tf_op jit(solution)/shard_map/ppermute | solution.py:249
  27.8 13.2 %collective-permute-start.13 = (s16[544,128]{1,0:T(8,128)(2,1)S(1)}, s16[544,128]{1,0:T(8,128)(2,1)S(1)}, u32[]{:S(2)}, u32[]{:S(2)}) collective-permute-start(s16[544,128]{1,0:T(8,128)(2,1)S(1)} %copy-done.5), channel_id=1, source_target_pairs={{0,28},{4,24},{8,20},{12,16},{16,12},{20,8},{24,4},{28,0},{1,29},{... | collective-permute-start | bytes 417800 | tf_op jit(solution)/shard_map/ppermute | solution.py:249
  28.2 14.4 %collective-permute-start = (s16[544,128]{1,0:T(8,128)(2,1)}, s16[544,128]{1,0:T(8,128)(2,1)S(1)}, u32[]{:S(2)}, u32[]{:S(2)}) collective-permute-start(s16[544,128]{1,0:T(8,128)(2,1)} %get-tuple-element.39), channel_id=1, source_target_pairs={{0,16},{4,20},{8,24},{12,28},{16,0},{20,4},{24,8},{28,12},{1,17},{... | collective-permute-start | bytes 417800 | tf_op jit(solution)/shard_map/ppermute | solution.py:249
  38.8 13.3 %collective-permute-start.2 = (s16[544,128]{1,0:T(8,128)(2,1)S(1)}, s16[544,128]{1,0:T(8,128)(2,1)S(1)}, u32[]{:S(2)}, u32[]{:S(2)}) collective-permute-start(s16[544,128]{1,0:T(8,128)(2,1)S(1)} %copy-done.10), channel_id=1, source_target_pairs={{0,8},{4,12},{8,0},{12,4},{16,24},{20,28},{24,16},{28,20},{1,9},{5... | collective-permute-start | bytes 417800 | tf_op jit(solution)/shard_map/ppermute | solution.py:249
  38.9 18.3 %collective-permute-start.3 = (s16[544,128]{1,0:T(8,128)(2,1)S(1)}, s16[544,128]{1,0:T(8,128)(2,1)S(1)}, u32[]{:S(2)}, u32[]{:S(2)}) collective-permute-start(s16[544,128]{1,0:T(8,128)(2,1)S(1)} %copy-done.9), channel_id=1, source_target_pairs={{0,20},{4,16},{8,28},{12,24},{16,4},{20,0},{24,12},{28,8},{1,21},{... | collective-permute-start | bytes 417800 | tf_op jit(solution)/shard_map/ppermute | solution.py:249
  40.9 17.4 %collective-permute-start.4 = (s16[544,128]{1,0:T(8,128)(2,1)S(1)}, s16[544,128]{1,0:T(8,128)(2,1)S(1)}, u32[]{:S(2)}, u32[]{:S(2)}) collective-permute-start(s16[544,128]{1,0:T(8,128)(2,1)S(1)} %copy-done.8), channel_id=1, source_target_pairs={{0,12},{4,8},{8,4},{12,0},{16,28},{20,24},{24,20},{28,16},{1,13},{... | collective-permute-start | bytes 417800 | tf_op jit(solution)/shard_map/ppermute | solution.py:249
  42.6 16.2 %collective-permute-start.5 = (s16[544,128]{1,0:T(8,128)(2,1)S(1)}, s16[544,128]{1,0:T(8,128)(2,1)S(1)}, u32[]{:S(2)}, u32[]{:S(2)}) collective-permute-start(s16[544,128]{1,0:T(8,128)(2,1)S(1)} %copy-done.7), channel_id=1, source_target_pairs={{0,24},{4,28},{8,16},{12,20},{16,8},{20,12},{24,0},{28,4},{1,25},{... | collective-permute-start | bytes 417800 | tf_op jit(solution)/shard_map/ppermute | solution.py:249
  43.4 24.2 %collective-permute-start.6 = (s16[544,128]{1,0:T(8,128)(2,1)S(1)}, s16[544,128]{1,0:T(8,128)(2,1)S(1)}, u32[]{:S(2)}, u32[]{:S(2)}) collective-permute-start(s16[544,128]{1,0:T(8,128)(2,1)S(1)} %copy-done.6), channel_id=1, source_target_pairs={{0,28},{4,24},{8,20},{12,16},{16,12},{20,8},{24,4},{28,0},{1,29},{... | collective-permute-start | bytes 417800 | tf_op jit(solution)/shard_map/ppermute | solution.py:249
  52.1 21.0 %collective-permute-start.21 = (s16[528,128]{1,0:T(8,128)(2,1)S(1)}, s16[528,128]{1,0:T(8,128)(2,1)S(1)}, u32[]{:S(2)}, u32[]{:S(2)}) collective-permute-start(s16[528,128]{1,0:T(8,128)(2,1)S(1)} %get-tuple-element.62), channel_id=1, source_target_pairs={{0,16},{4,20},{8,24},{12,28},{16,0},{20,4},{24,8},{28,12},{1,17},{... | collective-permute-start | bytes 405512 | tf_op jit(solution)/shard_map/ppermute | solution.py:249
  57.3 16.0 %collective-permute-start.22 = (s16[528,128]{1,0:T(8,128)(2,1)S(1)}, s16[528,128]{1,0:T(8,128)(2,1)S(1)}, u32[]{:S(2)}, u32[]{:S(2)}) collective-permute-start(s16[528,128]{1,0:T(8,128)(2,1)S(1)} %get-tuple-element.63), channel_id=1, source_target_pairs={{0,4},{4,0},{8,12},{12,8},{16,20},{20,16},{24,28},{28,24},{1,5},{5... | collective-permute-start | bytes 405512 | tf_op jit(solution)/shard_map/ppermute | solution.py:249
  58.4 14.9 %collective-permute-start.23 = (s16[528,128]{1,0:T(8,128)(2,1)S(1)}, s16[528,128]{1,0:T(8,128)(2,1)S(1)}, u32[]{:S(2)}, u32[]{:S(2)}) collective-permute-start(s16[528,128]{1,0:T(8,128)(2,1)S(1)} %get-tuple-element.64), channel_id=1, source_target_pairs={{0,8},{4,12},{8,0},{12,4},{16,24},{20,28},{24,16},{28,20},{1,9},{5... | collective-permute-start | bytes 405512 | tf_op jit(solution)/shard_map/ppermute | solution.py:249
  58.8 20.6 %collective-permute-start.24 = (s16[528,128]{1,0:T(8,128)(2,1)S(1)}, s16[528,128]{1,0:T(8,128)(2,1)S(1)}, u32[]{:S(2)}, u32[]{:S(2)}) collective-permute-start(s16[528,128]{1,0:T(8,128)(2,1)S(1)} %get-tuple-element.65), channel_id=1, source_target_pairs={{0,20},{4,16},{8,28},{12,24},{16,4},{20,0},{24,12},{28,8},{1,21},{... | collective-permute-start | bytes 405512 | tf_op jit(solution)/shard_map/ppermute | solution.py:249
  67.7 11.8 %collective-permute-start.25 = (s16[528,128]{1,0:T(8,128)(2,1)S(1)}, s16[528,128]{1,0:T(8,128)(2,1)S(1)}, u32[]{:S(2)}, u32[]{:S(2)}) collective-permute-start(s16[528,128]{1,0:T(8,128)(2,1)S(1)} %get-tuple-element.66), channel_id=1, source_target_pairs={{0,12},{4,8},{8,4},{12,0},{16,28},{20,24},{24,20},{28,16},{1,13},{... | collective-permute-start | bytes 405512 | tf_op jit(solution)/shard_map/ppermute | solution.py:249
  73.1 14.7 %collective-permute-start.26 = (s16[528,128]{1,0:T(8,128)(2,1)S(1)}, s16[528,128]{1,0:T(8,128)(2,1)S(1)}, u32[]{:S(2)}, u32[]{:S(2)}) collective-permute-start(s16[528,128]{1,0:T(8,128)(2,1)S(1)} %get-tuple-element.67), channel_id=1, source_target_pairs={{0,24},{4,28},{8,16},{12,20},{16,8},{20,12},{24,0},{28,4},{1,25},{... | collective-permute-start | bytes 405512 | tf_op jit(solution)/shard_map/ppermute | solution.py:249
  73.2 16.2 %collective-permute-start.27 = (s16[528,128]{1,0:T(8,128)(2,1)S(1)}, s16[528,128]{1,0:T(8,128)(2,1)S(1)}, u32[]{:S(2)}, u32[]{:S(2)}) collective-permute-start(s16[528,128]{1,0:T(8,128)(2,1)S(1)} %get-tuple-element.68), channel_id=1, source_target_pairs={{0,28},{4,24},{8,20},{12,16},{16,12},{20,8},{24,4},{28,0},{1,29},{... | collective-permute-start | bytes 405512 | tf_op jit(solution)/shard_map/ppermute | solution.py:249
  73.3 19.0 %collective-permute-start.17 = (s16[528,128]{1,0:T(8,128)(2,1)S(1)}, s16[528,128]{1,0:T(8,128)(2,1)S(1)}, u32[]{:S(2)}, u32[]{:S(2)}) collective-permute-start(s16[528,128]{1,0:T(8,128)(2,1)S(1)} %get-tuple-element.57), channel_id=1, source_target_pairs={{0,16},{4,20},{8,24},{12,28},{16,0},{20,4},{24,8},{28,12},{1,17},{... | collective-permute-start | bytes 405512 | tf_op jit(solution)/shard_map/ppermute | solution.py:249
  79.4 18.1 %collective-permute-start.18 = (s16[528,128]{1,0:T(8,128)(2,1)S(1)}, s16[528,128]{1,0:T(8,128)(2,1)S(1)}, u32[]{:S(2)}, u32[]{:S(2)}) collective-permute-start(s16[528,128]{1,0:T(8,128)(2,1)S(1)} %get-tuple-element.58), channel_id=1, source_target_pairs={{0,4},{4,0},{8,12},{12,8},{16,20},{20,16},{24,28},{28,24},{1,5},{5... | collective-permute-start | bytes 405512 | tf_op jit(solution)/shard_map/ppermute | solution.py:249
  79.4 20.1 %collective-permute-start.19 = (s16[528,128]{1,0:T(8,128)(2,1)S(1)}, s16[528,128]{1,0:T(8,128)(2,1)S(1)}, u32[]{:S(2)}, u32[]{:S(2)}) collective-permute-start(s16[528,128]{1,0:T(8,128)(2,1)S(1)} %get-tuple-element.59), channel_id=1, source_target_pairs={{0,8},{4,12},{8,0},{12,4},{16,24},{20,28},{24,16},{28,20},{1,9},{5... | collective-permute-start | bytes 405512 | tf_op jit(solution)/shard_map/ppermute | solution.py:249
  89.4 11.8 %collective-permute-start.14 = (s16[528,128]{1,0:T(8,128)(2,1)S(1)}, s16[528,128]{1,0:T(8,128)(2,1)S(1)}, u32[]{:S(2)}, u32[]{:S(2)}) collective-permute-start(s16[528,128]{1,0:T(8,128)(2,1)S(1)} %get-tuple-element.54), channel_id=1, source_target_pairs={{0,12},{4,8},{8,4},{12,0},{16,28},{20,24},{24,20},{28,16},{1,13},{... | collective-permute-start | bytes 405512 | tf_op jit(solution)/shard_map/ppermute | solution.py:249
  (15 other events, 117.4 us)

commit v5 on v4

--- a/solution.py
+++ b/solution.py
@@ -72,57 +72,85 @@
     return pl.ds(pl.multiple_of(slab * LANES, LANES), LANES)
 
 
-def right_side_kernel(slabs, partners, where, n_low, n_high, s_low, s_high, tab_ref, *refs):
-    outs, (buffer, values, tops, extra) = refs[-4 - partners : -4], refs[-4:]
-    levels = n_low.shape[1]
+def right_side_kernel(ks, slabs, skipped, width, nonlin, state, table, *refs):
+    count = len(ks)
+    outs, (n_buf, s_buf, tab_buf, messages, values, tops, extra, sems, out_sems) = refs[-9 - count : -9], refs[-9:]
+    levels = nonlin.shape[1]
     rows = 2 * levels
-    tab = tab_ref[...]
+    span = slabs // 2 * LANES
+    me = lax.axis_index("rad")
+
+    def fetches(at, first):
+        made = []
+        for half in range(2):
+            cols = pl.ds(pl.multiple_of(first + half * (width // 2), LANES), span)
+            made.append(pltpu.make_async_copy(nonlin.at[:, :, cols], n_buf.at[at, half], sems.at[at, half, 0]))
+            made.append(pltpu.make_async_copy(state.at[:, :, cols], s_buf.at[at, half], sems.at[at, half, 1]))
+        return made
+
+    here_rows = pl.ds(pl.multiple_of(me * levels, levels), levels)
+    tab_copy = pltpu.make_async_copy(table.at[here_rows, :], tab_buf, out_sems.at[count])
+    tab_copy.start()
+    for at, k in enumerate(ks):
+        for copy in fetches(at, lax.bitwise_xor(me, k) * width + skipped):
+            copy.start()
+    tab_copy.wait()
+    tab = tab_buf[...]
     below, here, above = (jnp.broadcast_to(tab[:, i : i + 1], (levels, LANES)) for i in range(3))
     row = lax.broadcasted_iota(jnp.int32, (levels, LANES), 0)
 
     def rows_of(slab):
         return pl.ds(pl.multiple_of(slab * rows, rows), rows)
 
-    def compute(pair, _):
-        cols = lanes_of(pair)
-        for half, (n_ref, s_ref) in enumerate(((n_low, s_low), (n_high, s_high))):
-            slab = pair * 2 + half
-            ends, top = [], jnp.zeros((8, LANES), jnp.float32)
-            for f in range(2):
-                n = n_ref[f, :, cols].astype(jnp.float32)
-                prev = jnp.where(row == 0, n, pltpu.roll(n, 1, 0))
-                succ = jnp.where(row == levels - 1, n, pltpu.roll(n, levels - 1, 0))
-                v = s_ref[f, :, cols] + (below * prev + here * n + above * succ)
-                values[pl.ds(pl.multiple_of(slab * rows + f * levels, levels), levels), :] = v
-                top = jnp.maximum(top, jnp.max(jnp.abs(v).reshape(levels // 8, 8, LANES), axis=0))
-                ends += [n[:1], n[levels - 1 :]]
-            tops[slab] = top
-            extra[slab] = jnp.concatenate(ends + [jnp.zeros((4, LANES), jnp.float32)], axis=0)
+    def one_partner(at, _):
+        for copy in fetches(at, 0):
+            copy.wait()
+
+        def compute(pair, _):
+            cols = lanes_of(pair)
+            for half in range(2):
+                slab = pair * 2 + half
+                ends, top = [], jnp.zeros((8, LANES), jnp.float32)
+                for f in range(2):
+                    n = n_buf[at, half, f, :, cols].astype(jnp.float32)
+                    prev = jnp.where(row == 0, n, pltpu.roll(n, 1, 0))
+                    succ = jnp.where(row == levels - 1, n, pltpu.roll(n, levels - 1, 0))
+                    v = s_buf[at, half, f, :, cols] + (below * prev + here * n + above * succ)
+                    values[pl.ds(pl.multiple_of(slab * rows + f * levels, levels), levels), :] = v
+                    top = jnp.maximum(top, jnp.max(jnp.abs(v).reshape(levels // 8, 8, LANES), axis=0))
+                    ends += [n[:1], n[levels - 1 :]]
+                tops[slab] = top
+                extra[slab] = jnp.concatenate(ends + [jnp.zeros((4, LANES), jnp.float32)], axis=0)
+            return 0
+
+        lax.fori_loop(0, slabs // 2, compute, 0)
+        ends = extra[...]
+        code = scale_code(jnp.max(tops[...], axis=1), FINE)
+        factor = encode_factor(code, TOP)
+        edge_code = scale_code(jnp.max(jnp.abs(ends), axis=1), 1.0)
+        edge_factor = encode_factor(edge_code, EDGE_TOP)
+        at_row = lax.broadcasted_iota(jnp.int32, ends.shape, 1)
+        ends = jnp.round(ends * edge_factor[:, None, :])
+        ends = jnp.where(at_row == 4, edge_code[:, None, :], jnp.where(at_row == 5, code[:, None, :], ends))
+        messages[at, slabs * rows :, :] = to_int16(ends.reshape(slabs * EXTRA, LANES))
+        tops[:, 0, :] = factor
+
+        def code_slab(slab, _):
+            messages[at, rows_of(slab), :] = to_int16(jnp.round(values[rows_of(slab), :] * tops[slab, 0:1, :]))
+            return 0
+
+        lax.fori_loop(0, slabs, code_slab, 0, unroll=2)
+        for i, out in enumerate(outs):
+
+            @pl.when(at == i)
+            def _():
+                pltpu.make_async_copy(messages.at[i], out, out_sems.at[i]).start()
+
         return 0
 
-    lax.fori_loop(0, slabs // 2, compute, 0)
-    ends = extra[...]
-    code = scale_code(jnp.max(tops[...], axis=1), FINE)
-    factor = encode_factor(code, TOP)
-    edge_code = scale_code(jnp.max(jnp.abs(ends), axis=1), 1.0)
-    edge_factor = encode_factor(edge_code, EDGE_TOP)
-    at_row = lax.broadcasted_iota(jnp.int32, ends.shape, 1)
-    ends = jnp.round(ends * edge_factor[:, None, :])
-    ends = jnp.where(at_row == 4, edge_code[:, None, :], jnp.where(at_row == 5, code[:, None, :], ends))
-    buffer[slabs * rows :, :] = to_int16(ends.reshape(slabs * EXTRA, LANES))
-    tops[:, 0, :] = factor
-
-    def code_slab(slab, _):
-        buffer[rows_of(slab), :] = to_int16(jnp.round(values[rows_of(slab), :] * tops[slab, 0:1, :]))
-        return 0
-
-    lax.fori_loop(0, slabs, code_slab, 0, unroll=2)
-    step = pl.program_id(0)
-    for at, out in enumerate(outs):
-
-        @pl.when(step == at)
-        def _():
-            out[...] = buffer[...]
+    lax.fori_loop(0, count, one_partner, 0)
+    for i, out in enumerate(outs):
+        pltpu.make_async_copy(messages.at[i], out, out_sems.at[i]).wait()
 
 
 def split_kernel(a_ref, both_ref):
@@ -137,15 +165,15 @@
     return jnp.concatenate([edges[1:2], edges[0:1], edges[3:4], edges[2:3]], axis=0)
 
 
-def product_kernel(order, first_slab, slabs, lower_slabs, where, edge_weight, *refs):
+def product_kernel(order, first_slab, slabs, lower_slabs, pair_ref, edge_weight, *refs):
     groups = len(order)
     ins, both_ref = refs[:groups], refs[groups]
     outs, scratch, all_codes = refs[-groups - 9 : -9], refs[-9:-1], refs[-1]
     size = both_ref.shape[1]
     levels = size // (2 * groups)
     rows = 2 * levels
-    me = where[0]
-    pair = where[1]
+    me = lax.axis_index("rad")
+    pair = pair_ref[0]
     peers = [lax.bitwise_xor(me, k) for k in order]
     near = lax.broadcasted_iota(jnp.int32, (8, LANES), 0)
 
@@ -221,7 +249,7 @@
         out[slabs * rows :, :] = to_int16(all_codes[i])
 
 
-def result_kernel(ks, slabs, skipped, width, where, *refs):
+def result_kernel(ks, slabs, skipped, width, *refs):
     count = len(ks)
     ins, (out_ref, buffer, sems) = refs[:count], refs[-3:]
     levels = out_ref.shape[1]
@@ -230,7 +258,7 @@
     copies = []
     for at, (message, k) in enumerate(zip(ins, ks)):
         scales = scale_of(to_float(message[slabs * rows :, :]), TOP)
-        first_col = lax.bitwise_xor(where[0], k) * width + skipped
+        first_col = lax.bitwise_xor(lax.axis_index("rad"), k) * width + skipped
         for half in range(2):
             for pair in range(slabs // 2):
                 slab = pair * 2 + half
@@ -249,20 +277,6 @@
     return message if k == 0 else lax.ppermute(message, "rad", [(i, i ^ k) for i in range(groups)])
 
 
-def columns_of(ks, width, first):
-    def at(step, w):
-        k = jnp.int32(ks[-1])
-        for i, value in enumerate(ks[:-1]):
-            k = jnp.where(step == i, value, k)
-        return (0, 0, pl.multiple_of(lax.bitwise_xor(w[0], k) * width + first, LANES))
-
-    return at
-
-
-def columns_block(levels, count, index_map):
-    return pl.BlockSpec((pl.Element(2), pl.Element(levels), pl.Element(count)), index_map)
-
-
 def local(slots, nonlin, state, inverse, pair_of_slot):
     levels = nonlin.shape[1]
     groups = lax.axis_size("rad")
@@ -274,8 +288,6 @@
     slabs = 2 * span // LANES
     rows = 2 * levels
     lower_slabs = -(-slots // LANES)
-    me = lax.axis_index("rad").astype(jnp.int32)
-    where = jnp.stack([me, pair_of_slot[0].astype(jnp.int32)])
     weights = stencil_table(levels * groups)
     table = jnp.asarray(weights)
     edge_weight = jnp.asarray(np.concatenate([weights[::levels, 0], weights[levels - 1 :: levels, 2]]))
@@ -299,32 +311,29 @@
         )
 
     def right_side(ks, chunk, *earlier):
-        low, high = (
-            columns_block(levels, span, columns_of(ks, width, first))
-            for first in (chunk * span, half_cols + chunk * span)
-        )
         out_rows = slabs * (rows + EXTRA)
+        count = len(ks)
         return call(
-            functools.partial(right_side_kernel, slabs, len(ks)),
+            functools.partial(right_side_kernel, ks, slabs, chunk * span, width),
             "right_side",
-            MIB * len(ks),
-            MIB * len(ks),
+            MIB * count,
+            MIB * count,
             56,
-            out_shape=[jax.ShapeDtypeStruct((out_rows, LANES), jnp.int16)] * len(ks),
-            grid_spec=pltpu.PrefetchScalarGridSpec(
-                num_scalar_prefetch=1,
-                grid=(len(ks),),
-                in_specs=[low, high, low, high, pl.BlockSpec((levels, LANES), lambda k, w: (w[0], 0))]
-                + [hbm for _ in earlier],
-                out_specs=[pl.BlockSpec((out_rows, LANES), lambda k, w: (0, 0))] * len(ks),
-                scratch_shapes=[
-                    pltpu.VMEM((out_rows, LANES), jnp.int16),
-                    pltpu.VMEM((slabs * rows, LANES), jnp.float32),
-                    pltpu.VMEM((slabs, 8, LANES), jnp.float32),
-                    pltpu.VMEM((slabs, EXTRA, LANES), jnp.float32),
-                ],
-            ),
-        )(where, nonlin, nonlin, state, state, table, *earlier)
+            out_shape=[jax.ShapeDtypeStruct((out_rows, LANES), jnp.int16)] * count,
+            in_specs=[hbm] * (3 + len(earlier)),
+            out_specs=[hbm] * count,
+            scratch_shapes=[
+                pltpu.VMEM((count, 2, 2, levels, span), jnp.bfloat16),
+                pltpu.VMEM((count, 2, 2, levels, span), jnp.float32),
+                pltpu.VMEM((levels, LANES), jnp.float32),
+                pltpu.VMEM((count, out_rows, LANES), jnp.int16),
+                pltpu.VMEM((slabs * rows, LANES), jnp.float32),
+                pltpu.VMEM((slabs, 8, LANES), jnp.float32),
+                pltpu.VMEM((slabs, EXTRA, LANES), jnp.float32),
+                pltpu.SemaphoreType.DMA((count, 2, 2)),
+                pltpu.SemaphoreType.DMA((count + 1,)),
+            ],
+        )(nonlin, state, table, *earlier)
 
     def split():
         block = pl.BlockSpec((1, size // 4, size), lambda i, j: (i, j, 0))
@@ -348,23 +357,19 @@
             10 * MIB,
             32,
             out_shape=[jax.ShapeDtypeStruct((slabs * rows + TILE, LANES), jnp.int16)] * groups,
-            grid_spec=pltpu.PrefetchScalarGridSpec(
-                num_scalar_prefetch=1,
-                grid=(),
-                in_specs=[pl.BlockSpec(memory_space=pltpu.SMEM)]
-                + [vmem] * (groups + 1)
-                + [hbm for _ in earlier],
-                out_specs=[vmem] * groups,
-                scratch_shapes=2
-                * [
-                    pltpu.VMEM((2 * size, 2 * LANES), jnp.bfloat16),
-                    pltpu.VMEM((size, 2 * LANES), jnp.float32),
-                    pltpu.VMEM((groups, 4, 2 * LANES), jnp.float32),
-                    pltpu.VMEM((2, groups, 8, LANES), jnp.float32),
-                ]
-                + [pltpu.VMEM((groups, TILE, LANES), jnp.float32)],
-            ),
-        )(where, edge_weight, *messages, both, *earlier)
+            in_specs=[pl.BlockSpec(memory_space=pltpu.SMEM)] * 2
+            + [vmem] * (groups + 1)
+            + [hbm for _ in earlier],
+            out_specs=[vmem] * groups,
+            scratch_shapes=2
+            * [
+                pltpu.VMEM((2 * size, 2 * LANES), jnp.bfloat16),
+                pltpu.VMEM((size, 2 * LANES), jnp.float32),
+                pltpu.VMEM((groups, 4, 2 * LANES), jnp.float32),
+                pltpu.VMEM((2, groups, 8, LANES), jnp.float32),
+            ]
+            + [pltpu.VMEM((groups, TILE, LANES), jnp.float32)],
+        )(pair_of_slot, edge_weight, *messages, both, *earlier)
 
     def result(ks, chunk, messages, previous):
         carried = [] if previous is None else [previous]
@@ -375,18 +380,14 @@
             2 * MIB,
             16,
             out_shape=jax.ShapeDtypeStruct(state.shape, jnp.float32),
-            grid_spec=pltpu.PrefetchScalarGridSpec(
-                num_scalar_prefetch=1,
-                grid=(),
-                in_specs=[vmem] * len(messages) + [hbm] * len(carried),
-                out_specs=hbm,
-                scratch_shapes=[
-                    pltpu.VMEM((len(ks), 2, 2, levels, span), jnp.float32),
-                    pltpu.SemaphoreType.DMA((len(ks), 2)),
-                ],
-            ),
-            input_output_aliases={} if previous is None else {len(ks) + 1: 0},
-        )(where, *messages, *carried)
+            in_specs=[vmem] * len(messages) + [hbm] * len(carried),
+            out_specs=hbm,
+            scratch_shapes=[
+                pltpu.VMEM((len(ks), 2, 2, levels, span), jnp.float32),
+                pltpu.SemaphoreType.DMA((len(ks), 2)),
+            ],
+            input_output_aliases={} if previous is None else {len(ks): 0},
+        )(*messages, *carried)
 
     made, got = [], {}
     for ks, chunk in ((far[:2], 0), (near + far[2:], 0), (far + near, 1)):

time: 110 us -> 103 us (0.936)
  Pallas kernels: 36.3 us -> 27 us
  starting transfers between devices: 43.2 us -> 45.1 us
    pallas_call x3, Pallas kernels: 17.5 us -> 10.9 us  [right_side(): call(functools.partial(right_side_kernel, ks, slabs, chunk * span, width)...]
    ppermute x28, starting transfers between devices: 43.2 us -> 45.1 us  [send(): lax.ppermute(message, 'rad', [(i, i ^ k) for i in range(groups)])]
    pallas_call x3, Pallas kernels: 5.17 us -> 3.55 us  [result(): call(functools.partial(result_kernel, ks, slabs, chunk * span, width), 'r...]
    unnamed x22 -> x20, local copies, waits for them, and re-layouts: 3.42 us -> 3.41 us
  transfers between devices with their start and end apart: 28 -> 28, of which waited for: 9 -> 8; matrix products, arithmetic and copies ran while one was open for 0% -> 0% of each run, Pallas kernels for 29% -> 23%
where the time goes in v5:
time: 103 us; the launch traced here: 102 us
  starting transfers between devices  45.1 us (44%)
  Pallas kernels  27 us (26%)
  waiting for transfers between devices  25.2 us (24%)
  local copies, waits for them, and re-layouts  3.41 us (3%)
    ppermute x28, starting transfers between devices, send(): lax.ppermute(message, 'rad', [(i, i ^ k) for i in range(groups)])  45.1 us
    ppermute x28, waiting for transfers between devices, send(): lax.ppermute(message, 'rad', [(i, i ^ k) for i in range(groups)])  25.2 us
    pallas_call x2, Pallas kernels, product(): call(functools.partial(product_kernel, order, chunk * span // LANES, slab...  11.3 us
    pallas_call x3, Pallas kernels, right_side(): call(functools.partial(right_side_kernel, ks, slabs, chunk * span, width)...  10.9 us
    pallas_call x3, Pallas kernels, result(): call(functools.partial(result_kernel, ks, slabs, chunk * span, width), 'r...  3.55 us
    unnamed x20, local copies, waits for them, and re-layouts  3.41 us
  transfers between devices with their start and end apart: 28, of which 8 were waited for; matrix products, arithmetic and copies ran while one was open for 0% of the time, Pallas kernels for 23%

profile of v5, /device:TPU:8, one launch (start us, length us, event | category | flops | bytes accessed | tf_op | source)
XLA Modules:
  0.0 101.6 jit_solution(16012291640251801596)
XLA Ops:
  0.0 2.3 %right_side.3 = (s16[544,128]{1,0:T(8,128)(2,1)}, s16[544,128]{1,0:T(8,128)(2,1)}) custom-call(bf16[2,64,8192]{2,1,0:T(8,128)(2,1)} %nonlin.5, f32[2,64,8192]{2,1,0:T(8,128)} %state.5, f32[512,128]{1,0:T(8,128)} %constant.4.clone.table), custom_call_target="tpu_custom_call" | custom-call | flops 2097152 | bytes 2097152 | tf_op jit(solution)/shard_map/right_side/pallas_call | solution.py:316
  2.3 2.7 %collective-permute-start.7 = (s16[544,128]{1,0:T(8,128)(2,1)}, s16[544,128]{1,0:T(8,128)(2,1)S(1)}, u32[]{:S(2)}, u32[]{:S(2)}) collective-permute-start(s16[544,128]{1,0:T(8,128)(2,1)} %get-tuple-element.47), channel_id=1, source_target_pairs={{0,16},{4,20},{8,24},{12,28},{16,0},{20,4},{24,8},{28,12},{1,17},{... | collective-permute-start | bytes 417800 | tf_op jit(solution)/shard_map/ppermute | solution.py:277
  6.3 3.9 %right_side.4 = (s16[544,128]{1,0:T(8,128)(2,1)}, s16[544,128]{1,0:T(8,128)(2,1)}, s16[544,128]{1,0:T(8,128)(2,1)}, s16[544,128]{1,0:T(8,128)(2,1)}, s16[544,128]{1,0:T(8,128)(2,1)}, /*index=5*/s16[544,128]{1,0:T(8,128)(2,1)}) custom-call(bf16[2,64,8192]{2,1,0:T(8,128)(2,1)} %nonlin.5, f32[2,64,8192]{2,1,0:T(8,128)} %state.5, ...), custom_call_target="tpu_custom_call" | custom-call | flops 6291456 | bytes 6291456 | tf_op jit(solution)/shard_map/right_side/pallas_call | solution.py:316
  11.0 2.8 %collective-permute-start.11 = (s16[544,128]{1,0:T(8,128)(2,1)}, s16[544,128]{1,0:T(8,128)(2,1)S(1)}, u32[]{:S(2)}, u32[]{:S(2)}) collective-permute-start(s16[544,128]{1,0:T(8,128)(2,1)} %get-tuple-element.50), channel_id=1, source_target_pairs={{0,12},{4,8},{8,4},{12,0},{16,28},{20,24},{24,20},{28,16},{1,13},{... | collective-permute-start | bytes 417800 | tf_op jit(solution)/shard_map/ppermute | solution.py:277
  15.3 4.7 %right_side.5 = (s16[544,128]{1,0:T(8,128)(2,1)}, s16[544,128]{1,0:T(8,128)(2,1)}, s16[544,128]{1,0:T(8,128)(2,1)}, s16[544,128]{1,0:T(8,128)(2,1)}, s16[544,128...) custom-call(bf16[2,64,8192]{2,1,0:T(8,128)(2,1)} %nonlin.5, ...), custom_call_target="tpu_custom_call" | custom-call | flops 8388608 | bytes 8388608 | tf_op jit(solution)/shard_map/right_side/pallas_call | solution.py:316
  20.0 2.0 %collective-permute-start.13 = (s16[544,128]{1,0:T(8,128)(2,1)S(1)}, s16[544,128]{1,0:T(8,128)(2,1)S(1)}, u32[]{:S(2)}, u32[]{:S(2)}) collective-permute-start(s16[544,128]{1,0:T(8,128)(2,1)S(1)} %copy-done.4), channel_id=1, source_target_pairs={{0,28},{4,24},{8,20},{12,16},{16,12},{20,8},{24,4},{28,0},{1,29},{... | collective-permute-start | bytes 417800 | tf_op jit(solution)/shard_map/ppermute | solution.py:277
  22.0 5.1 %collective-permute-start = (s16[544,128]{1,0:T(8,128)(2,1)}, s16[544,128]{1,0:T(8,128)(2,1)S(1)}, u32[]{:S(2)}, u32[]{:S(2)}) collective-permute-start(s16[544,128]{1,0:T(8,128)(2,1)} %get-tuple-element.39), channel_id=1, source_target_pairs={{0,16},{4,20},{8,24},{12,28},{16,0},{20,4},{24,8},{28,12},{1,17},{... | collective-permute-start | bytes 417800 | tf_op jit(solution)/shard_map/ppermute | solution.py:277
  28.3 3.4 %copy-done = f32[1,2,1024,1024]{3,2,1,0:T(8,128)S(1)} copy-done((f32[1,2,1024,1024]{3,2,1,0:T(8,128)S(1)}, f32[1,2,1024,1024]{3,2,1,0:T(8,128)}, u32[]{:S(2)}) %copy-start) | copy-done | bytes 8388632
  33.1 2.9 %collective-permute-start.3 = (s16[544,128]{1,0:T(8,128)(2,1)S(1)}, s16[544,128]{1,0:T(8,128)(2,1)S(1)}, u32[]{:S(2)}, u32[]{:S(2)}) collective-permute-start(s16[544,128]{1,0:T(8,128)(2,1)S(1)} %copy-done.8), channel_id=1, source_target_pairs={{0,20},{4,16},{8,28},{12,24},{16,4},{20,0},{24,12},{28,8},{1,21},{... | collective-permute-start | bytes 417800 | tf_op jit(solution)/shard_map/ppermute | solution.py:277
  37.6 1.4 %collective-permute-start.6 = (s16[544,128]{1,0:T(8,128)(2,1)S(1)}, s16[544,128]{1,0:T(8,128)(2,1)S(1)}, u32[]{:S(2)}, u32[]{:S(2)}) collective-permute-start(s16[544,128]{1,0:T(8,128)(2,1)S(1)} %copy-done.5), channel_id=1, source_target_pairs={{0,28},{4,24},{8,20},{12,16},{16,12},{20,8},{24,4},{28,0},{1,29},{... | collective-permute-start | bytes 417800 | tf_op jit(solution)/shard_map/ppermute | solution.py:277
  39.1 6.5 %product.2 = (s16[528,128]{1,0:T(8,128)(2,1)S(1)}, s16[528,128]{1,0:T(8,128)(2,1)S(1)}, s16[528,128]{1,0:T(8,128)(2,1)S(1)}, s16[528,128]{1,0:T(8,128)(2,1)S(1)}...) custom-call(s32[1]{0:T(128)S(6)} %copy.11.pair_ref, ...), custom_call_target="tpu_custom_call" | custom-call | flops 3221225472 | bytes 10485760 | tf_op jit(solution)/shard_map/product/pallas_call | solution.py:353
  45.5 5.4 %collective-permute-start.21 = (s16[528,128]{1,0:T(8,128)(2,1)S(1)}, s16[528,128]{1,0:T(8,128)(2,1)S(1)}, u32[]{:S(2)}, u32[]{:S(2)}) collective-permute-start(s16[528,128]{1,0:T(8,128)(2,1)S(1)} %get-tuple-element.62), channel_id=1, source_target_pairs={{0,16},{4,20},{8,24},{12,28},{16,0},{20,4},{24,8},{28,12},{1,17},{... | collective-permute-start | bytes 405512 | tf_op jit(solution)/shard_map/ppermute | solution.py:277
  52.7 2.9 %collective-permute-done.5.refs_5_ = s16[544,128]{1,0:T(8,128)(2,1)S(1)} collective-permute-done((s16[544,128]{1,0:T(8,128)(2,1)S(1)}, s16[544,128]{1,0:T(8,128)(2,1)S(1)}, u32[]{:S(2)}, u32[]{:S(2)}) %collective-permute-start.5) | collective-permute-done | bytes 139296 | tf_op jit(solution)/shard_map/ppermute | solution.py:277
  55.6 4.5 %collective-permute-done.6.refs_6_ = s16[544,128]{1,0:T(8,128)(2,1)S(1)} collective-permute-done((s16[544,128]{1,0:T(8,128)(2,1)S(1)}, s16[544,128]{1,0:T(8,128)(2,1)S(1)}, u32[]{:S(2)}, u32[]{:S(2)}) %collective-permute-start.6) | collective-permute-done | bytes 139296 | tf_op jit(solution)/shard_map/ppermute | solution.py:277
  60.1 4.9 %product.3 = (s16[528,128]{1,0:T(8,128)(2,1)S(1)}, s16[528,128]{1,0:T(8,128)(2,1)S(1)}, s16[528,128]{1,0:T(8,128)(2,1)S(1)}, s16[528,128]{1,0:T(8,128)(2,1)S(1)}...) custom-call(s32[1]{0:T(128)S(6)} %copy.11.pair_ref, ...), custom_call_target="tpu_custom_call" | custom-call | flops 3221225472 | bytes 10485760 | tf_op jit(solution)/shard_map/product/pallas_call | solution.py:353
  65.8 3.4 %collective-permute-start.27 = (s16[528,128]{1,0:T(8,128)(2,1)S(1)}, s16[528,128]{1,0:T(8,128)(2,1)S(1)}, u32[]{:S(2)}, u32[]{:S(2)}) collective-permute-start(s16[528,128]{1,0:T(8,128)(2,1)S(1)} %get-tuple-element.68), channel_id=1, source_target_pairs={{0,28},{4,24},{8,20},{12,16},{16,12},{20,8},{24,4},{28,0},{1,29},{... | collective-permute-start | bytes 405512 | tf_op jit(solution)/shard_map/ppermute | solution.py:277
  69.2 2.8 %collective-permute-start.17 = (s16[528,128]{1,0:T(8,128)(2,1)S(1)}, s16[528,128]{1,0:T(8,128)(2,1)S(1)}, u32[]{:S(2)}, u32[]{:S(2)}) collective-permute-start(s16[528,128]{1,0:T(8,128)(2,1)S(1)} %get-tuple-element.57), channel_id=1, source_target_pairs={{0,16},{4,20},{8,24},{12,28},{16,0},{20,4},{24,8},{28,12},{1,17},{... | collective-permute-start | bytes 405512 | tf_op jit(solution)/shard_map/ppermute | solution.py:277
  73.1 1.4 %collective-permute-start.19 = (s16[528,128]{1,0:T(8,128)(2,1)S(1)}, s16[528,128]{1,0:T(8,128)(2,1)S(1)}, u32[]{:S(2)}, u32[]{:S(2)}) collective-permute-start(s16[528,128]{1,0:T(8,128)(2,1)S(1)} %get-tuple-element.59), channel_id=1, source_target_pairs={{0,8},{4,12},{8,0},{12,4},{16,24},{20,28},{24,16},{28,20},{1,9},{5... | collective-permute-start | bytes 405512 | tf_op jit(solution)/shard_map/ppermute | solution.py:277
  74.6 4.8 %collective-permute-done.26.refs_5_ = s16[528,128]{1,0:T(8,128)(2,1)S(1)} collective-permute-done((s16[528,128]{1,0:T(8,128)(2,1)S(1)}, s16[528,128]{1,0:T(8,128)(2,1)S(1)}, u32[]{:S(2)}, u32[]{:S(2)}) %collective-permute-start.26) | collective-permute-done | bytes 135200 | tf_op jit(solution)/shard_map/ppermute | solution.py:277
  79.4 5.5 %collective-permute-done.27.refs_6_ = s16[528,128]{1,0:T(8,128)(2,1)S(1)} collective-permute-done((s16[528,128]{1,0:T(8,128)(2,1)S(1)}, s16[528,128]{1,0:T(8,128)(2,1)S(1)}, u32[]{:S(2)}, u32[]{:S(2)}) %collective-permute-start.27) | collective-permute-done | bytes 135200 | tf_op jit(solution)/shard_map/ppermute | solution.py:277
  86.1 5.3 %collective-permute-start.16 = (s16[528,128]{1,0:T(8,128)(2,1)S(1)}, s16[528,128]{1,0:T(8,128)(2,1)S(1)}, u32[]{:S(2)}, u32[]{:S(2)}) collective-permute-start(s16[528,128]{1,0:T(8,128)(2,1)S(1)} %get-tuple-element.56), channel_id=1, source_target_pairs={{0,28},{4,24},{8,20},{12,16},{16,12},{20,8},{24,4},{28,0},{1,29},{... | collective-permute-start | bytes 405512 | tf_op jit(solution)/shard_map/ppermute | solution.py:277
  91.4 1.5 %result.3.refs_5_ = f32[2,64,8192]{2,1,0:T(8,128)} custom-call(s16[528,128]{1,0:T(8,128)(2,1)S(1)} %collective-permute-done.21.refs_0_, s16[528,128]{1,0:T(8,128)(2,1)S(1)} %collective-permute-done.22.refs_1_, s16[528,128]{1,0:T(8,128)(2,1)S(1)} %collective-permute-done.23.refs_2_, s16[528,128]{1,0:T(8,128)(2,1)S(1)} %collective-permute-done.24.refs_3_, ...), custom_call_target="tpu_custom_call" | custom-call | flops 1048576 | bytes 2097152 | tf_op jit(solution)/shard_map/result/pallas_call | solution.py:376
  94.0 3.6 %collective-permute-done.15.refs_1_ = s16[528,128]{1,0:T(8,128)(2,1)S(1)} collective-permute-done((s16[528,128]{1,0:T(8,128)(2,1)S(1)}, s16[528,128]{1,0:T(8,128)(2,1)S(1)}, u32[]{:S(2)}, u32[]{:S(2)}) %collective-permute-start.15) | collective-permute-done | bytes 135200 | tf_op jit(solution)/shard_map/ppermute | solution.py:277
  97.6 3.0 %collective-permute-done.16.refs_2_ = s16[528,128]{1,0:T(8,128)(2,1)S(1)} collective-permute-done((s16[528,128]{1,0:T(8,128)(2,1)S(1)}, s16[528,128]{1,0:T(8,128)(2,1)S(1)}, u32[]{:S(2)}, u32[]{:S(2)}) %collective-permute-start.16) | collective-permute-done | bytes 135200 | tf_op jit(solution)/shard_map/ppermute | solution.py:277
  (61 shorter events, 14.2 us)
Async XLA Ops:
  5.0 15.0 %collective-permute-start.10 = (s16[544,128]{1,0:T(8,128)(2,1)}, s16[544,128]{1,0:T(8,128)(2,1)S(1)}, u32[]{:S(2)}, u32[]{:S(2)}) collective-permute-start(s16[544,128]{1,0:T(8,128)(2,1)} %get-tuple-element.37.refs_0_), channel_id=1, source_target_pairs={{0,20},{4,16},{8,28},{12,24},{16,4},{20,0},{24,12},{28,8},{1,21},{... | collective-permute-start | bytes 417800 | tf_op jit(solution)/shard_map/ppermute | solution.py:277
  10.8 16.3 %collective-permute-start.9 = (s16[544,128]{1,0:T(8,128)(2,1)}, s16[544,128]{1,0:T(8,128)(2,1)S(1)}, u32[]{:S(2)}, u32[]{:S(2)}) collective-permute-start(s16[544,128]{1,0:T(8,128)(2,1)} %get-tuple-element.49), channel_id=1, source_target_pairs={{0,8},{4,12},{8,0},{12,4},{16,24},{20,28},{24,16},{28,20},{1,9},{5... | collective-permute-start | bytes 417800 | tf_op jit(solution)/shard_map/ppermute | solution.py:277
  11.0 22.0 %collective-permute-start.11 = (s16[544,128]{1,0:T(8,128)(2,1)}, s16[544,128]{1,0:T(8,128)(2,1)S(1)}, u32[]{:S(2)}, u32[]{:S(2)}) collective-permute-start(s16[544,128]{1,0:T(8,128)(2,1)} %get-tuple-element.50), channel_id=1, source_target_pairs={{0,12},{4,8},{8,4},{12,0},{16,28},{20,24},{24,20},{28,16},{1,13},{... | collective-permute-start | bytes 417800 | tf_op jit(solution)/shard_map/ppermute | solution.py:277
  14.2 18.8 %collective-permute-start.12 = (s16[544,128]{1,0:T(8,128)(2,1)}, s16[544,128]{1,0:T(8,128)(2,1)S(1)}, u32[]{:S(2)}, u32[]{:S(2)}) collective-permute-start(s16[544,128]{1,0:T(8,128)(2,1)} %get-tuple-element.51), channel_id=1, source_target_pairs={{0,24},{4,28},{8,16},{12,20},{16,8},{20,12},{24,0},{28,4},{1,25},{... | collective-permute-start | bytes 417800 | tf_op jit(solution)/shard_map/ppermute | solution.py:277
  20.0 15.9 %collective-permute-start.13 = (s16[544,128]{1,0:T(8,128)(2,1)S(1)}, s16[544,128]{1,0:T(8,128)(2,1)S(1)}, u32[]{:S(2)}, u32[]{:S(2)}) collective-permute-start(s16[544,128]{1,0:T(8,128)(2,1)S(1)} %copy-done.4), channel_id=1, source_target_pairs={{0,28},{4,24},{8,20},{12,16},{16,12},{20,8},{24,4},{28,0},{1,29},{... | collective-permute-start | bytes 417800 | tf_op jit(solution)/shard_map/ppermute | solution.py:277
  22.0 14.3 %collective-permute-start = (s16[544,128]{1,0:T(8,128)(2,1)}, s16[544,128]{1,0:T(8,128)(2,1)S(1)}, u32[]{:S(2)}, u32[]{:S(2)}) collective-permute-start(s16[544,128]{1,0:T(8,128)(2,1)} %get-tuple-element.39), channel_id=1, source_target_pairs={{0,16},{4,20},{8,24},{12,28},{16,0},{20,4},{24,8},{28,12},{1,17},{... | collective-permute-start | bytes 417800 | tf_op jit(solution)/shard_map/ppermute | solution.py:277
  33.0 12.6 %collective-permute-start.2 = (s16[544,128]{1,0:T(8,128)(2,1)S(1)}, s16[544,128]{1,0:T(8,128)(2,1)S(1)}, u32[]{:S(2)}, u32[]{:S(2)}) collective-permute-start(s16[544,128]{1,0:T(8,128)(2,1)S(1)} %copy-done.9), channel_id=1, source_target_pairs={{0,8},{4,12},{8,0},{12,4},{16,24},{20,28},{24,16},{28,20},{1,9},{5... | collective-permute-start | bytes 417800 | tf_op jit(solution)/shard_map/ppermute | solution.py:277
  33.1 17.8 %collective-permute-start.3 = (s16[544,128]{1,0:T(8,128)(2,1)S(1)}, s16[544,128]{1,0:T(8,128)(2,1)S(1)}, u32[]{:S(2)}, u32[]{:S(2)}) collective-permute-start(s16[544,128]{1,0:T(8,128)(2,1)S(1)} %copy-done.8), channel_id=1, source_target_pairs={{0,20},{4,16},{8,28},{12,24},{16,4},{20,0},{24,12},{28,8},{1,21},{... | collective-permute-start | bytes 417800 | tf_op jit(solution)/shard_map/ppermute | solution.py:277
  35.9 15.4 %collective-permute-start.4 = (s16[544,128]{1,0:T(8,128)(2,1)S(1)}, s16[544,128]{1,0:T(8,128)(2,1)S(1)}, u32[]{:S(2)}, u32[]{:S(2)}) collective-permute-start(s16[544,128]{1,0:T(8,128)(2,1)S(1)} %copy-done.7), channel_id=1, source_target_pairs={{0,12},{4,8},{8,4},{12,0},{16,28},{20,24},{24,20},{28,16},{1,13},{... | collective-permute-start | bytes 417800 | tf_op jit(solution)/shard_map/ppermute | solution.py:277
  36.3 19.3 %collective-permute-start.5 = (s16[544,128]{1,0:T(8,128)(2,1)S(1)}, s16[544,128]{1,0:T(8,128)(2,1)S(1)}, u32[]{:S(2)}, u32[]{:S(2)}) collective-permute-start(s16[544,128]{1,0:T(8,128)(2,1)S(1)} %copy-done.6), channel_id=1, source_target_pairs={{0,24},{4,28},{8,16},{12,20},{16,8},{20,12},{24,0},{28,4},{1,25},{... | collective-permute-start | bytes 417800 | tf_op jit(solution)/shard_map/ppermute | solution.py:277
  37.6 22.5 %collective-permute-start.6 = (s16[544,128]{1,0:T(8,128)(2,1)S(1)}, s16[544,128]{1,0:T(8,128)(2,1)S(1)}, u32[]{:S(2)}, u32[]{:S(2)}) collective-permute-start(s16[544,128]{1,0:T(8,128)(2,1)S(1)} %copy-done.5), channel_id=1, source_target_pairs={{0,28},{4,24},{8,20},{12,16},{16,12},{20,8},{24,4},{28,0},{1,29},{... | collective-permute-start | bytes 417800 | tf_op jit(solution)/shard_map/ppermute | solution.py:277
  45.5 19.4 %collective-permute-start.21 = (s16[528,128]{1,0:T(8,128)(2,1)S(1)}, s16[528,128]{1,0:T(8,128)(2,1)S(1)}, u32[]{:S(2)}, u32[]{:S(2)}) collective-permute-start(s16[528,128]{1,0:T(8,128)(2,1)S(1)} %get-tuple-element.62), channel_id=1, source_target_pairs={{0,16},{4,20},{8,24},{12,28},{16,0},{20,4},{24,8},{28,12},{1,17},{... | collective-permute-start | bytes 405512 | tf_op jit(solution)/shard_map/ppermute | solution.py:277
  50.9 14.9 %collective-permute-start.22 = (s16[528,128]{1,0:T(8,128)(2,1)S(1)}, s16[528,128]{1,0:T(8,128)(2,1)S(1)}, u32[]{:S(2)}, u32[]{:S(2)}) collective-permute-start(s16[528,128]{1,0:T(8,128)(2,1)S(1)} %get-tuple-element.63), channel_id=1, source_target_pairs={{0,4},{4,0},{8,12},{12,8},{16,20},{20,16},{24,28},{28,24},{1,5},{5... | collective-permute-start | bytes 405512 | tf_op jit(solution)/shard_map/ppermute | solution.py:277
  51.3 17.9 %collective-permute-start.23 = (s16[528,128]{1,0:T(8,128)(2,1)S(1)}, s16[528,128]{1,0:T(8,128)(2,1)S(1)}, u32[]{:S(2)}, u32[]{:S(2)}) collective-permute-start(s16[528,128]{1,0:T(8,128)(2,1)S(1)} %get-tuple-element.64), channel_id=1, source_target_pairs={{0,8},{4,12},{8,0},{12,4},{16,24},{20,28},{24,16},{28,20},{1,9},{5... | collective-permute-start | bytes 405512 | tf_op jit(solution)/shard_map/ppermute | solution.py:277
  55.6 16.4 %collective-permute-start.24 = (s16[528,128]{1,0:T(8,128)(2,1)S(1)}, s16[528,128]{1,0:T(8,128)(2,1)S(1)}, u32[]{:S(2)}, u32[]{:S(2)}) collective-permute-start(s16[528,128]{1,0:T(8,128)(2,1)S(1)} %get-tuple-element.65), channel_id=1, source_target_pairs={{0,20},{4,16},{8,28},{12,24},{16,4},{20,0},{24,12},{28,8},{1,21},{... | collective-permute-start | bytes 405512 | tf_op jit(solution)/shard_map/ppermute | solution.py:277
  60.0 13.1 %collective-permute-start.25 = (s16[528,128]{1,0:T(8,128)(2,1)S(1)}, s16[528,128]{1,0:T(8,128)(2,1)S(1)}, u32[]{:S(2)}, u32[]{:S(2)}) collective-permute-start(s16[528,128]{1,0:T(8,128)(2,1)S(1)} %get-tuple-element.66), channel_id=1, source_target_pairs={{0,12},{4,8},{8,4},{12,0},{16,28},{20,24},{24,20},{28,16},{1,13},{... | collective-permute-start | bytes 405512 | tf_op jit(solution)/shard_map/ppermute | solution.py:277
  65.0 14.4 %collective-permute-start.26 = (s16[528,128]{1,0:T(8,128)(2,1)S(1)}, s16[528,128]{1,0:T(8,128)(2,1)S(1)}, u32[]{:S(2)}, u32[]{:S(2)}) collective-permute-start(s16[528,128]{1,0:T(8,128)(2,1)S(1)} %get-tuple-element.67), channel_id=1, source_target_pairs={{0,24},{4,28},{8,16},{12,20},{16,8},{20,12},{24,0},{28,4},{1,25},{... | collective-permute-start | bytes 405512 | tf_op jit(solution)/shard_map/ppermute | solution.py:277
  65.8 19.0 %collective-permute-start.27 = (s16[528,128]{1,0:T(8,128)(2,1)S(1)}, s16[528,128]{1,0:T(8,128)(2,1)S(1)}, u32[]{:S(2)}, u32[]{:S(2)}) collective-permute-start(s16[528,128]{1,0:T(8,128)(2,1)S(1)} %get-tuple-element.68), channel_id=1, source_target_pairs={{0,28},{4,24},{8,20},{12,16},{16,12},{20,8},{24,4},{28,0},{1,29},{... | collective-permute-start | bytes 405512 | tf_op jit(solution)/shard_map/ppermute | solution.py:277
  69.2 16.1 %collective-permute-start.17 = (s16[528,128]{1,0:T(8,128)(2,1)S(1)}, s16[528,128]{1,0:T(8,128)(2,1)S(1)}, u32[]{:S(2)}, u32[]{:S(2)}) collective-permute-start(s16[528,128]{1,0:T(8,128)(2,1)S(1)} %get-tuple-element.57), channel_id=1, source_target_pairs={{0,16},{4,20},{8,24},{12,28},{16,0},{20,4},{24,8},{28,12},{1,17},{... | collective-permute-start | bytes 405512 | tf_op jit(solution)/shard_map/ppermute | solution.py:277
  72.0 14.0 %collective-permute-start.18 = (s16[528,128]{1,0:T(8,128)(2,1)S(1)}, s16[528,128]{1,0:T(8,128)(2,1)S(1)}, u32[]{:S(2)}, u32[]{:S(2)}) collective-permute-start(s16[528,128]{1,0:T(8,128)(2,1)S(1)} %get-tuple-element.58), channel_id=1, source_target_pairs={{0,4},{4,0},{8,12},{12,8},{16,20},{20,16},{24,28},{28,24},{1,5},{5... | collective-permute-start | bytes 405512 | tf_op jit(solution)/shard_map/ppermute | solution.py:277
  73.1 19.7 %collective-permute-start.19 = (s16[528,128]{1,0:T(8,128)(2,1)S(1)}, s16[528,128]{1,0:T(8,128)(2,1)S(1)}, u32[]{:S(2)}, u32[]{:S(2)}) collective-permute-start(s16[528,128]{1,0:T(8,128)(2,1)S(1)} %get-tuple-element.59), channel_id=1, source_target_pairs={{0,8},{4,12},{8,0},{12,4},{16,24},{20,28},{24,16},{28,20},{1,9},{5... | collective-permute-start | bytes 405512 | tf_op jit(solution)/shard_map/ppermute | solution.py:277
  79.4 13.5 %collective-permute-start.20 = (s16[528,128]{1,0:T(8,128)(2,1)S(1)}, s16[528,128]{1,0:T(8,128)(2,1)S(1)}, u32[]{:S(2)}, u32[]{:S(2)}) collective-permute-start(s16[528,128]{1,0:T(8,128)(2,1)S(1)} %get-tuple-element.60), channel_id=1, source_target_pairs={{0,20},{4,16},{8,28},{12,24},{16,4},{20,0},{24,12},{28,8},{1,21},{... | collective-permute-start | bytes 405512 | tf_op jit(solution)/shard_map/ppermute | solution.py:277
  85.3 12.3 %collective-permute-start.15 = (s16[528,128]{1,0:T(8,128)(2,1)S(1)}, s16[528,128]{1,0:T(8,128)(2,1)S(1)}, u32[]{:S(2)}, u32[]{:S(2)}) collective-permute-start(s16[528,128]{1,0:T(8,128)(2,1)S(1)} %get-tuple-element.55), channel_id=1, source_target_pairs={{0,24},{4,28},{8,16},{12,20},{16,8},{20,12},{24,0},{28,4},{1,25},{... | collective-permute-start | bytes 405512 | tf_op jit(solution)/shard_map/ppermute | solution.py:277
  86.1 14.6 %collective-permute-start.16 = (s16[528,128]{1,0:T(8,128)(2,1)S(1)}, s16[528,128]{1,0:T(8,128)(2,1)S(1)}, u32[]{:S(2)}, u32[]{:S(2)}) collective-permute-start(s16[528,128]{1,0:T(8,128)(2,1)S(1)} %get-tuple-element.56), channel_id=1, source_target_pairs={{0,28},{4,24},{8,20},{12,16},{16,12},{20,8},{24,4},{28,0},{1,29},{... | collective-permute-start | bytes 405512 | tf_op jit(solution)/shard_map/ppermute | solution.py:277
  (14 other events, 109.9 us)

commit v6 on v5

--- a/solution.py
+++ b/solution.py
@@ -14,8 +14,8 @@
 blend_weight = 0.5
 
 LANES = 128
-TILE = 16
-EXTRA = 8
+EXTRA = 6
+CODES = 8
 CHUNKS = 2
 TOP = 32700.0
 EDGE_TOP = 16384.0
@@ -108,9 +108,10 @@
 
         def compute(pair, _):
             cols = lanes_of(pair)
+            ends = []
             for half in range(2):
                 slab = pair * 2 + half
-                ends, top = [], jnp.zeros((8, LANES), jnp.float32)
+                top = jnp.zeros((8, LANES), jnp.float32)
                 for f in range(2):
                     n = n_buf[at, half, f, :, cols].astype(jnp.float32)
                     prev = jnp.where(row == 0, n, pltpu.roll(n, 1, 0))
@@ -120,19 +121,20 @@
                     top = jnp.maximum(top, jnp.max(jnp.abs(v).reshape(levels // 8, 8, LANES), axis=0))
                     ends += [n[:1], n[levels - 1 :]]
                 tops[slab] = top
-                extra[slab] = jnp.concatenate(ends + [jnp.zeros((4, LANES), jnp.float32)], axis=0)
+            extra[pair] = jnp.concatenate(ends, axis=0)
             return 0
 
         lax.fori_loop(0, slabs // 2, compute, 0)
         ends = extra[...]
         code = scale_code(jnp.max(tops[...], axis=1), FINE)
         factor = encode_factor(code, TOP)
-        edge_code = scale_code(jnp.max(jnp.abs(ends), axis=1), 1.0)
-        edge_factor = encode_factor(edge_code, EDGE_TOP)
+        edge_codes = [scale_code(jnp.max(jnp.abs(e), axis=1), 1.0) for e in (ends[:, :4], ends[:, 4:])]
+        edge_factors = [encode_factor(c, EDGE_TOP)[:, None, :] for c in edge_codes]
         at_row = lax.broadcasted_iota(jnp.int32, ends.shape, 1)
-        ends = jnp.round(ends * edge_factor[:, None, :])
-        ends = jnp.where(at_row == 4, edge_code[:, None, :], jnp.where(at_row == 5, code[:, None, :], ends))
-        messages[at, slabs * rows :, :] = to_int16(ends.reshape(slabs * EXTRA, LANES))
+        ends = jnp.round(ends * jnp.where(at_row < 4, *edge_factors))
+        messages[at, slabs * rows :, :] = to_int16(
+            jnp.concatenate([ends.reshape(slabs * 4, LANES), *edge_codes, code], axis=0)
+        )
         tops[:, 0, :] = factor
 
         def code_slab(slab, _):
@@ -184,21 +186,21 @@
         v_both, y, edges, codes = scratch[t % 2 * 4 : t % 2 * 4 + 4]
         extras = []
         for ref, peer in zip(ins, peers):
-            at = slabs * rows + t * TILE
-            two = to_float(ref[at : at + TILE, :])
-            power = jnp.exp2(two * (1.0 / FINE))
-            extras.append(power)
+            extra = to_float(ref[slabs * rows :, :])
+            power = jnp.exp2(extra[4 * slabs :] * (1.0 / FINE))
+            extras.append(power[slabs + 2 * t : slabs + 2 * t + 2] * (1.0 / TOP))
             for j in range(2):
-                at = j * EXTRA
-                edges[peer, :, j * LANES : (j + 1) * LANES] = two[at : at + 4] * (
-                    power[at + 4 : at + 5] * (1.0 / EDGE_TOP)
+                at = t * 8 + j * 4
+                code = j * (slabs // 2) + t
+                edges[peer, :, j * LANES : (j + 1) * LANES] = extra[at : at + 4] * (
+                    power[code : code + 1] * (1.0 / EDGE_TOP)
                 )
-        for ref, peer, power in zip(ins, peers, extras):
+        for ref, peer, scales in zip(ins, peers, extras):
             before, after = jnp.maximum(peer - 1, 0), jnp.minimum(peer + 1, groups - 1)
             weight_before, weight_after = edge_weight[peer], edge_weight[groups + peer]
             for j in range(2):
                 cols = slice(j * LANES, (j + 1) * LANES)
-                scale = power[j * EXTRA + 5 : j * EXTRA + 6] * (1.0 / TOP)
+                scale = scales[j : j + 1]
                 here = swapped(edges[peer, :, cols])
                 low = weight_before * (edges[before, :, cols] - here)
                 high = weight_after * (edges[after, :, cols] - here)
@@ -329,7 +331,7 @@
                 pltpu.VMEM((count, out_rows, LANES), jnp.int16),
                 pltpu.VMEM((slabs * rows, LANES), jnp.float32),
                 pltpu.VMEM((slabs, 8, LANES), jnp.float32),
-                pltpu.VMEM((slabs, EXTRA, LANES), jnp.float32),
+                pltpu.VMEM((slabs // 2, 8, LANES), jnp.float32),
                 pltpu.SemaphoreType.DMA((count, 2, 2)),
                 pltpu.SemaphoreType.DMA((count + 1,)),
             ],
@@ -356,7 +358,7 @@
             6 * size * size * slabs * LANES,
             10 * MIB,
             32,
-            out_shape=[jax.ShapeDtypeStruct((slabs * rows + TILE, LANES), jnp.int16)] * groups,
+            out_shape=[jax.ShapeDtypeStruct((slabs * rows + CODES, LANES), jnp.int16)] * groups,
             in_specs=[pl.BlockSpec(memory_space=pltpu.SMEM)] * 2
             + [vmem] * (groups + 1)
             + [hbm for _ in earlier],
@@ -368,7 +370,7 @@
                 pltpu.VMEM((groups, 4, 2 * LANES), jnp.float32),
                 pltpu.VMEM((2, groups, 8, LANES), jnp.float32),
             ]
-            + [pltpu.VMEM((groups, TILE, LANES), jnp.float32)],
+            + [pltpu.VMEM((groups, CODES, LANES), jnp.float32)],
         )(pair_of_slot, edge_weight, *messages, both, *earlier)
 
     def result(ks, chunk, messages, previous):

time: 103 us -> 101 us (0.981)
  starting transfers between devices: 45.1 us -> 43.6 us
    ppermute x28, starting transfers between devices: 45.1 us -> 43.6 us  [send(): lax.ppermute(message, 'rad', [(i, i ^ k) for i in range(groups)])]
  transfers between devices with their start and end apart: 28 -> 28, of which waited for: 8 -> 8; matrix products, arithmetic and copies ran while one was open for 0% -> 0% of each run, Pallas kernels for 23% -> 24%
where the time goes in v6:
time: 101 us; the launch traced here: 100 us
  starting transfers between devices  43.6 us (43%)
  Pallas kernels  26.9 us (27%)
  waiting for transfers between devices  25.6 us (25%)
  local copies, waits for them, and re-layouts  3.41 us (3%)
    ppermute x28, starting transfers between devices, send(): lax.ppermute(message, 'rad', [(i, i ^ k) for i in range(groups)])  43.6 us
    ppermute x28, waiting for transfers between devices, send(): lax.ppermute(message, 'rad', [(i, i ^ k) for i in range(groups)])  25.6 us
    pallas_call x2, Pallas kernels, product(): call(functools.partial(product_kernel, order, chunk * span // LANES, slab...  11.4 us
    pallas_call x3, Pallas kernels, right_side(): call(functools.partial(right_side_kernel, ks, slabs, chunk * span, width)...  10.8 us
    pallas_call x3, Pallas kernels, result(): call(functools.partial(result_kernel, ks, slabs, chunk * span, width), 'r...  3.55 us
    unnamed x20, local copies, waits for them, and re-layouts  3.41 us
  transfers between devices with their start and end apart: 28, of which 8 were waited for; matrix products, arithmetic and copies ran while one was open for 0% of the time, Pallas kernels for 24%

profile of v6, /device:TPU:8, one launch (start us, length us, event | category | flops | bytes accessed | tf_op | source)
XLA Modules:
  0.0 100.4 jit_solution(9153287453682776441)
XLA Ops:
  0.0 2.3 %right_side.3 = (s16[536,128]{1,0:T(8,128)(2,1)}, s16[536,128]{1,0:T(8,128)(2,1)}) custom-call(bf16[2,64,8192]{2,1,0:T(8,128)(2,1)} %nonlin.5, f32[2,64,8192]{2,1,0:T(8,128)} %state.5, f32[512,128]{1,0:T(8,128)} %constant.4.clone.table), custom_call_target="tpu_custom_call" | custom-call | flops 2097152 | bytes 2097152 | tf_op jit(solution)/shard_map/right_side/pallas_call | solution.py:318
  2.3 2.7 %collective-permute-start.7 = (s16[536,128]{1,0:T(8,128)(2,1)}, s16[536,128]{1,0:T(8,128)(2,1)S(1)}, u32[]{:S(2)}, u32[]{:S(2)}) collective-permute-start(s16[536,128]{1,0:T(8,128)(2,1)} %get-tuple-element.47), channel_id=1, source_target_pairs={{0,16},{4,20},{8,24},{12,28},{16,0},{20,4},{24,8},{28,12},{1,17},{... | collective-permute-start | bytes 411656 | tf_op jit(solution)/shard_map/ppermute | solution.py:279
  6.3 3.8 %right_side.4 = (s16[536,128]{1,0:T(8,128)(2,1)}, s16[536,128]{1,0:T(8,128)(2,1)}, s16[536,128]{1,0:T(8,128)(2,1)}, s16[536,128]{1,0:T(8,128)(2,1)}, s16[536,128]{1,0:T(8,128)(2,1)}, /*index=5*/s16[536,128]{1,0:T(8,128)(2,1)}) custom-call(bf16[2,64,8192]{2,1,0:T(8,128)(2,1)} %nonlin.5, f32[2,64,8192]{2,1,0:T(8,128)} %state.5, ...), custom_call_target="tpu_custom_call" | custom-call | flops 6291456 | bytes 6291456 | tf_op jit(solution)/shard_map/right_side/pallas_call | solution.py:318
  10.9 2.8 %collective-permute-start.11 = (s16[536,128]{1,0:T(8,128)(2,1)}, s16[536,128]{1,0:T(8,128)(2,1)S(1)}, u32[]{:S(2)}, u32[]{:S(2)}) collective-permute-start(s16[536,128]{1,0:T(8,128)(2,1)} %get-tuple-element.50), channel_id=1, source_target_pairs={{0,12},{4,8},{8,4},{12,0},{16,28},{20,24},{24,20},{28,16},{1,13},{... | collective-permute-start | bytes 411656 | tf_op jit(solution)/shard_map/ppermute | solution.py:279
  15.3 4.6 %right_side.5 = (s16[536,128]{1,0:T(8,128)(2,1)}, s16[536,128]{1,0:T(8,128)(2,1)}, s16[536,128]{1,0:T(8,128)(2,1)}, s16[536,128]{1,0:T(8,128)(2,1)}, s16[536,128...) custom-call(bf16[2,64,8192]{2,1,0:T(8,128)(2,1)} %nonlin.5, ...), custom_call_target="tpu_custom_call" | custom-call | flops 8388608 | bytes 8388608 | tf_op jit(solution)/shard_map/right_side/pallas_call | solution.py:318
  19.9 1.9 %collective-permute-start.13 = (s16[536,128]{1,0:T(8,128)(2,1)S(1)}, s16[536,128]{1,0:T(8,128)(2,1)S(1)}, u32[]{:S(2)}, u32[]{:S(2)}) collective-permute-start(s16[536,128]{1,0:T(8,128)(2,1)S(1)} %copy-done.4), channel_id=1, source_target_pairs={{0,28},{4,24},{8,20},{12,16},{16,12},{20,8},{24,4},{28,0},{1,29},{... | collective-permute-start | bytes 411656 | tf_op jit(solution)/shard_map/ppermute | solution.py:279
  21.8 5.1 %collective-permute-start = (s16[536,128]{1,0:T(8,128)(2,1)}, s16[536,128]{1,0:T(8,128)(2,1)S(1)}, u32[]{:S(2)}, u32[]{:S(2)}) collective-permute-start(s16[536,128]{1,0:T(8,128)(2,1)} %get-tuple-element.39), channel_id=1, source_target_pairs={{0,16},{4,20},{8,24},{12,28},{16,0},{20,4},{24,8},{28,12},{1,17},{... | collective-permute-start | bytes 411656 | tf_op jit(solution)/shard_map/ppermute | solution.py:279
  28.1 3.4 %copy-done = f32[1,2,1024,1024]{3,2,1,0:T(8,128)S(1)} copy-done((f32[1,2,1024,1024]{3,2,1,0:T(8,128)S(1)}, f32[1,2,1024,1024]{3,2,1,0:T(8,128)}, u32[]{:S(2)}) %copy-start) | copy-done | bytes 8388632
  32.9 2.9 %collective-permute-start.3 = (s16[536,128]{1,0:T(8,128)(2,1)S(1)}, s16[536,128]{1,0:T(8,128)(2,1)S(1)}, u32[]{:S(2)}, u32[]{:S(2)}) collective-permute-start(s16[536,128]{1,0:T(8,128)(2,1)S(1)} %copy-done.8), channel_id=1, source_target_pairs={{0,20},{4,16},{8,28},{12,24},{16,4},{20,0},{24,12},{28,8},{1,21},{... | collective-permute-start | bytes 411656 | tf_op jit(solution)/shard_map/ppermute | solution.py:279
  37.4 1.4 %collective-permute-start.6 = (s16[536,128]{1,0:T(8,128)(2,1)S(1)}, s16[536,128]{1,0:T(8,128)(2,1)S(1)}, u32[]{:S(2)}, u32[]{:S(2)}) collective-permute-start(s16[536,128]{1,0:T(8,128)(2,1)S(1)} %copy-done.5), channel_id=1, source_target_pairs={{0,28},{4,24},{8,20},{12,16},{16,12},{20,8},{24,4},{28,0},{1,29},{... | collective-permute-start | bytes 411656 | tf_op jit(solution)/shard_map/ppermute | solution.py:279
  38.9 6.5 %product.2 = (s16[520,128]{1,0:T(8,128)(2,1)S(1)}, s16[520,128]{1,0:T(8,128)(2,1)S(1)}, s16[520,128]{1,0:T(8,128)(2,1)S(1)}, s16[520,128]{1,0:T(8,128)(2,1)S(1)}...) custom-call(s32[1]{0:T(128)S(6)} %copy.11.pair_ref, ...), custom_call_target="tpu_custom_call" | custom-call | flops 3221225472 | bytes 10485760 | tf_op jit(solution)/shard_map/product/pallas_call | solution.py:355
  45.4 4.7 %collective-permute-start.21 = (s16[520,128]{1,0:T(8,128)(2,1)S(1)}, s16[520,128]{1,0:T(8,128)(2,1)S(1)}, u32[]{:S(2)}, u32[]{:S(2)}) collective-permute-start(s16[520,128]{1,0:T(8,128)(2,1)S(1)} %get-tuple-element.62), channel_id=1, source_target_pairs={{0,16},{4,20},{8,24},{12,28},{16,0},{20,4},{24,8},{28,12},{1,17},{... | collective-permute-start | bytes 399368 | tf_op jit(solution)/shard_map/ppermute | solution.py:279
  50.6 1.7 %collective-permute-start.23 = (s16[520,128]{1,0:T(8,128)(2,1)S(1)}, s16[520,128]{1,0:T(8,128)(2,1)S(1)}, u32[]{:S(2)}, u32[]{:S(2)}) collective-permute-start(s16[520,128]{1,0:T(8,128)(2,1)S(1)} %get-tuple-element.64), channel_id=1, source_target_pairs={{0,8},{4,12},{8,0},{12,4},{16,24},{20,28},{24,16},{28,20},{1,9},{5... | collective-permute-start | bytes 399368 | tf_op jit(solution)/shard_map/ppermute | solution.py:279
  52.3 2.8 %collective-permute-done.5.refs_5_ = s16[536,128]{1,0:T(8,128)(2,1)S(1)} collective-permute-done((s16[536,128]{1,0:T(8,128)(2,1)S(1)}, s16[536,128]{1,0:T(8,128)(2,1)S(1)}, u32[]{:S(2)}, u32[]{:S(2)}) %collective-permute-start.5) | collective-permute-done | bytes 137248 | tf_op jit(solution)/shard_map/ppermute | solution.py:279
  55.1 4.4 %collective-permute-done.6.refs_6_ = s16[536,128]{1,0:T(8,128)(2,1)S(1)} collective-permute-done((s16[536,128]{1,0:T(8,128)(2,1)S(1)}, s16[536,128]{1,0:T(8,128)(2,1)S(1)}, u32[]{:S(2)}, u32[]{:S(2)}) %collective-permute-start.6) | collective-permute-done | bytes 137248 | tf_op jit(solution)/shard_map/ppermute | solution.py:279
  59.5 4.9 %product.3 = (s16[520,128]{1,0:T(8,128)(2,1)S(1)}, s16[520,128]{1,0:T(8,128)(2,1)S(1)}, s16[520,128]{1,0:T(8,128)(2,1)S(1)}, s16[520,128]{1,0:T(8,128)(2,1)S(1)}...) custom-call(s32[1]{0:T(128)S(6)} %copy.11.pair_ref, ...), custom_call_target="tpu_custom_call" | custom-call | flops 3221225472 | bytes 10485760 | tf_op jit(solution)/shard_map/product/pallas_call | solution.py:355
  65.2 2.2 %collective-permute-start.27 = (s16[520,128]{1,0:T(8,128)(2,1)S(1)}, s16[520,128]{1,0:T(8,128)(2,1)S(1)}, u32[]{:S(2)}, u32[]{:S(2)}) collective-permute-start(s16[520,128]{1,0:T(8,128)(2,1)S(1)} %get-tuple-element.68), channel_id=1, source_target_pairs={{0,28},{4,24},{8,20},{12,16},{16,12},{20,8},{24,4},{28,0},{1,29},{... | collective-permute-start | bytes 399368 | tf_op jit(solution)/shard_map/ppermute | solution.py:279
  67.4 3.9 %collective-permute-start.17 = (s16[520,128]{1,0:T(8,128)(2,1)S(1)}, s16[520,128]{1,0:T(8,128)(2,1)S(1)}, u32[]{:S(2)}, u32[]{:S(2)}) collective-permute-start(s16[520,128]{1,0:T(8,128)(2,1)S(1)} %get-tuple-element.57), channel_id=1, source_target_pairs={{0,16},{4,20},{8,24},{12,28},{16,0},{20,4},{24,8},{28,12},{1,17},{... | collective-permute-start | bytes 399368 | tf_op jit(solution)/shard_map/ppermute | solution.py:279
  72.8 5.0 %collective-permute-done.26.refs_5_ = s16[520,128]{1,0:T(8,128)(2,1)S(1)} collective-permute-done((s16[520,128]{1,0:T(8,128)(2,1)S(1)}, s16[520,128]{1,0:T(8,128)(2,1)S(1)}, u32[]{:S(2)}, u32[]{:S(2)}) %collective-permute-start.26) | collective-permute-done | bytes 133152 | tf_op jit(solution)/shard_map/ppermute | solution.py:279
  77.8 6.0 %collective-permute-done.27.refs_6_ = s16[520,128]{1,0:T(8,128)(2,1)S(1)} collective-permute-done((s16[520,128]{1,0:T(8,128)(2,1)S(1)}, s16[520,128]{1,0:T(8,128)(2,1)S(1)}, u32[]{:S(2)}, u32[]{:S(2)}) %collective-permute-start.27) | collective-permute-done | bytes 133152 | tf_op jit(solution)/shard_map/ppermute | solution.py:279
  84.8 5.2 %collective-permute-start.16 = (s16[520,128]{1,0:T(8,128)(2,1)S(1)}, s16[520,128]{1,0:T(8,128)(2,1)S(1)}, u32[]{:S(2)}, u32[]{:S(2)}) collective-permute-start(s16[520,128]{1,0:T(8,128)(2,1)S(1)} %get-tuple-element.56), channel_id=1, source_target_pairs={{0,28},{4,24},{8,20},{12,16},{16,12},{20,8},{24,4},{28,0},{1,29},{... | collective-permute-start | bytes 399368 | tf_op jit(solution)/shard_map/ppermute | solution.py:279
  90.0 1.5 %result.3.refs_5_ = f32[2,64,8192]{2,1,0:T(8,128)} custom-call(s16[520,128]{1,0:T(8,128)(2,1)S(1)} %collective-permute-done.21.refs_0_, s16[520,128]{1,0:T(8,128)(2,1)S(1)} %collective-permute-done.22.refs_1_, s16[520,128]{1,0:T(8,128)(2,1)S(1)} %collective-permute-done.23.refs_2_, s16[520,128]{1,0:T(8,128)(2,1)S(1)} %collective-permute-done.24.refs_3_, ...), custom_call_target="tpu_custom_call" | custom-call | flops 1048576 | bytes 2097152 | tf_op jit(solution)/shard_map/result/pallas_call | solution.py:378
  93.4 3.3 %collective-permute-done.15.refs_1_ = s16[520,128]{1,0:T(8,128)(2,1)S(1)} collective-permute-done((s16[520,128]{1,0:T(8,128)(2,1)S(1)}, s16[520,128]{1,0:T(8,128)(2,1)S(1)}, u32[]{:S(2)}, u32[]{:S(2)}) %collective-permute-start.15) | collective-permute-done | bytes 133152 | tf_op jit(solution)/shard_map/ppermute | solution.py:279
  96.7 2.8 %collective-permute-done.16.refs_2_ = s16[520,128]{1,0:T(8,128)(2,1)S(1)} collective-permute-done((s16[520,128]{1,0:T(8,128)(2,1)S(1)}, s16[520,128]{1,0:T(8,128)(2,1)S(1)}, u32[]{:S(2)}, u32[]{:S(2)}) %collective-permute-start.16) | collective-permute-done | bytes 133152 | tf_op jit(solution)/shard_map/ppermute | solution.py:279
  (61 shorter events, 13.5 us)
Async XLA Ops:
  5.0 14.9 %collective-permute-start.10 = (s16[536,128]{1,0:T(8,128)(2,1)}, s16[536,128]{1,0:T(8,128)(2,1)S(1)}, u32[]{:S(2)}, u32[]{:S(2)}) collective-permute-start(s16[536,128]{1,0:T(8,128)(2,1)} %get-tuple-element.37.refs_0_), channel_id=1, source_target_pairs={{0,20},{4,16},{8,28},{12,24},{16,4},{20,0},{24,12},{28,8},{1,21},{... | collective-permute-start | bytes 411656 | tf_op jit(solution)/shard_map/ppermute | solution.py:279
  10.7 16.2 %collective-permute-start.9 = (s16[536,128]{1,0:T(8,128)(2,1)}, s16[536,128]{1,0:T(8,128)(2,1)S(1)}, u32[]{:S(2)}, u32[]{:S(2)}) collective-permute-start(s16[536,128]{1,0:T(8,128)(2,1)} %get-tuple-element.49), channel_id=1, source_target_pairs={{0,8},{4,12},{8,0},{12,4},{16,24},{20,28},{24,16},{28,20},{1,9},{5... | collective-permute-start | bytes 411656 | tf_op jit(solution)/shard_map/ppermute | solution.py:279
  10.9 21.9 %collective-permute-start.11 = (s16[536,128]{1,0:T(8,128)(2,1)}, s16[536,128]{1,0:T(8,128)(2,1)S(1)}, u32[]{:S(2)}, u32[]{:S(2)}) collective-permute-start(s16[536,128]{1,0:T(8,128)(2,1)} %get-tuple-element.50), channel_id=1, source_target_pairs={{0,12},{4,8},{8,4},{12,0},{16,28},{20,24},{24,20},{28,16},{1,13},{... | collective-permute-start | bytes 411656 | tf_op jit(solution)/shard_map/ppermute | solution.py:279
  14.1 18.8 %collective-permute-start.12 = (s16[536,128]{1,0:T(8,128)(2,1)}, s16[536,128]{1,0:T(8,128)(2,1)S(1)}, u32[]{:S(2)}, u32[]{:S(2)}) collective-permute-start(s16[536,128]{1,0:T(8,128)(2,1)} %get-tuple-element.51), channel_id=1, source_target_pairs={{0,24},{4,28},{8,16},{12,20},{16,8},{20,12},{24,0},{28,4},{1,25},{... | collective-permute-start | bytes 411656 | tf_op jit(solution)/shard_map/ppermute | solution.py:279
  19.9 15.8 %collective-permute-start.13 = (s16[536,128]{1,0:T(8,128)(2,1)S(1)}, s16[536,128]{1,0:T(8,128)(2,1)S(1)}, u32[]{:S(2)}, u32[]{:S(2)}) collective-permute-start(s16[536,128]{1,0:T(8,128)(2,1)S(1)} %copy-done.4), channel_id=1, source_target_pairs={{0,28},{4,24},{8,20},{12,16},{16,12},{20,8},{24,4},{28,0},{1,29},{... | collective-permute-start | bytes 411656 | tf_op jit(solution)/shard_map/ppermute | solution.py:279
  21.8 14.3 %collective-permute-start = (s16[536,128]{1,0:T(8,128)(2,1)}, s16[536,128]{1,0:T(8,128)(2,1)S(1)}, u32[]{:S(2)}, u32[]{:S(2)}) collective-permute-start(s16[536,128]{1,0:T(8,128)(2,1)} %get-tuple-element.39), channel_id=1, source_target_pairs={{0,16},{4,20},{8,24},{12,28},{16,0},{20,4},{24,8},{28,12},{1,17},{... | collective-permute-start | bytes 411656 | tf_op jit(solution)/shard_map/ppermute | solution.py:279
  32.8 12.6 %collective-permute-start.2 = (s16[536,128]{1,0:T(8,128)(2,1)S(1)}, s16[536,128]{1,0:T(8,128)(2,1)S(1)}, u32[]{:S(2)}, u32[]{:S(2)}) collective-permute-start(s16[536,128]{1,0:T(8,128)(2,1)S(1)} %copy-done.9), channel_id=1, source_target_pairs={{0,8},{4,12},{8,0},{12,4},{16,24},{20,28},{24,16},{28,20},{1,9},{5... | collective-permute-start | bytes 411656 | tf_op jit(solution)/shard_map/ppermute | solution.py:279
  32.9 17.2 %collective-permute-start.3 = (s16[536,128]{1,0:T(8,128)(2,1)S(1)}, s16[536,128]{1,0:T(8,128)(2,1)S(1)}, u32[]{:S(2)}, u32[]{:S(2)}) collective-permute-start(s16[536,128]{1,0:T(8,128)(2,1)S(1)} %copy-done.8), channel_id=1, source_target_pairs={{0,20},{4,16},{8,28},{12,24},{16,4},{20,0},{24,12},{28,8},{1,21},{... | collective-permute-start | bytes 411656 | tf_op jit(solution)/shard_map/ppermute | solution.py:279
  35.7 14.9 %collective-permute-start.4 = (s16[536,128]{1,0:T(8,128)(2,1)S(1)}, s16[536,128]{1,0:T(8,128)(2,1)S(1)}, u32[]{:S(2)}, u32[]{:S(2)}) collective-permute-start(s16[536,128]{1,0:T(8,128)(2,1)S(1)} %copy-done.7), channel_id=1, source_target_pairs={{0,12},{4,8},{8,4},{12,0},{16,28},{20,24},{24,20},{28,16},{1,13},{... | collective-permute-start | bytes 411656 | tf_op jit(solution)/shard_map/ppermute | solution.py:279
  36.0 19.1 %collective-permute-start.5 = (s16[536,128]{1,0:T(8,128)(2,1)S(1)}, s16[536,128]{1,0:T(8,128)(2,1)S(1)}, u32[]{:S(2)}, u32[]{:S(2)}) collective-permute-start(s16[536,128]{1,0:T(8,128)(2,1)S(1)} %copy-done.6), channel_id=1, source_target_pairs={{0,24},{4,28},{8,16},{12,20},{16,8},{20,12},{24,0},{28,4},{1,25},{... | collective-permute-start | bytes 411656 | tf_op jit(solution)/shard_map/ppermute | solution.py:279
  37.4 22.1 %collective-permute-start.6 = (s16[536,128]{1,0:T(8,128)(2,1)S(1)}, s16[536,128]{1,0:T(8,128)(2,1)S(1)}, u32[]{:S(2)}, u32[]{:S(2)}) collective-permute-start(s16[536,128]{1,0:T(8,128)(2,1)S(1)} %copy-done.5), channel_id=1, source_target_pairs={{0,28},{4,24},{8,20},{12,16},{16,12},{20,8},{24,4},{28,0},{1,29},{... | collective-permute-start | bytes 411656 | tf_op jit(solution)/shard_map/ppermute | solution.py:279
  45.4 19.1 %collective-permute-start.21 = (s16[520,128]{1,0:T(8,128)(2,1)S(1)}, s16[520,128]{1,0:T(8,128)(2,1)S(1)}, u32[]{:S(2)}, u32[]{:S(2)}) collective-permute-start(s16[520,128]{1,0:T(8,128)(2,1)S(1)} %get-tuple-element.62), channel_id=1, source_target_pairs={{0,16},{4,20},{8,24},{12,28},{16,0},{20,4},{24,8},{28,12},{1,17},{... | collective-permute-start | bytes 399368 | tf_op jit(solution)/shard_map/ppermute | solution.py:279
  50.1 15.1 %collective-permute-start.22 = (s16[520,128]{1,0:T(8,128)(2,1)S(1)}, s16[520,128]{1,0:T(8,128)(2,1)S(1)}, u32[]{:S(2)}, u32[]{:S(2)}) collective-permute-start(s16[520,128]{1,0:T(8,128)(2,1)S(1)} %get-tuple-element.63), channel_id=1, source_target_pairs={{0,4},{4,0},{8,12},{12,8},{16,20},{20,16},{24,28},{28,24},{1,5},{5... | collective-permute-start | bytes 399368 | tf_op jit(solution)/shard_map/ppermute | solution.py:279
  50.6 16.8 %collective-permute-start.23 = (s16[520,128]{1,0:T(8,128)(2,1)S(1)}, s16[520,128]{1,0:T(8,128)(2,1)S(1)}, u32[]{:S(2)}, u32[]{:S(2)}) collective-permute-start(s16[520,128]{1,0:T(8,128)(2,1)S(1)} %get-tuple-element.64), channel_id=1, source_target_pairs={{0,8},{4,12},{8,0},{12,4},{16,24},{20,28},{24,16},{28,20},{1,9},{5... | collective-permute-start | bytes 399368 | tf_op jit(solution)/shard_map/ppermute | solution.py:279
  55.1 16.2 %collective-permute-start.24 = (s16[520,128]{1,0:T(8,128)(2,1)S(1)}, s16[520,128]{1,0:T(8,128)(2,1)S(1)}, u32[]{:S(2)}, u32[]{:S(2)}) collective-permute-start(s16[520,128]{1,0:T(8,128)(2,1)S(1)} %get-tuple-element.65), channel_id=1, source_target_pairs={{0,20},{4,16},{8,28},{12,24},{16,4},{20,0},{24,12},{28,8},{1,21},{... | collective-permute-start | bytes 399368 | tf_op jit(solution)/shard_map/ppermute | solution.py:279
  59.5 11.9 %collective-permute-start.25 = (s16[520,128]{1,0:T(8,128)(2,1)S(1)}, s16[520,128]{1,0:T(8,128)(2,1)S(1)}, u32[]{:S(2)}, u32[]{:S(2)}) collective-permute-start(s16[520,128]{1,0:T(8,128)(2,1)S(1)} %get-tuple-element.66), channel_id=1, source_target_pairs={{0,12},{4,8},{8,4},{12,0},{16,28},{20,24},{24,20},{28,16},{1,13},{... | collective-permute-start | bytes 399368 | tf_op jit(solution)/shard_map/ppermute | solution.py:279
  64.4 13.4 %collective-permute-start.26 = (s16[520,128]{1,0:T(8,128)(2,1)S(1)}, s16[520,128]{1,0:T(8,128)(2,1)S(1)}, u32[]{:S(2)}, u32[]{:S(2)}) collective-permute-start(s16[520,128]{1,0:T(8,128)(2,1)S(1)} %get-tuple-element.67), channel_id=1, source_target_pairs={{0,24},{4,28},{8,16},{12,20},{16,8},{20,12},{24,0},{28,4},{1,25},{... | collective-permute-start | bytes 399368 | tf_op jit(solution)/shard_map/ppermute | solution.py:279
  65.2 18.7 %collective-permute-start.27 = (s16[520,128]{1,0:T(8,128)(2,1)S(1)}, s16[520,128]{1,0:T(8,128)(2,1)S(1)}, u32[]{:S(2)}, u32[]{:S(2)}) collective-permute-start(s16[520,128]{1,0:T(8,128)(2,1)S(1)} %get-tuple-element.68), channel_id=1, source_target_pairs={{0,28},{4,24},{8,20},{12,16},{16,12},{20,8},{24,4},{28,0},{1,29},{... | collective-permute-start | bytes 399368 | tf_op jit(solution)/shard_map/ppermute | solution.py:279
  67.4 16.5 %collective-permute-start.17 = (s16[520,128]{1,0:T(8,128)(2,1)S(1)}, s16[520,128]{1,0:T(8,128)(2,1)S(1)}, u32[]{:S(2)}, u32[]{:S(2)}) collective-permute-start(s16[520,128]{1,0:T(8,128)(2,1)S(1)} %get-tuple-element.57), channel_id=1, source_target_pairs={{0,16},{4,20},{8,24},{12,28},{16,0},{20,4},{24,8},{28,12},{1,17},{... | collective-permute-start | bytes 399368 | tf_op jit(solution)/shard_map/ppermute | solution.py:279
  71.4 13.4 %collective-permute-start.18 = (s16[520,128]{1,0:T(8,128)(2,1)S(1)}, s16[520,128]{1,0:T(8,128)(2,1)S(1)}, u32[]{:S(2)}, u32[]{:S(2)}) collective-permute-start(s16[520,128]{1,0:T(8,128)(2,1)S(1)} %get-tuple-element.58), channel_id=1, source_target_pairs={{0,4},{4,0},{8,12},{12,8},{16,20},{20,16},{24,28},{28,24},{1,5},{5... | collective-permute-start | bytes 399368 | tf_op jit(solution)/shard_map/ppermute | solution.py:279
  71.4 20.1 %collective-permute-start.19 = (s16[520,128]{1,0:T(8,128)(2,1)S(1)}, s16[520,128]{1,0:T(8,128)(2,1)S(1)}, u32[]{:S(2)}, u32[]{:S(2)}) collective-permute-start(s16[520,128]{1,0:T(8,128)(2,1)S(1)} %get-tuple-element.59), channel_id=1, source_target_pairs={{0,8},{4,12},{8,0},{12,4},{16,24},{20,28},{24,16},{28,20},{1,9},{5... | collective-permute-start | bytes 399368 | tf_op jit(solution)/shard_map/ppermute | solution.py:279
  77.8 14.4 %collective-permute-start.20 = (s16[520,128]{1,0:T(8,128)(2,1)S(1)}, s16[520,128]{1,0:T(8,128)(2,1)S(1)}, u32[]{:S(2)}, u32[]{:S(2)}) collective-permute-start(s16[520,128]{1,0:T(8,128)(2,1)S(1)} %get-tuple-element.60), channel_id=1, source_target_pairs={{0,20},{4,16},{8,28},{12,24},{16,4},{20,0},{24,12},{28,8},{1,21},{... | collective-permute-start | bytes 399368 | tf_op jit(solution)/shard_map/ppermute | solution.py:279
  83.9 12.8 %collective-permute-start.15 = (s16[520,128]{1,0:T(8,128)(2,1)S(1)}, s16[520,128]{1,0:T(8,128)(2,1)S(1)}, u32[]{:S(2)}, u32[]{:S(2)}) collective-permute-start(s16[520,128]{1,0:T(8,128)(2,1)S(1)} %get-tuple-element.55), channel_id=1, source_target_pairs={{0,24},{4,28},{8,16},{12,20},{16,8},{20,12},{24,0},{28,4},{1,25},{... | collective-permute-start | bytes 399368 | tf_op jit(solution)/shard_map/ppermute | solution.py:279
  84.8 14.7 %collective-permute-start.16 = (s16[520,128]{1,0:T(8,128)(2,1)S(1)}, s16[520,128]{1,0:T(8,128)(2,1)S(1)}, u32[]{:S(2)}, u32[]{:S(2)}) collective-permute-start(s16[520,128]{1,0:T(8,128)(2,1)S(1)} %get-tuple-element.56), channel_id=1, source_target_pairs={{0,28},{4,24},{8,20},{12,16},{16,12},{20,8},{24,4},{28,0},{1,29},{... | collective-permute-start | bytes 399368 | tf_op jit(solution)/shard_map/ppermute | solution.py:279
  (14 other events, 109.4 us)

commit v7 on v6

--- a/solution.py
+++ b/solution.py
@@ -302,6 +302,7 @@
     for i, k in enumerate(far):
         order += [k] + others[2 * i : 2 * i + 2]
     order += near[:1]
+    in_turn = [k for both in zip(far, others) for k in both] + far[-1:] + near[:1]
 
     def call(kernel, name, flops, moved, vmem_mib, **kwargs):
         return pl.pallas_call(
@@ -402,7 +403,7 @@
         back.append({k: send(m, k, groups) for k, m in zip(order, made)})
     out = None
     for chunk, came in enumerate(back):
-        for ks in [order] if chunk < CHUNKS - 1 else [order[:4] + order[-1:], order[4:-1]]:
+        for ks in [in_turn] if chunk < CHUNKS - 1 else [far[:1] + others + near[:1], far[1:]]:
             out = result(ks, chunk, [came[k] for k in ks], out)
     return out
 

time: 101 us -> 101 us (level)
  transfers between devices with their start and end apart: 28 -> 28, of which waited for: 8 -> 9; matrix products, arithmetic and copies ran while one was open for 0% -> 0% of each run, Pallas kernels for 24% -> 24%
where the time goes in v7:
time: 101 us; the launch traced here: 100 us
  starting transfers between devices  43 us (43%)
  Pallas kernels  26.9 us (27%)
  waiting for transfers between devices  26.1 us (26%)
  local copies, waits for them, and re-layouts  3.41 us (3%)
    ppermute x28, starting transfers between devices, send(): lax.ppermute(message, 'rad', [(i, i ^ k) for i in range(groups)])  43 us
    ppermute x28, waiting for transfers between devices, send(): lax.ppermute(message, 'rad', [(i, i ^ k) for i in range(groups)])  26.1 us
    pallas_call x2, Pallas kernels, product(): call(functools.partial(product_kernel, order, chunk * span // LANES, slab...  11.4 us
    pallas_call x3, Pallas kernels, right_side(): call(functools.partial(right_side_kernel, ks, slabs, chunk * span, width)...  10.8 us
    pallas_call x3, Pallas kernels, result(): call(functools.partial(result_kernel, ks, slabs, chunk * span, width), 'r...  3.55 us
    unnamed x20, local copies, waits for them, and re-layouts  3.41 us
  transfers between devices with their start and end apart: 28, of which 9 were waited for; matrix products, arithmetic and copies ran while one was open for 0% of the time, Pallas kernels for 24%

profile of v7, /device:TPU:8, one launch (start us, length us, event | category | flops | bytes accessed | tf_op | source)
XLA Modules:
  0.0 100.4 jit_solution(4777800459114089247)
XLA Ops:
  0.0 2.3 %right_side.3 = (s16[536,128]{1,0:T(8,128)(2,1)}, s16[536,128]{1,0:T(8,128)(2,1)}) custom-call(bf16[2,64,8192]{2,1,0:T(8,128)(2,1)} %nonlin.5, f32[2,64,8192]{2,1,0:T(8,128)} %state.5, f32[512,128]{1,0:T(8,128)} %constant.4.clone.table), custom_call_target="tpu_custom_call" | custom-call | flops 2097152 | bytes 2097152 | tf_op jit(solution)/shard_map/right_side/pallas_call | solution.py:319
  2.3 2.7 %collective-permute-start.7 = (s16[536,128]{1,0:T(8,128)(2,1)}, s16[536,128]{1,0:T(8,128)(2,1)S(1)}, u32[]{:S(2)}, u32[]{:S(2)}) collective-permute-start(s16[536,128]{1,0:T(8,128)(2,1)} %get-tuple-element.47), channel_id=1, source_target_pairs={{0,16},{4,20},{8,24},{12,28},{16,0},{20,4},{24,8},{28,12},{1,17},{... | collective-permute-start | bytes 411656 | tf_op jit(solution)/shard_map/ppermute | solution.py:279
  6.3 3.8 %right_side.4 = (s16[536,128]{1,0:T(8,128)(2,1)}, s16[536,128]{1,0:T(8,128)(2,1)}, s16[536,128]{1,0:T(8,128)(2,1)}, s16[536,128]{1,0:T(8,128)(2,1)}, s16[536,128]{1,0:T(8,128)(2,1)}, /*index=5*/s16[536,128]{1,0:T(8,128)(2,1)}) custom-call(bf16[2,64,8192]{2,1,0:T(8,128)(2,1)} %nonlin.5, f32[2,64,8192]{2,1,0:T(8,128)} %state.5, ...), custom_call_target="tpu_custom_call" | custom-call | flops 6291456 | bytes 6291456 | tf_op jit(solution)/shard_map/right_side/pallas_call | solution.py:319
  10.9 2.8 %collective-permute-start.11 = (s16[536,128]{1,0:T(8,128)(2,1)}, s16[536,128]{1,0:T(8,128)(2,1)S(1)}, u32[]{:S(2)}, u32[]{:S(2)}) collective-permute-start(s16[536,128]{1,0:T(8,128)(2,1)} %get-tuple-element.50), channel_id=1, source_target_pairs={{0,12},{4,8},{8,4},{12,0},{16,28},{20,24},{24,20},{28,16},{1,13},{... | collective-permute-start | bytes 411656 | tf_op jit(solution)/shard_map/ppermute | solution.py:279
  15.3 4.6 %right_side.5 = (s16[536,128]{1,0:T(8,128)(2,1)}, s16[536,128]{1,0:T(8,128)(2,1)}, s16[536,128]{1,0:T(8,128)(2,1)}, s16[536,128]{1,0:T(8,128)(2,1)}, s16[536,128...) custom-call(bf16[2,64,8192]{2,1,0:T(8,128)(2,1)} %nonlin.5, ...), custom_call_target="tpu_custom_call" | custom-call | flops 8388608 | bytes 8388608 | tf_op jit(solution)/shard_map/right_side/pallas_call | solution.py:319
  19.9 1.9 %collective-permute-start.13 = (s16[536,128]{1,0:T(8,128)(2,1)S(1)}, s16[536,128]{1,0:T(8,128)(2,1)S(1)}, u32[]{:S(2)}, u32[]{:S(2)}) collective-permute-start(s16[536,128]{1,0:T(8,128)(2,1)S(1)} %copy-done.4), channel_id=1, source_target_pairs={{0,28},{4,24},{8,20},{12,16},{16,12},{20,8},{24,4},{28,0},{1,29},{... | collective-permute-start | bytes 411656 | tf_op jit(solution)/shard_map/ppermute | solution.py:279
  21.8 5.1 %collective-permute-start = (s16[536,128]{1,0:T(8,128)(2,1)}, s16[536,128]{1,0:T(8,128)(2,1)S(1)}, u32[]{:S(2)}, u32[]{:S(2)}) collective-permute-start(s16[536,128]{1,0:T(8,128)(2,1)} %get-tuple-element.39), channel_id=1, source_target_pairs={{0,16},{4,20},{8,24},{12,28},{16,0},{20,4},{24,8},{28,12},{1,17},{... | collective-permute-start | bytes 411656 | tf_op jit(solution)/shard_map/ppermute | solution.py:279
  28.1 3.4 %copy-done = f32[1,2,1024,1024]{3,2,1,0:T(8,128)S(1)} copy-done((f32[1,2,1024,1024]{3,2,1,0:T(8,128)S(1)}, f32[1,2,1024,1024]{3,2,1,0:T(8,128)}, u32[]{:S(2)}) %copy-start) | copy-done | bytes 8388632
  32.9 2.9 %collective-permute-start.3 = (s16[536,128]{1,0:T(8,128)(2,1)S(1)}, s16[536,128]{1,0:T(8,128)(2,1)S(1)}, u32[]{:S(2)}, u32[]{:S(2)}) collective-permute-start(s16[536,128]{1,0:T(8,128)(2,1)S(1)} %copy-done.8), channel_id=1, source_target_pairs={{0,20},{4,16},{8,28},{12,24},{16,4},{20,0},{24,12},{28,8},{1,21},{... | collective-permute-start | bytes 411656 | tf_op jit(solution)/shard_map/ppermute | solution.py:279
  38.9 6.5 %product.2 = (s16[520,128]{1,0:T(8,128)(2,1)S(1)}, s16[520,128]{1,0:T(8,128)(2,1)S(1)}, s16[520,128]{1,0:T(8,128)(2,1)S(1)}, s16[520,128]{1,0:T(8,128)(2,1)S(1)}...) custom-call(s32[1]{0:T(128)S(6)} %copy.11.pair_ref, ...), custom_call_target="tpu_custom_call" | custom-call | flops 3221225472 | bytes 10485760 | tf_op jit(solution)/shard_map/product/pallas_call | solution.py:356
  45.4 4.7 %collective-permute-start.21 = (s16[520,128]{1,0:T(8,128)(2,1)S(1)}, s16[520,128]{1,0:T(8,128)(2,1)S(1)}, u32[]{:S(2)}, u32[]{:S(2)}) collective-permute-start(s16[520,128]{1,0:T(8,128)(2,1)S(1)} %get-tuple-element.62), channel_id=1, source_target_pairs={{0,16},{4,20},{8,24},{12,28},{16,0},{20,4},{24,8},{28,12},{1,17},{... | collective-permute-start | bytes 399368 | tf_op jit(solution)/shard_map/ppermute | solution.py:279
  50.6 3.0 %collective-permute-start.23 = (s16[520,128]{1,0:T(8,128)(2,1)S(1)}, s16[520,128]{1,0:T(8,128)(2,1)S(1)}, u32[]{:S(2)}, u32[]{:S(2)}) collective-permute-start(s16[520,128]{1,0:T(8,128)(2,1)S(1)} %get-tuple-element.64), channel_id=1, source_target_pairs={{0,20},{4,16},{8,28},{12,24},{16,4},{20,0},{24,12},{28,8},{1,21},{... | collective-permute-start | bytes 399368 | tf_op jit(solution)/shard_map/ppermute | solution.py:279
  53.6 4.5 %collective-permute-done.5.refs_5_ = s16[536,128]{1,0:T(8,128)(2,1)S(1)} collective-permute-done((s16[536,128]{1,0:T(8,128)(2,1)S(1)}, s16[536,128]{1,0:T(8,128)(2,1)S(1)}, u32[]{:S(2)}, u32[]{:S(2)}) %collective-permute-start.5) | collective-permute-done | bytes 137248 | tf_op jit(solution)/shard_map/ppermute | solution.py:279
  58.0 2.7 %collective-permute-done.6.refs_6_ = s16[536,128]{1,0:T(8,128)(2,1)S(1)} collective-permute-done((s16[536,128]{1,0:T(8,128)(2,1)S(1)}, s16[536,128]{1,0:T(8,128)(2,1)S(1)}, u32[]{:S(2)}, u32[]{:S(2)}) %collective-permute-start.6) | collective-permute-done | bytes 137248 | tf_op jit(solution)/shard_map/ppermute | solution.py:279
  61.9 4.9 %product.3 = (s16[520,128]{1,0:T(8,128)(2,1)S(1)}, s16[520,128]{1,0:T(8,128)(2,1)S(1)}, s16[520,128]{1,0:T(8,128)(2,1)S(1)}, s16[520,128]{1,0:T(8,128)(2,1)S(1)}...) custom-call(s32[1]{0:T(128)S(6)} %copy.11.pair_ref, ...), custom_call_target="tpu_custom_call" | custom-call | flops 3221225472 | bytes 10485760 | tf_op jit(solution)/shard_map/product/pallas_call | solution.py:356
  68.0 2.4 %collective-permute-start.27 = (s16[520,128]{1,0:T(8,128)(2,1)S(1)}, s16[520,128]{1,0:T(8,128)(2,1)S(1)}, u32[]{:S(2)}, u32[]{:S(2)}) collective-permute-start(s16[520,128]{1,0:T(8,128)(2,1)S(1)} %get-tuple-element.68), channel_id=1, source_target_pairs={{0,28},{4,24},{8,20},{12,16},{16,12},{20,8},{24,4},{28,0},{1,29},{... | collective-permute-start | bytes 399368 | tf_op jit(solution)/shard_map/ppermute | solution.py:279
  70.4 1.8 %collective-permute-start.17 = (s16[520,128]{1,0:T(8,128)(2,1)S(1)}, s16[520,128]{1,0:T(8,128)(2,1)S(1)}, u32[]{:S(2)}, u32[]{:S(2)}) collective-permute-start(s16[520,128]{1,0:T(8,128)(2,1)S(1)} %get-tuple-element.57), channel_id=1, source_target_pairs={{0,16},{4,20},{8,24},{12,28},{16,0},{20,4},{24,8},{28,12},{1,17},{... | collective-permute-start | bytes 399368 | tf_op jit(solution)/shard_map/ppermute | solution.py:279
  72.2 2.2 %collective-permute-start.18 = (s16[520,128]{1,0:T(8,128)(2,1)S(1)}, s16[520,128]{1,0:T(8,128)(2,1)S(1)}, u32[]{:S(2)}, u32[]{:S(2)}) collective-permute-start(s16[520,128]{1,0:T(8,128)(2,1)S(1)} %get-tuple-element.58), channel_id=1, source_target_pairs={{0,4},{4,0},{8,12},{12,8},{16,20},{20,16},{24,28},{28,24},{1,5},{5... | collective-permute-start | bytes 399368 | tf_op jit(solution)/shard_map/ppermute | solution.py:279
  74.9 1.6 %collective-permute-start.20 = (s16[520,128]{1,0:T(8,128)(2,1)S(1)}, s16[520,128]{1,0:T(8,128)(2,1)S(1)}, u32[]{:S(2)}, u32[]{:S(2)}) collective-permute-start(s16[520,128]{1,0:T(8,128)(2,1)S(1)} %get-tuple-element.60), channel_id=1, source_target_pairs={{0,12},{4,8},{8,4},{12,0},{16,28},{20,24},{24,20},{28,16},{1,13},{... | collective-permute-start | bytes 399368 | tf_op jit(solution)/shard_map/ppermute | solution.py:279
  76.5 3.9 %collective-permute-done.27.refs_6_ = s16[520,128]{1,0:T(8,128)(2,1)S(1)} collective-permute-done((s16[520,128]{1,0:T(8,128)(2,1)S(1)}, s16[520,128]{1,0:T(8,128)(2,1)S(1)}, u32[]{:S(2)}, u32[]{:S(2)}) %collective-permute-start.27) | collective-permute-done | bytes 133152 | tf_op jit(solution)/shard_map/ppermute | solution.py:279
  81.2 1.9 %collective-permute-done.17.refs_0_ = s16[520,128]{1,0:T(8,128)(2,1)S(1)} collective-permute-done((s16[520,128]{1,0:T(8,128)(2,1)S(1)}, s16[520,128]{1,0:T(8,128)(2,1)S(1)}, u32[]{:S(2)}, u32[]{:S(2)}) %collective-permute-start.17) | collective-permute-done | bytes 133152 | tf_op jit(solution)/shard_map/ppermute | solution.py:279
  87.3 5.7 %collective-permute-done.14.refs_0_ = s16[520,128]{1,0:T(8,128)(2,1)S(1)} collective-permute-done((s16[520,128]{1,0:T(8,128)(2,1)S(1)}, s16[520,128]{1,0:T(8,128)(2,1)S(1)}, u32[]{:S(2)}, u32[]{:S(2)}) %collective-permute-start.14) | collective-permute-done | bytes 133152 | tf_op jit(solution)/shard_map/ppermute | solution.py:279
  92.9 5.0 %collective-permute-done.15.refs_1_ = s16[520,128]{1,0:T(8,128)(2,1)S(1)} collective-permute-done((s16[520,128]{1,0:T(8,128)(2,1)S(1)}, s16[520,128]{1,0:T(8,128)(2,1)S(1)}, u32[]{:S(2)}, u32[]{:S(2)}) %collective-permute-start.15) | collective-permute-done | bytes 133152 | tf_op jit(solution)/shard_map/ppermute | solution.py:279
  97.9 1.6 %collective-permute-done.16.refs_2_ = s16[520,128]{1,0:T(8,128)(2,1)S(1)} collective-permute-done((s16[520,128]{1,0:T(8,128)(2,1)S(1)}, s16[520,128]{1,0:T(8,128)(2,1)S(1)}, u32[]{:S(2)}, u32[]{:S(2)}) %collective-permute-start.16) | collective-permute-done | bytes 133152 | tf_op jit(solution)/shard_map/ppermute | solution.py:279
  (61 shorter events, 17.8 us)
Async XLA Ops:
  2.3 11.8 %collective-permute-start.7 = (s16[536,128]{1,0:T(8,128)(2,1)}, s16[536,128]{1,0:T(8,128)(2,1)S(1)}, u32[]{:S(2)}, u32[]{:S(2)}) collective-permute-start(s16[536,128]{1,0:T(8,128)(2,1)} %get-tuple-element.47), channel_id=1, source_target_pairs={{0,16},{4,20},{8,24},{12,28},{16,0},{20,4},{24,8},{28,12},{1,17},{... | collective-permute-start | bytes 411656 | tf_op jit(solution)/shard_map/ppermute | solution.py:279
  5.0 14.9 %collective-permute-start.10 = (s16[536,128]{1,0:T(8,128)(2,1)}, s16[536,128]{1,0:T(8,128)(2,1)S(1)}, u32[]{:S(2)}, u32[]{:S(2)}) collective-permute-start(s16[536,128]{1,0:T(8,128)(2,1)} %get-tuple-element.37.refs_0_), channel_id=1, source_target_pairs={{0,20},{4,16},{8,28},{12,24},{16,4},{20,0},{24,12},{28,8},{1,21},{... | collective-permute-start | bytes 411656 | tf_op jit(solution)/shard_map/ppermute | solution.py:279
  10.1 11.6 %collective-permute-start.8 = (s16[536,128]{1,0:T(8,128)(2,1)}, s16[536,128]{1,0:T(8,128)(2,1)S(1)}, u32[]{:S(2)}, u32[]{:S(2)}) collective-permute-start(s16[536,128]{1,0:T(8,128)(2,1)} %get-tuple-element.48), channel_id=1, source_target_pairs={{0,4},{4,0},{8,12},{12,8},{16,20},{20,16},{24,28},{28,24},{1,5},{5... | collective-permute-start | bytes 411656 | tf_op jit(solution)/shard_map/ppermute | solution.py:279
  10.7 16.2 %collective-permute-start.9 = (s16[536,128]{1,0:T(8,128)(2,1)}, s16[536,128]{1,0:T(8,128)(2,1)S(1)}, u32[]{:S(2)}, u32[]{:S(2)}) collective-permute-start(s16[536,128]{1,0:T(8,128)(2,1)} %get-tuple-element.49), channel_id=1, source_target_pairs={{0,8},{4,12},{8,0},{12,4},{16,24},{20,28},{24,16},{28,20},{1,9},{5... | collective-permute-start | bytes 411656 | tf_op jit(solution)/shard_map/ppermute | solution.py:279
  10.9 21.9 %collective-permute-start.11 = (s16[536,128]{1,0:T(8,128)(2,1)}, s16[536,128]{1,0:T(8,128)(2,1)S(1)}, u32[]{:S(2)}, u32[]{:S(2)}) collective-permute-start(s16[536,128]{1,0:T(8,128)(2,1)} %get-tuple-element.50), channel_id=1, source_target_pairs={{0,12},{4,8},{8,4},{12,0},{16,28},{20,24},{24,20},{28,16},{1,13},{... | collective-permute-start | bytes 411656 | tf_op jit(solution)/shard_map/ppermute | solution.py:279
  14.1 18.8 %collective-permute-start.12 = (s16[536,128]{1,0:T(8,128)(2,1)}, s16[536,128]{1,0:T(8,128)(2,1)S(1)}, u32[]{:S(2)}, u32[]{:S(2)}) collective-permute-start(s16[536,128]{1,0:T(8,128)(2,1)} %get-tuple-element.51), channel_id=1, source_target_pairs={{0,24},{4,28},{8,16},{12,20},{16,8},{20,12},{24,0},{28,4},{1,25},{... | collective-permute-start | bytes 411656 | tf_op jit(solution)/shard_map/ppermute | solution.py:279
  19.9 15.8 %collective-permute-start.13 = (s16[536,128]{1,0:T(8,128)(2,1)S(1)}, s16[536,128]{1,0:T(8,128)(2,1)S(1)}, u32[]{:S(2)}, u32[]{:S(2)}) collective-permute-start(s16[536,128]{1,0:T(8,128)(2,1)S(1)} %copy-done.4), channel_id=1, source_target_pairs={{0,28},{4,24},{8,20},{12,16},{16,12},{20,8},{24,4},{28,0},{1,29},{... | collective-permute-start | bytes 411656 | tf_op jit(solution)/shard_map/ppermute | solution.py:279
  21.8 14.3 %collective-permute-start = (s16[536,128]{1,0:T(8,128)(2,1)}, s16[536,128]{1,0:T(8,128)(2,1)S(1)}, u32[]{:S(2)}, u32[]{:S(2)}) collective-permute-start(s16[536,128]{1,0:T(8,128)(2,1)} %get-tuple-element.39), channel_id=1, source_target_pairs={{0,16},{4,20},{8,24},{12,28},{16,0},{20,4},{24,8},{28,12},{1,17},{... | collective-permute-start | bytes 411656 | tf_op jit(solution)/shard_map/ppermute | solution.py:279
  32.8 12.6 %collective-permute-start.2 = (s16[536,128]{1,0:T(8,128)(2,1)S(1)}, s16[536,128]{1,0:T(8,128)(2,1)S(1)}, u32[]{:S(2)}, u32[]{:S(2)}) collective-permute-start(s16[536,128]{1,0:T(8,128)(2,1)S(1)} %copy-done.9), channel_id=1, source_target_pairs={{0,8},{4,12},{8,0},{12,4},{16,24},{20,28},{24,16},{28,20},{1,9},{5... | collective-permute-start | bytes 411656 | tf_op jit(solution)/shard_map/ppermute | solution.py:279
  32.9 17.2 %collective-permute-start.3 = (s16[536,128]{1,0:T(8,128)(2,1)S(1)}, s16[536,128]{1,0:T(8,128)(2,1)S(1)}, u32[]{:S(2)}, u32[]{:S(2)}) collective-permute-start(s16[536,128]{1,0:T(8,128)(2,1)S(1)} %copy-done.8), channel_id=1, source_target_pairs={{0,20},{4,16},{8,28},{12,24},{16,4},{20,0},{24,12},{28,8},{1,21},{... | collective-permute-start | bytes 411656 | tf_op jit(solution)/shard_map/ppermute | solution.py:279
  35.7 14.9 %collective-permute-start.4 = (s16[536,128]{1,0:T(8,128)(2,1)S(1)}, s16[536,128]{1,0:T(8,128)(2,1)S(1)}, u32[]{:S(2)}, u32[]{:S(2)}) collective-permute-start(s16[536,128]{1,0:T(8,128)(2,1)S(1)} %copy-done.7), channel_id=1, source_target_pairs={{0,12},{4,8},{8,4},{12,0},{16,28},{20,24},{24,20},{28,16},{1,13},{... | collective-permute-start | bytes 411656 | tf_op jit(solution)/shard_map/ppermute | solution.py:279
  36.0 22.0 %collective-permute-start.5 = (s16[536,128]{1,0:T(8,128)(2,1)S(1)}, s16[536,128]{1,0:T(8,128)(2,1)S(1)}, u32[]{:S(2)}, u32[]{:S(2)}) collective-permute-start(s16[536,128]{1,0:T(8,128)(2,1)S(1)} %copy-done.6), channel_id=1, source_target_pairs={{0,24},{4,28},{8,16},{12,20},{16,8},{20,12},{24,0},{28,4},{1,25},{... | collective-permute-start | bytes 411656 | tf_op jit(solution)/shard_map/ppermute | solution.py:279
  37.4 23.4 %collective-permute-start.6 = (s16[536,128]{1,0:T(8,128)(2,1)S(1)}, s16[536,128]{1,0:T(8,128)(2,1)S(1)}, u32[]{:S(2)}, u32[]{:S(2)}) collective-permute-start(s16[536,128]{1,0:T(8,128)(2,1)S(1)} %copy-done.5), channel_id=1, source_target_pairs={{0,28},{4,24},{8,20},{12,16},{16,12},{20,8},{24,4},{28,0},{1,29},{... | collective-permute-start | bytes 411656 | tf_op jit(solution)/shard_map/ppermute | solution.py:279
  45.4 21.5 %collective-permute-start.21 = (s16[520,128]{1,0:T(8,128)(2,1)S(1)}, s16[520,128]{1,0:T(8,128)(2,1)S(1)}, u32[]{:S(2)}, u32[]{:S(2)}) collective-permute-start(s16[520,128]{1,0:T(8,128)(2,1)S(1)} %get-tuple-element.62), channel_id=1, source_target_pairs={{0,16},{4,20},{8,24},{12,28},{16,0},{20,4},{24,8},{28,12},{1,17},{... | collective-permute-start | bytes 399368 | tf_op jit(solution)/shard_map/ppermute | solution.py:279
  50.1 17.9 %collective-permute-start.22 = (s16[520,128]{1,0:T(8,128)(2,1)S(1)}, s16[520,128]{1,0:T(8,128)(2,1)S(1)}, u32[]{:S(2)}, u32[]{:S(2)}) collective-permute-start(s16[520,128]{1,0:T(8,128)(2,1)S(1)} %get-tuple-element.63), channel_id=1, source_target_pairs={{0,4},{4,0},{8,12},{12,8},{16,20},{20,16},{24,28},{28,24},{1,5},{5... | collective-permute-start | bytes 399368 | tf_op jit(solution)/shard_map/ppermute | solution.py:279
  50.6 19.8 %collective-permute-start.23 = (s16[520,128]{1,0:T(8,128)(2,1)S(1)}, s16[520,128]{1,0:T(8,128)(2,1)S(1)}, u32[]{:S(2)}, u32[]{:S(2)}) collective-permute-start(s16[520,128]{1,0:T(8,128)(2,1)S(1)} %get-tuple-element.64), channel_id=1, source_target_pairs={{0,20},{4,16},{8,28},{12,24},{16,4},{20,0},{24,12},{28,8},{1,21},{... | collective-permute-start | bytes 399368 | tf_op jit(solution)/shard_map/ppermute | solution.py:279
  58.0 14.2 %collective-permute-start.24 = (s16[520,128]{1,0:T(8,128)(2,1)S(1)}, s16[520,128]{1,0:T(8,128)(2,1)S(1)}, u32[]{:S(2)}, u32[]{:S(2)}) collective-permute-start(s16[520,128]{1,0:T(8,128)(2,1)S(1)} %get-tuple-element.65), channel_id=1, source_target_pairs={{0,8},{4,12},{8,0},{12,4},{16,24},{20,28},{24,16},{28,20},{1,9},{5... | collective-permute-start | bytes 399368 | tf_op jit(solution)/shard_map/ppermute | solution.py:279
  60.8 14.1 %collective-permute-start.25 = (s16[520,128]{1,0:T(8,128)(2,1)S(1)}, s16[520,128]{1,0:T(8,128)(2,1)S(1)}, u32[]{:S(2)}, u32[]{:S(2)}) collective-permute-start(s16[520,128]{1,0:T(8,128)(2,1)S(1)} %get-tuple-element.66), channel_id=1, source_target_pairs={{0,24},{4,28},{8,16},{12,20},{16,8},{20,12},{24,0},{28,4},{1,25},{... | collective-permute-start | bytes 399368 | tf_op jit(solution)/shard_map/ppermute | solution.py:279
  68.0 12.4 %collective-permute-start.27 = (s16[520,128]{1,0:T(8,128)(2,1)S(1)}, s16[520,128]{1,0:T(8,128)(2,1)S(1)}, u32[]{:S(2)}, u32[]{:S(2)}) collective-permute-start(s16[520,128]{1,0:T(8,128)(2,1)S(1)} %get-tuple-element.68), channel_id=1, source_target_pairs={{0,28},{4,24},{8,20},{12,16},{16,12},{20,8},{24,4},{28,0},{1,29},{... | collective-permute-start | bytes 399368 | tf_op jit(solution)/shard_map/ppermute | solution.py:279
  70.4 12.7 %collective-permute-start.17 = (s16[520,128]{1,0:T(8,128)(2,1)S(1)}, s16[520,128]{1,0:T(8,128)(2,1)S(1)}, u32[]{:S(2)}, u32[]{:S(2)}) collective-permute-start(s16[520,128]{1,0:T(8,128)(2,1)S(1)} %get-tuple-element.57), channel_id=1, source_target_pairs={{0,16},{4,20},{8,24},{12,28},{16,0},{20,4},{24,8},{28,12},{1,17},{... | collective-permute-start | bytes 399368 | tf_op jit(solution)/shard_map/ppermute | solution.py:279
  72.2 12.4 %collective-permute-start.18 = (s16[520,128]{1,0:T(8,128)(2,1)S(1)}, s16[520,128]{1,0:T(8,128)(2,1)S(1)}, u32[]{:S(2)}, u32[]{:S(2)}) collective-permute-start(s16[520,128]{1,0:T(8,128)(2,1)S(1)} %get-tuple-element.58), channel_id=1, source_target_pairs={{0,4},{4,0},{8,12},{12,8},{16,20},{20,16},{24,28},{28,24},{1,5},{5... | collective-permute-start | bytes 399368 | tf_op jit(solution)/shard_map/ppermute | solution.py:279
  80.4 12.5 %collective-permute-start.14 = (s16[520,128]{1,0:T(8,128)(2,1)S(1)}, s16[520,128]{1,0:T(8,128)(2,1)S(1)}, u32[]{:S(2)}, u32[]{:S(2)}) collective-permute-start(s16[520,128]{1,0:T(8,128)(2,1)S(1)} %get-tuple-element.54), channel_id=1, source_target_pairs={{0,20},{4,16},{8,28},{12,24},{16,4},{20,0},{24,12},{28,8},{1,21},{... | collective-permute-start | bytes 399368 | tf_op jit(solution)/shard_map/ppermute | solution.py:279
  83.1 14.8 %collective-permute-start.15 = (s16[520,128]{1,0:T(8,128)(2,1)S(1)}, s16[520,128]{1,0:T(8,128)(2,1)S(1)}, u32[]{:S(2)}, u32[]{:S(2)}) collective-permute-start(s16[520,128]{1,0:T(8,128)(2,1)S(1)} %get-tuple-element.55), channel_id=1, source_target_pairs={{0,24},{4,28},{8,16},{12,20},{16,8},{20,12},{24,0},{28,4},{1,25},{... | collective-permute-start | bytes 399368 | tf_op jit(solution)/shard_map/ppermute | solution.py:279
  84.6 14.8 %collective-permute-start.16 = (s16[520,128]{1,0:T(8,128)(2,1)S(1)}, s16[520,128]{1,0:T(8,128)(2,1)S(1)}, u32[]{:S(2)}, u32[]{:S(2)}) collective-permute-start(s16[520,128]{1,0:T(8,128)(2,1)S(1)} %get-tuple-element.56), channel_id=1, source_target_pairs={{0,28},{4,24},{8,20},{12,16},{16,12},{20,8},{24,4},{28,0},{1,29},{... | collective-permute-start | bytes 399368 | tf_op jit(solution)/shard_map/ppermute | solution.py:279
  (14 other events, 109.4 us)

commit v8 on v6

--- a/solution.py
+++ b/solution.py
@@ -97,7 +97,7 @@
     tab_copy.wait()
     tab = tab_buf[...]
     below, here, above = (jnp.broadcast_to(tab[:, i : i + 1], (levels, LANES)) for i in range(3))
-    row = lax.broadcasted_iota(jnp.int32, (levels, LANES), 0)
+    row = lax.broadcasted_iota(jnp.int32, (8, LANES), 0)
 
     def rows_of(slab):
         return pl.ds(pl.multiple_of(slab * rows, rows), rows)
@@ -114,8 +114,9 @@
                 top = jnp.zeros((8, LANES), jnp.float32)
                 for f in range(2):
                     n = n_buf[at, half, f, :, cols].astype(jnp.float32)
-                    prev = jnp.where(row == 0, n, pltpu.roll(n, 1, 0))
-                    succ = jnp.where(row == levels - 1, n, pltpu.roll(n, levels - 1, 0))
+                    prev, succ = pltpu.roll(n, 1, 0), pltpu.roll(n, levels - 1, 0)
+                    prev = jnp.concatenate([jnp.where(row == 0, n[:8], prev[:8]), prev[8:]], axis=0)
+                    succ = jnp.concatenate([succ[:-8], jnp.where(row == 7, n[-8:], succ[-8:])], axis=0)
                     v = s_buf[at, half, f, :, cols] + (below * prev + here * n + above * succ)
                     values[pl.ds(pl.multiple_of(slab * rows + f * levels, levels), levels), :] = v
                     top = jnp.maximum(top, jnp.max(jnp.abs(v).reshape(levels // 8, 8, LANES), axis=0))

time: 101 us -> 101 us (level)
  no operation moved by 1% of the time
where the time goes in v8:
time: 101 us; the launch traced here: 100 us
  starting transfers between devices  43.6 us (43%)
  Pallas kernels  26.9 us (27%)
  waiting for transfers between devices  25.6 us (25%)
  local copies, waits for them, and re-layouts  3.41 us (3%)
    ppermute x28, starting transfers between devices, send(): lax.ppermute(message, 'rad', [(i, i ^ k) for i in range(groups)])  43.6 us
    ppermute x28, waiting for transfers between devices, send(): lax.ppermute(message, 'rad', [(i, i ^ k) for i in range(groups)])  25.6 us
    pallas_call x2, Pallas kernels, product(): call(functools.partial(product_kernel, order, chunk * span // LANES, slab...  11.4 us
    pallas_call x3, Pallas kernels, right_side(): call(functools.partial(right_side_kernel, ks, slabs, chunk * span, width)...  10.7 us
    pallas_call x3, Pallas kernels, result(): call(functools.partial(result_kernel, ks, slabs, chunk * span, width), 'r...  3.55 us
    unnamed x20, local copies, waits for them, and re-layouts  3.41 us
  transfers between devices with their start and end apart: 28, of which 8 were waited for; matrix products, arithmetic and copies ran while one was open for 0% of the time, Pallas kernels for 24%

profile of v8, /device:TPU:8, one launch (start us, length us, event | category | flops | bytes accessed | tf_op | source)
XLA Modules:
  0.0 100.4 jit_solution(16360357561817241444)
XLA Ops:
  0.0 2.3 %right_side.3 = (s16[536,128]{1,0:T(8,128)(2,1)}, s16[536,128]{1,0:T(8,128)(2,1)}) custom-call(bf16[2,64,8192]{2,1,0:T(8,128)(2,1)} %nonlin.5, f32[2,64,8192]{2,1,0:T(8,128)} %state.5, f32[512,128]{1,0:T(8,128)} %constant.4.clone.table), custom_call_target="tpu_custom_call" | custom-call | flops 2097152 | bytes 2097152 | tf_op jit(solution)/shard_map/right_side/pallas_call | solution.py:319
  2.3 2.7 %collective-permute-start.7 = (s16[536,128]{1,0:T(8,128)(2,1)}, s16[536,128]{1,0:T(8,128)(2,1)S(1)}, u32[]{:S(2)}, u32[]{:S(2)}) collective-permute-start(s16[536,128]{1,0:T(8,128)(2,1)} %get-tuple-element.47), channel_id=1, source_target_pairs={{0,16},{4,20},{8,24},{12,28},{16,0},{20,4},{24,8},{28,12},{1,17},{... | collective-permute-start | bytes 411656 | tf_op jit(solution)/shard_map/ppermute | solution.py:280
  6.3 3.8 %right_side.4 = (s16[536,128]{1,0:T(8,128)(2,1)}, s16[536,128]{1,0:T(8,128)(2,1)}, s16[536,128]{1,0:T(8,128)(2,1)}, s16[536,128]{1,0:T(8,128)(2,1)}, s16[536,128]{1,0:T(8,128)(2,1)}, /*index=5*/s16[536,128]{1,0:T(8,128)(2,1)}) custom-call(bf16[2,64,8192]{2,1,0:T(8,128)(2,1)} %nonlin.5, f32[2,64,8192]{2,1,0:T(8,128)} %state.5, ...), custom_call_target="tpu_custom_call" | custom-call | flops 6291456 | bytes 6291456 | tf_op jit(solution)/shard_map/right_side/pallas_call | solution.py:319
  10.9 2.8 %collective-permute-start.11 = (s16[536,128]{1,0:T(8,128)(2,1)}, s16[536,128]{1,0:T(8,128)(2,1)S(1)}, u32[]{:S(2)}, u32[]{:S(2)}) collective-permute-start(s16[536,128]{1,0:T(8,128)(2,1)} %get-tuple-element.50), channel_id=1, source_target_pairs={{0,12},{4,8},{8,4},{12,0},{16,28},{20,24},{24,20},{28,16},{1,13},{... | collective-permute-start | bytes 411656 | tf_op jit(solution)/shard_map/ppermute | solution.py:280
  15.3 4.6 %right_side.5 = (s16[536,128]{1,0:T(8,128)(2,1)}, s16[536,128]{1,0:T(8,128)(2,1)}, s16[536,128]{1,0:T(8,128)(2,1)}, s16[536,128]{1,0:T(8,128)(2,1)}, s16[536,128...) custom-call(bf16[2,64,8192]{2,1,0:T(8,128)(2,1)} %nonlin.5, ...), custom_call_target="tpu_custom_call" | custom-call | flops 8388608 | bytes 8388608 | tf_op jit(solution)/shard_map/right_side/pallas_call | solution.py:319
  19.9 1.9 %collective-permute-start.13 = (s16[536,128]{1,0:T(8,128)(2,1)S(1)}, s16[536,128]{1,0:T(8,128)(2,1)S(1)}, u32[]{:S(2)}, u32[]{:S(2)}) collective-permute-start(s16[536,128]{1,0:T(8,128)(2,1)S(1)} %copy-done.4), channel_id=1, source_target_pairs={{0,28},{4,24},{8,20},{12,16},{16,12},{20,8},{24,4},{28,0},{1,29},{... | collective-permute-start | bytes 411656 | tf_op jit(solution)/shard_map/ppermute | solution.py:280
  21.8 5.1 %collective-permute-start = (s16[536,128]{1,0:T(8,128)(2,1)}, s16[536,128]{1,0:T(8,128)(2,1)S(1)}, u32[]{:S(2)}, u32[]{:S(2)}) collective-permute-start(s16[536,128]{1,0:T(8,128)(2,1)} %get-tuple-element.39), channel_id=1, source_target_pairs={{0,16},{4,20},{8,24},{12,28},{16,0},{20,4},{24,8},{28,12},{1,17},{... | collective-permute-start | bytes 411656 | tf_op jit(solution)/shard_map/ppermute | solution.py:280
  28.1 3.4 %copy-done = f32[1,2,1024,1024]{3,2,1,0:T(8,128)S(1)} copy-done((f32[1,2,1024,1024]{3,2,1,0:T(8,128)S(1)}, f32[1,2,1024,1024]{3,2,1,0:T(8,128)}, u32[]{:S(2)}) %copy-start) | copy-done | bytes 8388632
  32.9 2.9 %collective-permute-start.3 = (s16[536,128]{1,0:T(8,128)(2,1)S(1)}, s16[536,128]{1,0:T(8,128)(2,1)S(1)}, u32[]{:S(2)}, u32[]{:S(2)}) collective-permute-start(s16[536,128]{1,0:T(8,128)(2,1)S(1)} %copy-done.8), channel_id=1, source_target_pairs={{0,20},{4,16},{8,28},{12,24},{16,4},{20,0},{24,12},{28,8},{1,21},{... | collective-permute-start | bytes 411656 | tf_op jit(solution)/shard_map/ppermute | solution.py:280
  37.4 1.4 %collective-permute-start.6 = (s16[536,128]{1,0:T(8,128)(2,1)S(1)}, s16[536,128]{1,0:T(8,128)(2,1)S(1)}, u32[]{:S(2)}, u32[]{:S(2)}) collective-permute-start(s16[536,128]{1,0:T(8,128)(2,1)S(1)} %copy-done.5), channel_id=1, source_target_pairs={{0,28},{4,24},{8,20},{12,16},{16,12},{20,8},{24,4},{28,0},{1,29},{... | collective-permute-start | bytes 411656 | tf_op jit(solution)/shard_map/ppermute | solution.py:280
  38.8 6.5 %product.2 = (s16[520,128]{1,0:T(8,128)(2,1)S(1)}, s16[520,128]{1,0:T(8,128)(2,1)S(1)}, s16[520,128]{1,0:T(8,128)(2,1)S(1)}, s16[520,128]{1,0:T(8,128)(2,1)S(1)}...) custom-call(s32[1]{0:T(128)S(6)} %copy.11.pair_ref, ...), custom_call_target="tpu_custom_call" | custom-call | flops 3221225472 | bytes 10485760 | tf_op jit(solution)/shard_map/product/pallas_call | solution.py:356
  45.3 4.7 %collective-permute-start.21 = (s16[520,128]{1,0:T(8,128)(2,1)S(1)}, s16[520,128]{1,0:T(8,128)(2,1)S(1)}, u32[]{:S(2)}, u32[]{:S(2)}) collective-permute-start(s16[520,128]{1,0:T(8,128)(2,1)S(1)} %get-tuple-element.62), channel_id=1, source_target_pairs={{0,16},{4,20},{8,24},{12,28},{16,0},{20,4},{24,8},{28,12},{1,17},{... | collective-permute-start | bytes 399368 | tf_op jit(solution)/shard_map/ppermute | solution.py:280
  50.6 1.7 %collective-permute-start.23 = (s16[520,128]{1,0:T(8,128)(2,1)S(1)}, s16[520,128]{1,0:T(8,128)(2,1)S(1)}, u32[]{:S(2)}, u32[]{:S(2)}) collective-permute-start(s16[520,128]{1,0:T(8,128)(2,1)S(1)} %get-tuple-element.64), channel_id=1, source_target_pairs={{0,8},{4,12},{8,0},{12,4},{16,24},{20,28},{24,16},{28,20},{1,9},{5... | collective-permute-start | bytes 399368 | tf_op jit(solution)/shard_map/ppermute | solution.py:280
  52.3 2.8 %collective-permute-done.5.refs_5_ = s16[536,128]{1,0:T(8,128)(2,1)S(1)} collective-permute-done((s16[536,128]{1,0:T(8,128)(2,1)S(1)}, s16[536,128]{1,0:T(8,128)(2,1)S(1)}, u32[]{:S(2)}, u32[]{:S(2)}) %collective-permute-start.5) | collective-permute-done | bytes 137248 | tf_op jit(solution)/shard_map/ppermute | solution.py:280
  55.1 4.4 %collective-permute-done.6.refs_6_ = s16[536,128]{1,0:T(8,128)(2,1)S(1)} collective-permute-done((s16[536,128]{1,0:T(8,128)(2,1)S(1)}, s16[536,128]{1,0:T(8,128)(2,1)S(1)}, u32[]{:S(2)}, u32[]{:S(2)}) %collective-permute-start.6) | collective-permute-done | bytes 137248 | tf_op jit(solution)/shard_map/ppermute | solution.py:280
  59.5 4.9 %product.3 = (s16[520,128]{1,0:T(8,128)(2,1)S(1)}, s16[520,128]{1,0:T(8,128)(2,1)S(1)}, s16[520,128]{1,0:T(8,128)(2,1)S(1)}, s16[520,128]{1,0:T(8,128)(2,1)S(1)}...) custom-call(s32[1]{0:T(128)S(6)} %copy.11.pair_ref, ...), custom_call_target="tpu_custom_call" | custom-call | flops 3221225472 | bytes 10485760 | tf_op jit(solution)/shard_map/product/pallas_call | solution.py:356
  65.2 2.3 %collective-permute-start.27 = (s16[520,128]{1,0:T(8,128)(2,1)S(1)}, s16[520,128]{1,0:T(8,128)(2,1)S(1)}, u32[]{:S(2)}, u32[]{:S(2)}) collective-permute-start(s16[520,128]{1,0:T(8,128)(2,1)S(1)} %get-tuple-element.68), channel_id=1, source_target_pairs={{0,28},{4,24},{8,20},{12,16},{16,12},{20,8},{24,4},{28,0},{1,29},{... | collective-permute-start | bytes 399368 | tf_op jit(solution)/shard_map/ppermute | solution.py:280
  67.4 3.9 %collective-permute-start.17 = (s16[520,128]{1,0:T(8,128)(2,1)S(1)}, s16[520,128]{1,0:T(8,128)(2,1)S(1)}, u32[]{:S(2)}, u32[]{:S(2)}) collective-permute-start(s16[520,128]{1,0:T(8,128)(2,1)S(1)} %get-tuple-element.57), channel_id=1, source_target_pairs={{0,16},{4,20},{8,24},{12,28},{16,0},{20,4},{24,8},{28,12},{1,17},{... | collective-permute-start | bytes 399368 | tf_op jit(solution)/shard_map/ppermute | solution.py:280
  72.8 5.1 %collective-permute-done.26.refs_5_ = s16[520,128]{1,0:T(8,128)(2,1)S(1)} collective-permute-done((s16[520,128]{1,0:T(8,128)(2,1)S(1)}, s16[520,128]{1,0:T(8,128)(2,1)S(1)}, u32[]{:S(2)}, u32[]{:S(2)}) %collective-permute-start.26) | collective-permute-done | bytes 133152 | tf_op jit(solution)/shard_map/ppermute | solution.py:280
  77.8 6.0 %collective-permute-done.27.refs_6_ = s16[520,128]{1,0:T(8,128)(2,1)S(1)} collective-permute-done((s16[520,128]{1,0:T(8,128)(2,1)S(1)}, s16[520,128]{1,0:T(8,128)(2,1)S(1)}, u32[]{:S(2)}, u32[]{:S(2)}) %collective-permute-start.27) | collective-permute-done | bytes 133152 | tf_op jit(solution)/shard_map/ppermute | solution.py:280
  84.8 5.2 %collective-permute-start.16 = (s16[520,128]{1,0:T(8,128)(2,1)S(1)}, s16[520,128]{1,0:T(8,128)(2,1)S(1)}, u32[]{:S(2)}, u32[]{:S(2)}) collective-permute-start(s16[520,128]{1,0:T(8,128)(2,1)S(1)} %get-tuple-element.56), channel_id=1, source_target_pairs={{0,28},{4,24},{8,20},{12,16},{16,12},{20,8},{24,4},{28,0},{1,29},{... | collective-permute-start | bytes 399368 | tf_op jit(solution)/shard_map/ppermute | solution.py:280
  90.0 1.5 %result.3.refs_5_ = f32[2,64,8192]{2,1,0:T(8,128)} custom-call(s16[520,128]{1,0:T(8,128)(2,1)S(1)} %collective-permute-done.21.refs_0_, s16[520,128]{1,0:T(8,128)(2,1)S(1)} %collective-permute-done.22.refs_1_, s16[520,128]{1,0:T(8,128)(2,1)S(1)} %collective-permute-done.23.refs_2_, s16[520,128]{1,0:T(8,128)(2,1)S(1)} %collective-permute-done.24.refs_3_, ...), custom_call_target="tpu_custom_call" | custom-call | flops 1048576 | bytes 2097152 | tf_op jit(solution)/shard_map/result/pallas_call | solution.py:379
  93.4 3.3 %collective-permute-done.15.refs_1_ = s16[520,128]{1,0:T(8,128)(2,1)S(1)} collective-permute-done((s16[520,128]{1,0:T(8,128)(2,1)S(1)}, s16[520,128]{1,0:T(8,128)(2,1)S(1)}, u32[]{:S(2)}, u32[]{:S(2)}) %collective-permute-start.15) | collective-permute-done | bytes 133152 | tf_op jit(solution)/shard_map/ppermute | solution.py:280
  96.6 2.8 %collective-permute-done.16.refs_2_ = s16[520,128]{1,0:T(8,128)(2,1)S(1)} collective-permute-done((s16[520,128]{1,0:T(8,128)(2,1)S(1)}, s16[520,128]{1,0:T(8,128)(2,1)S(1)}, u32[]{:S(2)}, u32[]{:S(2)}) %collective-permute-start.16) | collective-permute-done | bytes 133152 | tf_op jit(solution)/shard_map/ppermute | solution.py:280
  (61 shorter events, 13.6 us)
Async XLA Ops:
  5.0 14.9 %collective-permute-start.10 = (s16[536,128]{1,0:T(8,128)(2,1)}, s16[536,128]{1,0:T(8,128)(2,1)S(1)}, u32[]{:S(2)}, u32[]{:S(2)}) collective-permute-start(s16[536,128]{1,0:T(8,128)(2,1)} %get-tuple-element.37.refs_0_), channel_id=1, source_target_pairs={{0,20},{4,16},{8,28},{12,24},{16,4},{20,0},{24,12},{28,8},{1,21},{... | collective-permute-start | bytes 411656 | tf_op jit(solution)/shard_map/ppermute | solution.py:280
  10.7 16.2 %collective-permute-start.9 = (s16[536,128]{1,0:T(8,128)(2,1)}, s16[536,128]{1,0:T(8,128)(2,1)S(1)}, u32[]{:S(2)}, u32[]{:S(2)}) collective-permute-start(s16[536,128]{1,0:T(8,128)(2,1)} %get-tuple-element.49), channel_id=1, source_target_pairs={{0,8},{4,12},{8,0},{12,4},{16,24},{20,28},{24,16},{28,20},{1,9},{5... | collective-permute-start | bytes 411656 | tf_op jit(solution)/shard_map/ppermute | solution.py:280
  10.9 21.9 %collective-permute-start.11 = (s16[536,128]{1,0:T(8,128)(2,1)}, s16[536,128]{1,0:T(8,128)(2,1)S(1)}, u32[]{:S(2)}, u32[]{:S(2)}) collective-permute-start(s16[536,128]{1,0:T(8,128)(2,1)} %get-tuple-element.50), channel_id=1, source_target_pairs={{0,12},{4,8},{8,4},{12,0},{16,28},{20,24},{24,20},{28,16},{1,13},{... | collective-permute-start | bytes 411656 | tf_op jit(solution)/shard_map/ppermute | solution.py:280
  14.1 18.7 %collective-permute-start.12 = (s16[536,128]{1,0:T(8,128)(2,1)}, s16[536,128]{1,0:T(8,128)(2,1)S(1)}, u32[]{:S(2)}, u32[]{:S(2)}) collective-permute-start(s16[536,128]{1,0:T(8,128)(2,1)} %get-tuple-element.51), channel_id=1, source_target_pairs={{0,24},{4,28},{8,16},{12,20},{16,8},{20,12},{24,0},{28,4},{1,25},{... | collective-permute-start | bytes 411656 | tf_op jit(solution)/shard_map/ppermute | solution.py:280
  19.9 15.8 %collective-permute-start.13 = (s16[536,128]{1,0:T(8,128)(2,1)S(1)}, s16[536,128]{1,0:T(8,128)(2,1)S(1)}, u32[]{:S(2)}, u32[]{:S(2)}) collective-permute-start(s16[536,128]{1,0:T(8,128)(2,1)S(1)} %copy-done.4), channel_id=1, source_target_pairs={{0,28},{4,24},{8,20},{12,16},{16,12},{20,8},{24,4},{28,0},{1,29},{... | collective-permute-start | bytes 411656 | tf_op jit(solution)/shard_map/ppermute | solution.py:280
  21.8 14.3 %collective-permute-start = (s16[536,128]{1,0:T(8,128)(2,1)}, s16[536,128]{1,0:T(8,128)(2,1)S(1)}, u32[]{:S(2)}, u32[]{:S(2)}) collective-permute-start(s16[536,128]{1,0:T(8,128)(2,1)} %get-tuple-element.39), channel_id=1, source_target_pairs={{0,16},{4,20},{8,24},{12,28},{16,0},{20,4},{24,8},{28,12},{1,17},{... | collective-permute-start | bytes 411656 | tf_op jit(solution)/shard_map/ppermute | solution.py:280
  32.8 12.6 %collective-permute-start.2 = (s16[536,128]{1,0:T(8,128)(2,1)S(1)}, s16[536,128]{1,0:T(8,128)(2,1)S(1)}, u32[]{:S(2)}, u32[]{:S(2)}) collective-permute-start(s16[536,128]{1,0:T(8,128)(2,1)S(1)} %copy-done.9), channel_id=1, source_target_pairs={{0,8},{4,12},{8,0},{12,4},{16,24},{20,28},{24,16},{28,20},{1,9},{5... | collective-permute-start | bytes 411656 | tf_op jit(solution)/shard_map/ppermute | solution.py:280
  32.9 17.2 %collective-permute-start.3 = (s16[536,128]{1,0:T(8,128)(2,1)S(1)}, s16[536,128]{1,0:T(8,128)(2,1)S(1)}, u32[]{:S(2)}, u32[]{:S(2)}) collective-permute-start(s16[536,128]{1,0:T(8,128)(2,1)S(1)} %copy-done.8), channel_id=1, source_target_pairs={{0,20},{4,16},{8,28},{12,24},{16,4},{20,0},{24,12},{28,8},{1,21},{... | collective-permute-start | bytes 411656 | tf_op jit(solution)/shard_map/ppermute | solution.py:280
  35.7 14.9 %collective-permute-start.4 = (s16[536,128]{1,0:T(8,128)(2,1)S(1)}, s16[536,128]{1,0:T(8,128)(2,1)S(1)}, u32[]{:S(2)}, u32[]{:S(2)}) collective-permute-start(s16[536,128]{1,0:T(8,128)(2,1)S(1)} %copy-done.7), channel_id=1, source_target_pairs={{0,12},{4,8},{8,4},{12,0},{16,28},{20,24},{24,20},{28,16},{1,13},{... | collective-permute-start | bytes 411656 | tf_op jit(solution)/shard_map/ppermute | solution.py:280
  36.0 19.1 %collective-permute-start.5 = (s16[536,128]{1,0:T(8,128)(2,1)S(1)}, s16[536,128]{1,0:T(8,128)(2,1)S(1)}, u32[]{:S(2)}, u32[]{:S(2)}) collective-permute-start(s16[536,128]{1,0:T(8,128)(2,1)S(1)} %copy-done.6), channel_id=1, source_target_pairs={{0,24},{4,28},{8,16},{12,20},{16,8},{20,12},{24,0},{28,4},{1,25},{... | collective-permute-start | bytes 411656 | tf_op jit(solution)/shard_map/ppermute | solution.py:280
  37.4 22.1 %collective-permute-start.6 = (s16[536,128]{1,0:T(8,128)(2,1)S(1)}, s16[536,128]{1,0:T(8,128)(2,1)S(1)}, u32[]{:S(2)}, u32[]{:S(2)}) collective-permute-start(s16[536,128]{1,0:T(8,128)(2,1)S(1)} %copy-done.5), channel_id=1, source_target_pairs={{0,28},{4,24},{8,20},{12,16},{16,12},{20,8},{24,4},{28,0},{1,29},{... | collective-permute-start | bytes 411656 | tf_op jit(solution)/shard_map/ppermute | solution.py:280
  45.3 19.1 %collective-permute-start.21 = (s16[520,128]{1,0:T(8,128)(2,1)S(1)}, s16[520,128]{1,0:T(8,128)(2,1)S(1)}, u32[]{:S(2)}, u32[]{:S(2)}) collective-permute-start(s16[520,128]{1,0:T(8,128)(2,1)S(1)} %get-tuple-element.62), channel_id=1, source_target_pairs={{0,16},{4,20},{8,24},{12,28},{16,0},{20,4},{24,8},{28,12},{1,17},{... | collective-permute-start | bytes 399368 | tf_op jit(solution)/shard_map/ppermute | solution.py:280
  50.1 15.1 %collective-permute-start.22 = (s16[520,128]{1,0:T(8,128)(2,1)S(1)}, s16[520,128]{1,0:T(8,128)(2,1)S(1)}, u32[]{:S(2)}, u32[]{:S(2)}) collective-permute-start(s16[520,128]{1,0:T(8,128)(2,1)S(1)} %get-tuple-element.63), channel_id=1, source_target_pairs={{0,4},{4,0},{8,12},{12,8},{16,20},{20,16},{24,28},{28,24},{1,5},{5... | collective-permute-start | bytes 399368 | tf_op jit(solution)/shard_map/ppermute | solution.py:280
  50.6 16.9 %collective-permute-start.23 = (s16[520,128]{1,0:T(8,128)(2,1)S(1)}, s16[520,128]{1,0:T(8,128)(2,1)S(1)}, u32[]{:S(2)}, u32[]{:S(2)}) collective-permute-start(s16[520,128]{1,0:T(8,128)(2,1)S(1)} %get-tuple-element.64), channel_id=1, source_target_pairs={{0,8},{4,12},{8,0},{12,4},{16,24},{20,28},{24,16},{28,20},{1,9},{5... | collective-permute-start | bytes 399368 | tf_op jit(solution)/shard_map/ppermute | solution.py:280
  55.1 16.2 %collective-permute-start.24 = (s16[520,128]{1,0:T(8,128)(2,1)S(1)}, s16[520,128]{1,0:T(8,128)(2,1)S(1)}, u32[]{:S(2)}, u32[]{:S(2)}) collective-permute-start(s16[520,128]{1,0:T(8,128)(2,1)S(1)} %get-tuple-element.65), channel_id=1, source_target_pairs={{0,20},{4,16},{8,28},{12,24},{16,4},{20,0},{24,12},{28,8},{1,21},{... | collective-permute-start | bytes 399368 | tf_op jit(solution)/shard_map/ppermute | solution.py:280
  59.5 11.9 %collective-permute-start.25 = (s16[520,128]{1,0:T(8,128)(2,1)S(1)}, s16[520,128]{1,0:T(8,128)(2,1)S(1)}, u32[]{:S(2)}, u32[]{:S(2)}) collective-permute-start(s16[520,128]{1,0:T(8,128)(2,1)S(1)} %get-tuple-element.66), channel_id=1, source_target_pairs={{0,12},{4,8},{8,4},{12,0},{16,28},{20,24},{24,20},{28,16},{1,13},{... | collective-permute-start | bytes 399368 | tf_op jit(solution)/shard_map/ppermute | solution.py:280
  64.4 13.4 %collective-permute-start.26 = (s16[520,128]{1,0:T(8,128)(2,1)S(1)}, s16[520,128]{1,0:T(8,128)(2,1)S(1)}, u32[]{:S(2)}, u32[]{:S(2)}) collective-permute-start(s16[520,128]{1,0:T(8,128)(2,1)S(1)} %get-tuple-element.67), channel_id=1, source_target_pairs={{0,24},{4,28},{8,16},{12,20},{16,8},{20,12},{24,0},{28,4},{1,25},{... | collective-permute-start | bytes 399368 | tf_op jit(solution)/shard_map/ppermute | solution.py:280
  65.2 18.7 %collective-permute-start.27 = (s16[520,128]{1,0:T(8,128)(2,1)S(1)}, s16[520,128]{1,0:T(8,128)(2,1)S(1)}, u32[]{:S(2)}, u32[]{:S(2)}) collective-permute-start(s16[520,128]{1,0:T(8,128)(2,1)S(1)} %get-tuple-element.68), channel_id=1, source_target_pairs={{0,28},{4,24},{8,20},{12,16},{16,12},{20,8},{24,4},{28,0},{1,29},{... | collective-permute-start | bytes 399368 | tf_op jit(solution)/shard_map/ppermute | solution.py:280
  67.4 16.5 %collective-permute-start.17 = (s16[520,128]{1,0:T(8,128)(2,1)S(1)}, s16[520,128]{1,0:T(8,128)(2,1)S(1)}, u32[]{:S(2)}, u32[]{:S(2)}) collective-permute-start(s16[520,128]{1,0:T(8,128)(2,1)S(1)} %get-tuple-element.57), channel_id=1, source_target_pairs={{0,16},{4,20},{8,24},{12,28},{16,0},{20,4},{24,8},{28,12},{1,17},{... | collective-permute-start | bytes 399368 | tf_op jit(solution)/shard_map/ppermute | solution.py:280
  71.4 13.4 %collective-permute-start.18 = (s16[520,128]{1,0:T(8,128)(2,1)S(1)}, s16[520,128]{1,0:T(8,128)(2,1)S(1)}, u32[]{:S(2)}, u32[]{:S(2)}) collective-permute-start(s16[520,128]{1,0:T(8,128)(2,1)S(1)} %get-tuple-element.58), channel_id=1, source_target_pairs={{0,4},{4,0},{8,12},{12,8},{16,20},{20,16},{24,28},{28,24},{1,5},{5... | collective-permute-start | bytes 399368 | tf_op jit(solution)/shard_map/ppermute | solution.py:280
  71.4 20.1 %collective-permute-start.19 = (s16[520,128]{1,0:T(8,128)(2,1)S(1)}, s16[520,128]{1,0:T(8,128)(2,1)S(1)}, u32[]{:S(2)}, u32[]{:S(2)}) collective-permute-start(s16[520,128]{1,0:T(8,128)(2,1)S(1)} %get-tuple-element.59), channel_id=1, source_target_pairs={{0,8},{4,12},{8,0},{12,4},{16,24},{20,28},{24,16},{28,20},{1,9},{5... | collective-permute-start | bytes 399368 | tf_op jit(solution)/shard_map/ppermute | solution.py:280
  77.8 14.4 %collective-permute-start.20 = (s16[520,128]{1,0:T(8,128)(2,1)S(1)}, s16[520,128]{1,0:T(8,128)(2,1)S(1)}, u32[]{:S(2)}, u32[]{:S(2)}) collective-permute-start(s16[520,128]{1,0:T(8,128)(2,1)S(1)} %get-tuple-element.60), channel_id=1, source_target_pairs={{0,20},{4,16},{8,28},{12,24},{16,4},{20,0},{24,12},{28,8},{1,21},{... | collective-permute-start | bytes 399368 | tf_op jit(solution)/shard_map/ppermute | solution.py:280
  83.9 12.8 %collective-permute-start.15 = (s16[520,128]{1,0:T(8,128)(2,1)S(1)}, s16[520,128]{1,0:T(8,128)(2,1)S(1)}, u32[]{:S(2)}, u32[]{:S(2)}) collective-permute-start(s16[520,128]{1,0:T(8,128)(2,1)S(1)} %get-tuple-element.55), channel_id=1, source_target_pairs={{0,24},{4,28},{8,16},{12,20},{16,8},{20,12},{24,0},{28,4},{1,25},{... | collective-permute-start | bytes 399368 | tf_op jit(solution)/shard_map/ppermute | solution.py:280
  84.8 14.7 %collective-permute-start.16 = (s16[520,128]{1,0:T(8,128)(2,1)S(1)}, s16[520,128]{1,0:T(8,128)(2,1)S(1)}, u32[]{:S(2)}, u32[]{:S(2)}) collective-permute-start(s16[520,128]{1,0:T(8,128)(2,1)S(1)} %get-tuple-element.56), channel_id=1, source_target_pairs={{0,28},{4,24},{8,20},{12,16},{16,12},{20,8},{24,4},{28,0},{1,29},{... | collective-permute-start | bytes 399368 | tf_op jit(solution)/shard_map/ppermute | solution.py:280
  (14 other events, 109.4 us)
